TPU v7x, 256 devices: a whole 4x4x8 slice. The times are simulated.
256 devices in a mesh: lat: 16 (over y_hi, x, core), lon: 16 (over y_lo, z).
Axes of the slice: x: 4, y: 4 (y_hi: 2, y_lo: 2; y = y_hi * 2 + y_lo), z: 8, core: 2. Of those that a mesh axis runs over, the one named last changes fastest.
Arguments:
- grid_features: bfloat16 [32, 2048, 512], P('lat', 'lon'), may hold values from -18 to 18
- widths: int32 [32], replicated, may hold values from 32 to 1024, as said below
- w_query: bfloat16 [512, 512], replicated, may hold values from -1 to 1
- w_keyval: bfloat16 [1536, 1024], replicated, may hold values from -1 to 1
- w_out: bfloat16 [512, 512], replicated, may hold values from -0.25 to 0.25
Outputs:
- layer_out: bfloat16 [32, 2048, 512], P('lat', 'lon')
Inputs may be any that keep to these rules, and one draw needn't show every extreme that they name: `widths`: rows 0 and 31 hold 2048 // 2 (their neighborhood is the whole longitude circle); every other row holds a value from 32 to 128, and some such row holds exactly 128.
All inputs are finite; a program needn't handle non-finite values.
Results may differ from a plain program's by a relative error of at most 0.0085.
Values may be sent and summed in bfloat16 or wider, within the bound.
No kernel may reach another device: no remote copies, remote signals or barrier semaphores. Data moves between devices by JAX's collectives and lax.ppermute only.
A program may use at most 128 MiB of HBM per device.

v0:
```python
import math

import jax
import jax.numpy as jnp
from jax import lax
from jax.sharding import PartitionSpec as P

HEADS = 8
HDIM = 64


MASKED_SCORE = -1e30


def from_root(block, axis, source):
    block = jnp.where(lax.axis_index(axis) == source, block, jnp.zeros_like(block))
    return lax.psum(block, axis)


def extended(cells, sides, width):
    for axis, dim in sides:
        count = lax.axis_size(axis)
        head = lax.slice_in_dim(cells, 0, width, axis=dim)
        tail = lax.slice_in_dim(cells, cells.shape[dim] - width, cells.shape[dim], axis=dim)
        cells = jnp.concatenate(
            [
                lax.ppermute(tail, axis, [(i, (i + 1) % count) for i in range(count)]),
                cells,
                lax.ppermute(head, axis, [((i + 1) % count, i) for i in range(count)]),
            ],
            axis=dim,
        )
    return cells


def passed_along(value, axis, steps):
    count = lax.axis_size(axis)
    pairs = [(source, (source + steps) % count) for source in range(count)]
    return lax.ppermute(value, axis, pairs)


def row_weight(row_ids, row_total):
    inside = (row_ids >= 0) & (row_ids < row_total)
    clipped = jnp.clip(row_ids, 0, row_total - 1).astype(jnp.float32)
    return jnp.where(inside, jnp.sin(jnp.pi * (clipped + 0.5) / row_total), jnp.zeros_like(clipped))


def log_weight(weight):
    return jnp.log(jnp.where(weight > 0, weight, jnp.ones_like(weight)))


def pole_row(piece, root):
    return from_root(piece, "lat", root)


def body(grid_features, widths, w_query, w_keyval, w_out):
    rows_dev, lon_dev, channels = grid_features.shape
    lat_count = lax.axis_size("lat")
    lon_count = lax.axis_size("lon")
    lat_total = rows_dev * lat_count
    lon_total = lon_dev * lon_count
    lat_index = lax.axis_index("lat")
    lon_index = lax.axis_index("lon")
    first_row = lat_index * rows_dev
    local_rows = first_row + jnp.arange(rows_dev, dtype=jnp.int32)
    beside_all = extended(grid_features, (("lat", 0), ("lon", 1)), 1)
    upper_row = beside_all[:-2, 1:-1].astype(jnp.float32)
    lower_row = beside_all[2:, 1:-1].astype(jnp.float32)
    west_col = beside_all[1:-1, :-2].astype(jnp.float32)
    east_col = beside_all[1:-1, 2:].astype(jnp.float32)
    upper_weight = row_weight(local_rows - 1, lat_total)[:, None, None]
    lower_weight = row_weight(local_rows + 1, lat_total)[:, None, None]
    lat_mix = (
        (upper_weight * upper_row + lower_weight * lower_row) / (upper_weight + lower_weight)
    ).astype(jnp.bfloat16)
    lon_mix = (0.5 * (west_col + east_col)).astype(jnp.bfloat16)
    basis_cat = jnp.concatenate([grid_features, lat_mix, lon_mix], axis=2).reshape(-1, 3 * channels)
    keyval = jnp.dot(basis_cat, w_keyval, preferred_element_type=jnp.float32).astype(jnp.bfloat16)
    keyval = keyval.reshape(rows_dev, lon_dev, 2 * channels)
    queries = jnp.dot(
        grid_features.reshape(-1, channels), w_query, preferred_element_type=jnp.float32
    )
    queries = queries.astype(jnp.bfloat16).reshape(-1, HEADS, HDIM)
    kv_block = extended(keyval, (("lat", 0),), 1)
    north_row = pole_row(keyval[0], 0)
    south_row = pole_row(keyval[rows_dev - 1], lat_count - 1)
    pole_cells = jnp.concatenate([north_row, south_row], axis=0)
    score_scale = 1.0 / math.sqrt(HDIM)
    query_count = rows_dev * lon_dev
    query_cols = lon_index * lon_dev + jnp.arange(lon_dev, dtype=jnp.int32)
    local_widths = lax.dynamic_slice_in_dim(widths, first_row, rows_dev)
    key_rows = first_row - 1 + jnp.arange(rows_dev + 2, dtype=jnp.int32)
    key_weight = row_weight(key_rows, lat_total)
    key_logs = jnp.repeat(log_weight(key_weight), lon_dev)
    query_slot = jnp.arange(rows_dev, dtype=jnp.int32)[:, None]
    key_slot = jnp.arange(rows_dev + 2, dtype=jnp.int32)[None, :]
    row_ok = (key_slot >= query_slot) & (key_slot <= query_slot + 2) & (key_weight > 0)[None, :]

    def absorb(softmax_state, keyvals, allowed, logs_in):
        running_max, denominator, weighted = softmax_state
        key_part = keyvals[:, :channels].reshape(-1, HEADS, HDIM)
        value_part = keyvals[:, channels:].reshape(-1, HEADS, HDIM)
        scores = (
            jnp.einsum("qhd,khd->hqk", queries, key_part, preferred_element_type=jnp.float32)
            * score_scale
        )
        scores = scores + logs_in[None, None, :]
        scores = jnp.where(allowed[None], scores, MASKED_SCORE)
        new_max = jnp.maximum(running_max, jnp.max(scores, axis=2))
        exp_scores = jnp.exp(scores - new_max[:, :, None])
        shrink = jnp.exp(running_max - new_max)
        denominator = denominator * shrink + jnp.sum(exp_scores, axis=2)
        contribution = jnp.einsum(
            "hqk,khd->qhd",
            exp_scores.astype(jnp.bfloat16),
            value_part,
            preferred_element_type=jnp.float32,
        )
        weighted = weighted * jnp.transpose(shrink)[:, :, None] + contribution
        return (new_max, denominator, weighted)

    def attend_to(softmax_state, keyvals, source):
        key_cols = source * lon_dev + jnp.arange(lon_dev, dtype=jnp.int32)
        forward_gap = jnp.mod(key_cols[None, :] - query_cols[:, None], lon_total)
        distance = jnp.minimum(forward_gap, lon_total - forward_gap)
        inside = distance[None, :, None, :] <= local_widths[:, None, None, None]
        allowed = (row_ok[:, None, :, None] & inside).reshape(query_count, (rows_dev + 2) * lon_dev)
        return absorb(softmax_state, keyvals.reshape(-1, 2 * channels), allowed, key_logs)

    def attend_some(softmax_state, keyvals, source):
        return attend_to(softmax_state, keyvals, source)

    initial = (
        jnp.full((HEADS, query_count), MASKED_SCORE, jnp.float32),
        jnp.zeros((HEADS, query_count), jnp.float32),
        jnp.zeros((query_count, HEADS, HDIM), jnp.float32),
    )
    softmax_state = absorb(
        initial,
        pole_cells,
        jnp.ones((query_count, 2 * lon_dev), dtype=bool),
        jnp.zeros((2 * lon_dev,), jnp.float32),
    )
    softmax_state = attend_to(softmax_state, kv_block, lon_index)

    def turn_one(turn_index, loop_carry):
        current_state, current = loop_carry
        current = passed_along(current, "lon", 1)
        current_state = attend_some(
            current_state, current, jnp.mod(lon_index - turn_index, lon_count)
        )
        return (current_state, current)

    softmax_state, kv_last = lax.fori_loop(1, lon_count, turn_one, (softmax_state, kv_block))
    running_max, denominator, weighted = softmax_state
    attended = (
        (weighted / jnp.transpose(denominator)[:, :, None])
        .reshape(-1, channels)
        .astype(jnp.bfloat16)
    )
    layer_out = jnp.dot(attended, w_out, preferred_element_type=jnp.float32).astype(jnp.bfloat16)
    return layer_out.reshape(rows_dev, lon_dev, channels)


def solution(mesh):
    in_specs = (P("lat", "lon", None), P(), P(), P(), P())
    out_specs = P("lat", "lon", None)
    return jax.shard_map(body, mesh=mesh, in_specs=in_specs, out_specs=out_specs, check_vma=False)
```

profile of v0, /device:TPU:22, one launch (start us, length us, event | category | flops | bytes accessed | tf_op | source)
XLA Modules:
  0.0 696.5 jit_solution(8686012108850524138)
XLA Ops:
  6.5 1.8 fusion.52
  10.9 2.1 convolution_convert_fusion.2
  18.3 6.7 collective-permute-start.4
  26.4 4.4 collective-permute-done.3
  36.6 2.0 copy.18
  38.6 2.0 copy.19
  40.6 1.9 copy.17
  42.5 3.1 pad_maximum_fusion
  47.7 3.5 fusion.24
  51.2 126.3 %all-reduce.3.cloned.1.call-done = (bf16[128,1024]{1,0:T(8,128)(2,1)}, bf16[128,1024]{1,0:T(8,128)(2,1)}) async-done(((bf16[128,1024]{1,0:T(8,128)(2,1)}, bf16[128,1024]{1,0:T(8,128)(2,1)}), (bf16[128,1024]{1,0:T(8,128)(2,1)}, bf16[128,1024]{1,0:T(8,128)(2,1)})) %all-reduce.3.cloned.1.call-update) | async-done | bytes 524304 | tf_op jit(solution)/shard_map/psum | solution.py:17
  180.3 1.8 copy.16
  182.1 2.9 multiply_reduce_fusion
  187.6 4.0 fusion.23
  191.6 2.8 fusion.30
  196.2 1.9 fusion.29
  198.9 3.0 fusion.35
  202.0 484.5 %while.23 = (s32[]{:T(128)}, f32[8,256]{1,0:T(8,128)S(1)}, f32[8,256]{1,0:T(8,128)S(1)}, f32[256,8,64]{0,2,1:T(8,128)}, bf16[4,128,1024]{1,0,2:T(4,128)(2,1)}, /...) while((s32[]{:T(128)}, f32[8,256]{1,0:T(8,128)S(1)}, ...), condition=%wide.region_9.10_spmd.clone, body=%wide.region_6.9_spmd.clone.sunk | while | flops 283777344 | bytes 30747068 | solution.py:154
  204.3 22.9 %collective-permute-done = bf16[4,128,1024]{1,0,2:T(4,128)(2,1)} collective-permute-done((bf16[4,128,1024]{1,0,2:T(4,128)(2,1)}, bf16[4,128,1024]{1,0,2:T(4,128)(2,1)}, u32[]{:S(2)}, u32[]{:S(2)}) %collective-permute-start) | collective-permute-done | bytes 1048608 | tf_op jit(solution)/shard_map/while/body/eval_jaxpr/ppermute | solution.py:39
  232.5 2.7 copy.58
  235.9 24.9 %collective-permute-done = bf16[4,128,1024]{1,0,2:T(4,128)(2,1)} collective-permute-done((bf16[4,128,1024]{1,0,2:T(4,128)(2,1)}, bf16[4,128,1024]{1,0,2:T(4,128)(2,1)}, u32[]{:S(2)}, u32[]{:S(2)}) %collective-permute-start) | collective-permute-done | bytes 1048608 | tf_op jit(solution)/shard_map/while/body/eval_jaxpr/ppermute | solution.py:39
  266.0 2.7 copy.58
  269.4 26.0 %collective-permute-done = bf16[4,128,1024]{1,0,2:T(4,128)(2,1)} collective-permute-done((bf16[4,128,1024]{1,0,2:T(4,128)(2,1)}, bf16[4,128,1024]{1,0,2:T(4,128)(2,1)}, u32[]{:S(2)}, u32[]{:S(2)}) %collective-permute-start) | collective-permute-done | bytes 1048608 | tf_op jit(solution)/shard_map/while/body/eval_jaxpr/ppermute | solution.py:39
  300.7 2.7 copy.58
  304.1 27.1 %collective-permute-done = bf16[4,128,1024]{1,0,2:T(4,128)(2,1)} collective-permute-done((bf16[4,128,1024]{1,0,2:T(4,128)(2,1)}, bf16[4,128,1024]{1,0,2:T(4,128)(2,1)}, u32[]{:S(2)}, u32[]{:S(2)}) %collective-permute-start) | collective-permute-done | bytes 1048608 | tf_op jit(solution)/shard_map/while/body/eval_jaxpr/ppermute | solution.py:39
  336.5 2.7 copy.58
  339.9 27.3 %collective-permute-done = bf16[4,128,1024]{1,0,2:T(4,128)(2,1)} collective-permute-done((bf16[4,128,1024]{1,0,2:T(4,128)(2,1)}, bf16[4,128,1024]{1,0,2:T(4,128)(2,1)}, u32[]{:S(2)}, u32[]{:S(2)}) %collective-permute-start) | collective-permute-done | bytes 1048608 | tf_op jit(solution)/shard_map/while/body/eval_jaxpr/ppermute | solution.py:39
  372.6 2.7 copy.58
  376.0 26.5 %collective-permute-done = bf16[4,128,1024]{1,0,2:T(4,128)(2,1)} collective-permute-done((bf16[4,128,1024]{1,0,2:T(4,128)(2,1)}, bf16[4,128,1024]{1,0,2:T(4,128)(2,1)}, u32[]{:S(2)}, u32[]{:S(2)}) %collective-permute-start) | collective-permute-done | bytes 1048608 | tf_op jit(solution)/shard_map/while/body/eval_jaxpr/ppermute | solution.py:39
  407.8 2.7 copy.58
  411.2 25.7 %collective-permute-done = bf16[4,128,1024]{1,0,2:T(4,128)(2,1)} collective-permute-done((bf16[4,128,1024]{1,0,2:T(4,128)(2,1)}, bf16[4,128,1024]{1,0,2:T(4,128)(2,1)}, u32[]{:S(2)}, u32[]{:S(2)}) %collective-permute-start) | collective-permute-done | bytes 1048608 | tf_op jit(solution)/shard_map/while/body/eval_jaxpr/ppermute | solution.py:39
  442.1 2.7 copy.58
  445.6 24.7 %collective-permute-done = bf16[4,128,1024]{1,0,2:T(4,128)(2,1)} collective-permute-done((bf16[4,128,1024]{1,0,2:T(4,128)(2,1)}, bf16[4,128,1024]{1,0,2:T(4,128)(2,1)}, u32[]{:S(2)}, u32[]{:S(2)}) %collective-permute-start) | collective-permute-done | bytes 1048608 | tf_op jit(solution)/shard_map/while/body/eval_jaxpr/ppermute | solution.py:39
  475.6 2.7 copy.58
  479.0 23.8 %collective-permute-done = bf16[4,128,1024]{1,0,2:T(4,128)(2,1)} collective-permute-done((bf16[4,128,1024]{1,0,2:T(4,128)(2,1)}, bf16[4,128,1024]{1,0,2:T(4,128)(2,1)}, u32[]{:S(2)}, u32[]{:S(2)}) %collective-permute-start) | collective-permute-done | bytes 1048608 | tf_op jit(solution)/shard_map/while/body/eval_jaxpr/ppermute | solution.py:39
  508.1 2.7 copy.58
  511.5 22.9 %collective-permute-done = bf16[4,128,1024]{1,0,2:T(4,128)(2,1)} collective-permute-done((bf16[4,128,1024]{1,0,2:T(4,128)(2,1)}, bf16[4,128,1024]{1,0,2:T(4,128)(2,1)}, u32[]{:S(2)}, u32[]{:S(2)}) %collective-permute-start) | collective-permute-done | bytes 1048608 | tf_op jit(solution)/shard_map/while/body/eval_jaxpr/ppermute | solution.py:39
  539.7 2.7 copy.58
  543.1 22.0 %collective-permute-done = bf16[4,128,1024]{1,0,2:T(4,128)(2,1)} collective-permute-done((bf16[4,128,1024]{1,0,2:T(4,128)(2,1)}, bf16[4,128,1024]{1,0,2:T(4,128)(2,1)}, u32[]{:S(2)}, u32[]{:S(2)}) %collective-permute-start) | collective-permute-done | bytes 1048608 | tf_op jit(solution)/shard_map/while/body/eval_jaxpr/ppermute | solution.py:39
  570.3 2.7 copy.58
  573.7 21.0 %collective-permute-done = bf16[4,128,1024]{1,0,2:T(4,128)(2,1)} collective-permute-done((bf16[4,128,1024]{1,0,2:T(4,128)(2,1)}, bf16[4,128,1024]{1,0,2:T(4,128)(2,1)}, u32[]{:S(2)}, u32[]{:S(2)}) %collective-permute-start) | collective-permute-done | bytes 1048608 | tf_op jit(solution)/shard_map/while/body/eval_jaxpr/ppermute | solution.py:39
  600.0 2.7 copy.58
  603.4 20.1 %collective-permute-done = bf16[4,128,1024]{1,0,2:T(4,128)(2,1)} collective-permute-done((bf16[4,128,1024]{1,0,2:T(4,128)(2,1)}, bf16[4,128,1024]{1,0,2:T(4,128)(2,1)}, u32[]{:S(2)}, u32[]{:S(2)}) %collective-permute-start) | collective-permute-done | bytes 1048608 | tf_op jit(solution)/shard_map/while/body/eval_jaxpr/ppermute | solution.py:39
  628.9 2.7 copy.58
  632.3 19.2 %collective-permute-done = bf16[4,128,1024]{1,0,2:T(4,128)(2,1)} collective-permute-done((bf16[4,128,1024]{1,0,2:T(4,128)(2,1)}, bf16[4,128,1024]{1,0,2:T(4,128)(2,1)}, u32[]{:S(2)}, u32[]{:S(2)}) %collective-permute-start) | collective-permute-done | bytes 1048608 | tf_op jit(solution)/shard_map/while/body/eval_jaxpr/ppermute | solution.py:39
  656.7 2.7 copy.58
  660.1 18.3 %collective-permute-done = bf16[4,128,1024]{1,0,2:T(4,128)(2,1)} collective-permute-done((bf16[4,128,1024]{1,0,2:T(4,128)(2,1)}, bf16[4,128,1024]{1,0,2:T(4,128)(2,1)}, u32[]{:S(2)}, u32[]{:S(2)}) %collective-permute-start) | collective-permute-done | bytes 1048608 | tf_op jit(solution)/shard_map/while/body/eval_jaxpr/ppermute | solution.py:39
  683.7 2.7 copy.58
  687.5 2.1 convolution_convert_fusion.1
  (390 shorter events, 115.2 us)
Async XLA Ops:
  6.5 24.4 %copy-start = (bf16[1536,1024]{1,0:T(8,128)(2,1)S(1)}, bf16[1536,1024]{1,0:T(8,128)(2,1)}, u32[]{:S(2)}) copy-start(bf16[1536,1024]{1,0:T(8,128)(2,1)} %param.10) | copy-start | bytes 9437188
  6.5 24.4 %copy-start.1 = (bf16[2,128,512]{2,1,0:T(8,128)(2,1)S(1)}, bf16[2,128,512]{2,1,0:T(8,128)(2,1)}, u32[]{:S(2)}) copy-start(bf16[2,128,512]{2,1,0:T(8,128)(2,1)} %param.7) | copy-start | bytes 786436
  6.5 170.9 %all-reduce.3.cloned.1.call-start = ((), (), s32[]{:S(2)}) async-start(), calls=%async_computation | async-start | bytes 1048576 | tf_op jit(solution)/shard_map/psum | solution.py:17
  8.4 8.0 %collective-permute-start.1 = (bf16[1,128,512]{2,1,0:T(8,128)(2,1)}, bf16[1,128,512]{2,1,0:T(8,128)(2,1)S(1)}, u32[]{:S(2)}, u32[]{:S(2)}) collective-permute-start(bf16[1,128,512]{2,1,0:T(8,128)(2,1)} %get-tuple-element.393), channel_id=1, source_target_pairs={{0,16},{16,32},{32,48},{48,64},{64,80},{80,96},{96,112},{112,128},... | collective-permute-start | bytes 393224 | tf_op jit(solution)/shard_map/ppermute | solution.py:27
  8.4 9.0 %collective-permute-start.2 = (bf16[1,128,512]{2,1,0:T(8,128)(2,1)}, bf16[1,128,512]{2,1,0:T(8,128)(2,1)}, u32[]{:S(2)}, u32[]{:S(2)}) collective-permute-start(bf16[1,128,512]{2,1,0:T(8,128)(2,1)} %get-tuple-element.392), channel_id=1, source_target_pairs={{16,0},{32,16},{48,32},{64,48},{80,64},{96,80},{112,96},{128,112},... | collective-permute-start | bytes 393224 | tf_op jit(solution)/shard_map/ppermute | solution.py:29
  10.1 5.2 copy-start.13
  10.9 21.1 %copy-start.15 = (pred[4]{0:T(512)(128)(4,1)}, pred[4]{0:T(512)(128)(4,1)S(1)}, u32[]{:S(2)}) copy-start(pred[4]{0:T(512)(128)(4,1)S(1)} %broadcast_compare_fusion.2) | copy-start | bytes 16
  18.3 8.0 %collective-permute-start.4 = (bf16[4,1,512]{2,1,0:T(2,128)(2,1)S(1)}, bf16[4,1,512]{2,1,0:T(2,128)(2,1)S(1)}, u32[]{:S(2)}, u32[]{:S(2)}) collective-permute-start(bf16[4,1,512]{2,1,0:T(2,128)(2,1)S(1)} %get-tuple-element.391), channel_id=1, source_target_pairs={{1,0},{2,1},{3,2},{4,3},{5,4},{6,5},{7,6},{8,7},{9,8},{10,9},{11,1... | collective-permute-start | bytes 12296 | tf_op jit(solution)/shard_map/ppermute | solution.py:29
  25.0 5.8 collective-permute-start.3
  33.9 4.7 collective-permute-start.6
  33.9 6.7 collective-permute-start.5
  34.4 12.4 %copy-start.10 = (f32[4]{0:T(128)}, f32[4]{0:T(128)S(1)}, u32[]{:S(2)}) copy-start(f32[4]{0:T(128)S(1)} %select_log_fusion) | copy-start | bytes 52
  36.6 11.1 %copy-start.12 = (f32[512]{0:T(512)}, f32[512]{0:T(512)S(1)}, u32[]{:S(2)}) copy-start(f32[512]{0:T(512)S(1)} %broadcast_bitcast_fusion.1) | copy-start | bytes 6148
  182.1 9.5 %copy-start.2 = (f32[8,256,512]{2,1,0:T(8,128)S(1)}, f32[8,256,512]{2,1,0:T(8,128)}, u32[]{:S(2)}) copy-start(f32[8,256,512]{2,1,0:T(8,128)} %get-tuple-element.401) | copy-start | bytes 12582916
  182.1 9.5 %copy-start.7 = (bf16[512,512]{0,1:T(8,128)(2,1)S(1)}, bf16[512,512]{0,1:T(8,128)(2,1)}, u32[]{:S(2)}) copy-start(bf16[512,512]{0,1:T(8,128)(2,1)} %get-tuple-element.382) | copy-start | bytes 1572868
  194.4 7.5 %copy-start.9 = (s32[2]{0:T(128)S(1)}, s32[2]{0:T(128)}, u32[]{:S(2)}) copy-start(s32[2]{0:T(128)} %copy-done.8) | copy-start | bytes 28
  194.4 7.5 %copy-start.11 = (f32[4]{0:T(128)S(1)}, f32[4]{0:T(128)}, u32[]{:S(2)}) copy-start(f32[4]{0:T(128)} %copy-done.10) | copy-start | bytes 52
  194.4 7.5 %copy-start.14 = (s32[2]{0:T(128)S(1)}, s32[2]{0:T(128)}, u32[]{:S(2)}) copy-start(s32[2]{0:T(128)} %copy-done.13) | copy-start | bytes 28
  194.4 7.5 %copy-start.16 = (pred[4]{0:T(512)(128)(4,1)S(1)}, pred[4]{0:T(512)(128)(4,1)}, u32[]{:S(2)}) copy-start(pred[4]{0:T(512)(128)(4,1)} %copy-done.15) | copy-start | bytes 16
  202.2 25.0 %collective-permute-start = (bf16[4,128,1024]{1,0,2:T(4,128)(2,1)}, bf16[4,128,1024]{1,0,2:T(4,128)(2,1)}, u32[]{:S(2)}, u32[]{:S(2)}) collective-permute-start(bf16[4,128,1024]{1,0,2:T(4,128)(2,1)} %get-tuple-element.510), channel_id=1, source_target_pairs={{0,1},{1,2},{2,3},{3,4},{4,5},{5,6},{6,7},{7,8},{8,9},{9,10},{10,1... | collective-permute-start | bytes 3145736 | tf_op jit(solution)/shard_map/while/body/eval_jaxpr/ppermute | solution.py:39
  232.4 2.8 copy-start.6
  235.2 25.5 %collective-permute-start = (bf16[4,128,1024]{1,0,2:T(4,128)(2,1)}, bf16[4,128,1024]{1,0,2:T(4,128)(2,1)}, u32[]{:S(2)}, u32[]{:S(2)}) collective-permute-start(bf16[4,128,1024]{1,0,2:T(4,128)(2,1)} %get-tuple-element.510), channel_id=1, source_target_pairs={{0,1},{1,2},{2,3},{3,4},{4,5},{5,6},{6,7},{7,8},{8,9},{9,10},{10,1... | collective-permute-start | bytes 3145736 | tf_op jit(solution)/shard_map/while/body/eval_jaxpr/ppermute | solution.py:39
  266.0 2.8 copy-start.6
  268.8 26.6 %collective-permute-start = (bf16[4,128,1024]{1,0,2:T(4,128)(2,1)}, bf16[4,128,1024]{1,0,2:T(4,128)(2,1)}, u32[]{:S(2)}, u32[]{:S(2)}) collective-permute-start(bf16[4,128,1024]{1,0,2:T(4,128)(2,1)} %get-tuple-element.510), channel_id=1, source_target_pairs={{0,1},{1,2},{2,3},{3,4},{4,5},{5,6},{6,7},{7,8},{8,9},{9,10},{10,1... | collective-permute-start | bytes 3145736 | tf_op jit(solution)/shard_map/while/body/eval_jaxpr/ppermute | solution.py:39
  300.7 2.8 copy-start.6
  303.4 27.8 %collective-permute-start = (bf16[4,128,1024]{1,0,2:T(4,128)(2,1)}, bf16[4,128,1024]{1,0,2:T(4,128)(2,1)}, u32[]{:S(2)}, u32[]{:S(2)}) collective-permute-start(bf16[4,128,1024]{1,0,2:T(4,128)(2,1)} %get-tuple-element.510), channel_id=1, source_target_pairs={{0,1},{1,2},{2,3},{3,4},{4,5},{5,6},{6,7},{7,8},{8,9},{9,10},{10,1... | collective-permute-start | bytes 3145736 | tf_op jit(solution)/shard_map/while/body/eval_jaxpr/ppermute | solution.py:39
  336.5 2.8 copy-start.6
  339.3 28.0 %collective-permute-start = (bf16[4,128,1024]{1,0,2:T(4,128)(2,1)}, bf16[4,128,1024]{1,0,2:T(4,128)(2,1)}, u32[]{:S(2)}, u32[]{:S(2)}) collective-permute-start(bf16[4,128,1024]{1,0,2:T(4,128)(2,1)} %get-tuple-element.510), channel_id=1, source_target_pairs={{0,1},{1,2},{2,3},{3,4},{4,5},{5,6},{6,7},{7,8},{8,9},{9,10},{10,1... | collective-permute-start | bytes 3145736 | tf_op jit(solution)/shard_map/while/body/eval_jaxpr/ppermute | solution.py:39
  372.5 2.8 copy-start.6
  375.3 27.2 %collective-permute-start = (bf16[4,128,1024]{1,0,2:T(4,128)(2,1)}, bf16[4,128,1024]{1,0,2:T(4,128)(2,1)}, u32[]{:S(2)}, u32[]{:S(2)}) collective-permute-start(bf16[4,128,1024]{1,0,2:T(4,128)(2,1)} %get-tuple-element.510), channel_id=1, source_target_pairs={{0,1},{1,2},{2,3},{3,4},{4,5},{5,6},{6,7},{7,8},{8,9},{9,10},{10,1... | collective-permute-start | bytes 3145736 | tf_op jit(solution)/shard_map/while/body/eval_jaxpr/ppermute | solution.py:39
  407.8 2.8 copy-start.6
  410.5 26.3 %collective-permute-start = (bf16[4,128,1024]{1,0,2:T(4,128)(2,1)}, bf16[4,128,1024]{1,0,2:T(4,128)(2,1)}, u32[]{:S(2)}, u32[]{:S(2)}) collective-permute-start(bf16[4,128,1024]{1,0,2:T(4,128)(2,1)} %get-tuple-element.510), channel_id=1, source_target_pairs={{0,1},{1,2},{2,3},{3,4},{4,5},{5,6},{6,7},{7,8},{8,9},{9,10},{10,1... | collective-permute-start | bytes 3145736 | tf_op jit(solution)/shard_map/while/body/eval_jaxpr/ppermute | solution.py:39
  442.1 2.8 copy-start.6
  444.9 25.4 %collective-permute-start = (bf16[4,128,1024]{1,0,2:T(4,128)(2,1)}, bf16[4,128,1024]{1,0,2:T(4,128)(2,1)}, u32[]{:S(2)}, u32[]{:S(2)}) collective-permute-start(bf16[4,128,1024]{1,0,2:T(4,128)(2,1)} %get-tuple-element.510), channel_id=1, source_target_pairs={{0,1},{1,2},{2,3},{3,4},{4,5},{5,6},{6,7},{7,8},{8,9},{9,10},{10,1... | collective-permute-start | bytes 3145736 | tf_op jit(solution)/shard_map/while/body/eval_jaxpr/ppermute | solution.py:39
  475.6 2.8 copy-start.6
  478.3 24.5 %collective-permute-start = (bf16[4,128,1024]{1,0,2:T(4,128)(2,1)}, bf16[4,128,1024]{1,0,2:T(4,128)(2,1)}, u32[]{:S(2)}, u32[]{:S(2)}) collective-permute-start(bf16[4,128,1024]{1,0,2:T(4,128)(2,1)} %get-tuple-element.510), channel_id=1, source_target_pairs={{0,1},{1,2},{2,3},{3,4},{4,5},{5,6},{6,7},{7,8},{8,9},{9,10},{10,1... | collective-permute-start | bytes 3145736 | tf_op jit(solution)/shard_map/while/body/eval_jaxpr/ppermute | solution.py:39
  508.1 2.8 copy-start.6
  510.8 23.5 %collective-permute-start = (bf16[4,128,1024]{1,0,2:T(4,128)(2,1)}, bf16[4,128,1024]{1,0,2:T(4,128)(2,1)}, u32[]{:S(2)}, u32[]{:S(2)}) collective-permute-start(bf16[4,128,1024]{1,0,2:T(4,128)(2,1)} %get-tuple-element.510), channel_id=1, source_target_pairs={{0,1},{1,2},{2,3},{3,4},{4,5},{5,6},{6,7},{7,8},{8,9},{9,10},{10,1... | collective-permute-start | bytes 3145736 | tf_op jit(solution)/shard_map/while/body/eval_jaxpr/ppermute | solution.py:39
  539.6 2.8 copy-start.6
  542.4 22.6 %collective-permute-start = (bf16[4,128,1024]{1,0,2:T(4,128)(2,1)}, bf16[4,128,1024]{1,0,2:T(4,128)(2,1)}, u32[]{:S(2)}, u32[]{:S(2)}) collective-permute-start(bf16[4,128,1024]{1,0,2:T(4,128)(2,1)} %get-tuple-element.510), channel_id=1, source_target_pairs={{0,1},{1,2},{2,3},{3,4},{4,5},{5,6},{6,7},{7,8},{8,9},{9,10},{10,1... | collective-permute-start | bytes 3145736 | tf_op jit(solution)/shard_map/while/body/eval_jaxpr/ppermute | solution.py:39
  570.3 2.8 copy-start.6
  573.1 21.7 %collective-permute-start = (bf16[4,128,1024]{1,0,2:T(4,128)(2,1)}, bf16[4,128,1024]{1,0,2:T(4,128)(2,1)}, u32[]{:S(2)}, u32[]{:S(2)}) collective-permute-start(bf16[4,128,1024]{1,0,2:T(4,128)(2,1)} %get-tuple-element.510), channel_id=1, source_target_pairs={{0,1},{1,2},{2,3},{3,4},{4,5},{5,6},{6,7},{7,8},{8,9},{9,10},{10,1... | collective-permute-start | bytes 3145736 | tf_op jit(solution)/shard_map/while/body/eval_jaxpr/ppermute | solution.py:39
  600.0 2.8 copy-start.6
  602.8 20.8 %collective-permute-start = (bf16[4,128,1024]{1,0,2:T(4,128)(2,1)}, bf16[4,128,1024]{1,0,2:T(4,128)(2,1)}, u32[]{:S(2)}, u32[]{:S(2)}) collective-permute-start(bf16[4,128,1024]{1,0,2:T(4,128)(2,1)} %get-tuple-element.510), channel_id=1, source_target_pairs={{0,1},{1,2},{2,3},{3,4},{4,5},{5,6},{6,7},{7,8},{8,9},{9,10},{10,1... | collective-permute-start | bytes 3145736 | tf_op jit(solution)/shard_map/while/body/eval_jaxpr/ppermute | solution.py:39
  628.8 2.8 copy-start.6
  631.6 19.8 %collective-permute-start = (bf16[4,128,1024]{1,0,2:T(4,128)(2,1)}, bf16[4,128,1024]{1,0,2:T(4,128)(2,1)}, u32[]{:S(2)}, u32[]{:S(2)}) collective-permute-start(bf16[4,128,1024]{1,0,2:T(4,128)(2,1)} %get-tuple-element.510), channel_id=1, source_target_pairs={{0,1},{1,2},{2,3},{3,4},{4,5},{5,6},{6,7},{7,8},{8,9},{9,10},{10,1... | collective-permute-start | bytes 3145736 | tf_op jit(solution)/shard_map/while/body/eval_jaxpr/ppermute | solution.py:39
  656.7 2.8 copy-start.6
  659.5 18.9 %collective-permute-start = (bf16[4,128,1024]{1,0,2:T(4,128)(2,1)}, bf16[4,128,1024]{1,0,2:T(4,128)(2,1)}, u32[]{:S(2)}, u32[]{:S(2)}) collective-permute-start(bf16[4,128,1024]{1,0,2:T(4,128)(2,1)} %get-tuple-element.510), channel_id=1, source_target_pairs={{0,1},{1,2},{2,3},{3,4},{4,5},{5,6},{6,7},{7,8},{8,9},{9,10},{10,1... | collective-permute-start | bytes 3145736 | tf_op jit(solution)/shard_map/while/body/eval_jaxpr/ppermute | solution.py:39
  (19 other events, 41.6 us)
Sparse Core Ops, SparseCore 0:
  38.7 138.6 all-reduce.2
where the time goes:
time: 698 us; the launch traced here: 696 us
  waiting for transfers between devices  483 us (69%)
  local copies, waits for them, and re-layouts  87.9 us (13%)
  matrix products  54 us (8%)
  other arithmetic  45.7 us (7%)
  between operations  13.6 us (2%)
  starting transfers between devices  10.4 us (1%)
    ppermute x15, waiting for transfers between devices, passed_along(): return lax.ppermute(value, axis, pairs)  352 us
    psum x1, waiting for transfers between devices, from_root(): return lax.psum(block, axis)  126 us
    while x120, local copies, waits for them, and re-layouts  63.5 us
    dot_general x17, matrix products, absorb(): jnp.einsum('hqk,khd->qhd', exp_scores.astype(jnp.bfloat16), value_part, p...  26.1 us
    reduce_sum x17, other arithmetic, absorb(): denominator = denominator * shrink + jnp.sum(exp_scores, axis=2)  25.4 us
    dot_general x17, matrix products, absorb(): jnp.einsum('qhd,khd->hqk', queries, key_part, preferred_element_type=jnp....  22.7 us
  transfers between devices with their start and end apart: 22, of which 18 were waited for; matrix products, arithmetic and copies ran while one was open for 5% of the time, Pallas kernels for 0%

commit v1 on v0

v1 whole, which is shorter than its diff:
```python
import jax
import jax.numpy as jnp
import numpy as np
from jax import lax
from jax.experimental import pallas as pl
from jax.experimental.pallas import tpu as pltpu
from jax.sharding import PartitionSpec as P

HEADS = 8
HDIM = 64
PAIRS = 4
LANES = 128
MASKED = -1e30
F32 = jnp.float32
BF16 = jnp.bfloat16
VMEM = pl.BlockSpec(memory_space=pltpu.VMEM)
SMEM = pl.BlockSpec(memory_space=pltpu.SMEM)
PARAMS = pltpu.CompilerParams(vmem_limit_bytes=48 * 1024 * 1024)


def cost(flops, nbytes):
    return pl.CostEstimate(flops=flops, bytes_accessed=nbytes, transcendentals=0)


def row_weight(row_ids, row_total):
    inside = (row_ids >= 0) & (row_ids < row_total)
    clipped = jnp.clip(row_ids, 0, row_total - 1).astype(F32)
    return jnp.where(inside, jnp.sin(jnp.pi * (clipped + 0.5) / row_total), jnp.zeros_like(clipped))


def lane_ids(shape):
    return lax.broadcasted_iota(jnp.int32, shape, len(shape) - 1)


def dot_nn(a, b):
    return lax.dot_general(a, b, (((1,), (0,)), ((), ())), preferred_element_type=F32)


def dot_nt(a, b):
    return lax.dot_general(a, b, (((1,), (1,)), ((), ())), preferred_element_type=F32)


def three_parts(x):
    a = x.astype(BF16)
    rest = x - a.astype(F32)
    b = rest.astype(BF16)
    c = (rest - b.astype(F32)).astype(BF16)
    return a.astype(F32), b.astype(F32), c.astype(F32)


def early_kernel(f_ref, wq_ref, wk_ref, q_ref, base_ref):
    f = f_ref[...].reshape(256, 512)
    q = dot_nn(f, wq_ref[...]).astype(BF16) * jnp.asarray(HDIM ** -0.5, BF16)
    for p in range(PAIRS):
        q_ref[p] = q[:, p * LANES : (p + 1) * LANES].reshape(2, 128, LANES)
    base_ref[...] = dot_nn(f, wk_ref[...])


def keyval_kernel(coef_ref, f_ref, up_ref, dn_ref, west_ref, east_ref, base_ref, w1_ref, w2_ref, kv_ref):
    rows = [up_ref[0], f_ref[0], f_ref[1], dn_ref[0]]
    rows = [r.astype(F32) for r in rows]
    cell = lax.broadcasted_iota(jnp.int32, (128, 512), 0)
    lat, lon = [], []
    for r in range(2):
        lat.append((coef_ref[2 * r] * rows[r] + coef_ref[2 * r + 1] * rows[r + 2]).astype(BF16))
        mid = rows[r + 1]
        w = jnp.where(cell == 0, west_ref[r].astype(F32), pltpu.roll(mid, 1, 0))
        e = jnp.where(cell == 127, east_ref[r].astype(F32), pltpu.roll(mid, 127, 0))
        lon.append((0.5 * (w + e)).astype(BF16))
    lat = jnp.concatenate(lat, axis=0)
    lon = jnp.concatenate(lon, axis=0)
    low = lane_ids((256, LANES)) < HDIM
    for p in range(PAIRS):
        parts = []
        for side in range(2):
            c = slice(512 * side + p * LANES, 512 * side + (p + 1) * LANES)
            parts.append(base_ref[:, c] + dot_nn(lat, w1_ref[:, c]) + dot_nn(lon, w2_ref[:, c]))
        k, v = parts
        v = pltpu.roll(v, HDIM, 1)
        kv_ref[2 * p] = jnp.where(low, k, v).astype(BF16).reshape(2, 128, LANES)
        kv_ref[2 * p + 1] = jnp.where(low, v, k).astype(BF16).reshape(2, 128, LANES)


def window_kernel(
    width_ref, log_ref, q_ref, qn_ref, qs_ref, kv_ref, kvw_ref, kve_ref, pn_ref, ps_ref,
    o_ref, st_ref, rn_ref, rs_ref, bias_a, bias_b,
):
    ahead = lax.broadcasted_iota(jnp.int32, (128, 384), 1) - 128
    here = lax.broadcasted_iota(jnp.int32, (128, 384), 0)
    gap = jnp.abs(ahead - here)
    for t in range(4):
        inside = gap <= width_ref[t]
        if t < 3:
            bias_a[t * 128 : (t + 1) * 128] = jnp.where(inside, log_ref[0], MASKED)
        if t > 0:
            bias_b[(t - 1) * 128 : t * 128] = jnp.where(inside, log_ref[1], MASKED)
    low = lane_ids((128, LANES)) < HDIM
    lane = lane_ids((128, LANES))
    ones = jnp.ones((384, LANES), BF16)
    stats = [jnp.zeros((128, LANES), F32) for _ in range(4)]
    for p in range(PAIRS):
        halves = []
        for odd in range(2):
            h = 2 * p + odd
            keep = (lane >= HDIM) if odd else low
            qs = [qn_ref[p], q_ref[p, 0], q_ref[p, 1], qs_ref[p]]
            qs = [jnp.where(keep, x, jnp.zeros_like(x)) for x in qs]
            kva = jnp.concatenate([kvw_ref[h, 0], kv_ref[h, 0], kve_ref[h, 0]], axis=0)
            kvb = jnp.concatenate([kvw_ref[h, 1], kv_ref[h, 1], kve_ref[h, 1]], axis=0)
            kvp = jnp.concatenate([pn_ref[h], ps_ref[h]], axis=0)
            sa = dot_nt(jnp.concatenate(qs[:3], axis=0), kva) + bias_a[...]
            sb = dot_nt(jnp.concatenate(qs[1:], axis=0), kvb) + bias_b[...]
            sp = dot_nt(jnp.concatenate(qs[1:3], axis=0), kvp)
            ma = jnp.max(sa, axis=1, keepdims=True)
            mb = jnp.max(sb, axis=1, keepdims=True)
            mp = jnp.max(sp, axis=1, keepdims=True)
            mid = jnp.maximum(jnp.maximum(ma[128:], mb[:256]), mp)
            mn = ma[:128]
            ms = mb[256:]
            pa = jnp.exp(sa - jnp.concatenate([mn, mid], axis=0)).astype(BF16)
            pb = jnp.exp(sb - jnp.concatenate([mid, ms], axis=0)).astype(BF16)
            pp = jnp.exp(sp - mid).astype(BF16)
            oa = dot_nn(pa, jnp.concatenate([kva, ones], axis=1))
            ob = dot_nn(pb, jnp.concatenate([kvb, ones], axis=1))
            op = dot_nn(pp, jnp.concatenate([kvp, ones[:256]], axis=1))
            om = oa[128:] + ob[:256] + op
            full = [oa[:128], om[:128], om[128:], ob[256:]]
            tops = [mn, mid[:128], mid[128:], ms]
            halves.append([x[:, :LANES] / x[:, LANES:] for x in full])
            for t in range(4):
                parts = three_parts(tops[t] + jnp.log(full[t][:, LANES:]))
                for i in range(3):
                    stats[t] = jnp.where(lane == 3 * h + i, parts[i], stats[t])
        both = [jnp.where(low, halves[1][t], halves[0][t]) for t in range(4)]
        rn_ref[p] = both[0].astype(BF16)
        o_ref[p, 0] = both[1]
        o_ref[p, 1] = both[2]
        rs_ref[p] = both[3].astype(BF16)
    rn_ref[PAIRS] = stats[0].astype(BF16)
    st_ref[0] = stats[1].astype(BF16)
    st_ref[1] = stats[2].astype(BF16)
    rs_ref[PAIRS] = stats[3].astype(BF16)


def polar_kernel(odd_ref, log_ref, q_ref, kv_ref, out_ref, wide):
    odd = odd_ref[0]
    wide[:, :LANES] = kv_ref[...].reshape(2048, LANES)
    wide[:, LANES:] = jnp.ones((2048, LANES), BF16)
    lane = lane_ids((128, LANES))
    keep = (lane // HDIM) == odd
    start = odd * HDIM

    def block(b, carry):
        q = q_ref[b]
        q = jnp.where(keep, q, jnp.zeros_like(q))
        s = dot_nt(q, wide[:, :LANES])
        m = jnp.max(s, axis=1, keepdims=True)
        e = jnp.exp(s - m).astype(BF16)
        full = dot_nn(e, wide[...])
        total = full[:, LANES:]
        out = full[:, :LANES] / total
        parts = three_parts(m + jnp.log(total) + log_ref[0])
        for i in range(3):
            out = jnp.where(lane == start + i, parts[i], out)
        out_ref[b] = out.astype(BF16)
        return carry

    lax.fori_loop(0, 8, block, 0, unroll=2)


def final_kernel(role_ref, o_ref, st_ref, ra_ref, rb_ref, p1_ref, p2_ref, wo_ref, out_ref, att):
    src = lax.broadcasted_iota(jnp.int32, (LANES, 512), 0) // 3
    dst = lax.broadcasted_iota(jnp.int32, (LANES, 512), 1)
    head = 2 * (dst // LANES) + jnp.where(dst % LANES < HDIM, 1, 0)
    pick = jnp.where(src == head, 1.0, 0.0).astype(BF16)
    for r, ret in ((0, ra_ref), (1, rb_ref)):
        lse = dot_nn(st_ref[r], pick)
        lse_ret = jnp.where(role_ref[r] == 1, MASKED, dot_nn(ret[PAIRS], pick))
        mine = jnp.concatenate([o_ref[p, r] for p in range(PAIRS)], axis=1)
        other = jnp.concatenate([ret[p] for p in range(PAIRS)], axis=1).astype(F32)
        other = jnp.where(role_ref[r] == 1, 0.0, other)
        top = jnp.maximum(lse, lse_ret)
        wa = jnp.exp(lse - top)
        wb = jnp.exp(lse_ret - top)
        att[r * 128 : (r + 1) * 128] = ((mine * wa + other * wb) / (wa + wb)).astype(BF16)

        @pl.when(role_ref[r] == 1)
        def _():
            lane = lane_ids((128, LANES))
            row = lax.broadcasted_iota(jnp.int32, (LANES, LANES), 0)
            col = lax.broadcasted_iota(jnp.int32, (LANES, LANES), 1)
            pick_even = jnp.where((row < 3) & (col >= HDIM), 1.0, 0.0).astype(BF16)
            pick_odd = jnp.where((row >= HDIM) & (row < HDIM + 3) & (col < HDIM), 1.0, 0.0).astype(BF16)
            for p in range(PAIRS):
                mo = o_ref[p, r]
                ml = lse[:, p * LANES : (p + 1) * LANES]
                vals, logs = [], []
                for ref in (p1_ref, p2_ref):
                    even, odd = ref[2 * p], ref[2 * p + 1]
                    vals.append(jnp.where(lane < HDIM, odd, even).astype(F32))
                    logs.append(dot_nn(even, pick_even) + dot_nn(odd, pick_odd))
                best = jnp.maximum(ml, jnp.maximum(logs[0], logs[1]))
                w0 = jnp.exp(ml - best)
                w1 = jnp.exp(logs[0] - best)
                w2 = jnp.exp(logs[1] - best)
                merged = (mo * w0 + vals[0] * w1 + vals[1] * w2) / (w0 + w1 + w2)
                att[r * 128 : (r + 1) * 128, p * LANES : (p + 1) * LANES] = merged.astype(BF16)

    order = []
    for p in range(PAIRS):
        order += [wo_ref[p * LANES + HDIM : (p + 1) * LANES], wo_ref[p * LANES : p * LANES + HDIM]]
    w = jnp.concatenate(order, axis=0)
    out_ref[...] = dot_nn(att[...], w).astype(BF16).reshape(2, 128, 512)


def call(kernel, outs, in_specs, flops, nbytes, scratch=()):
    return pl.pallas_call(
        kernel,
        out_shape=outs,
        grid=(1,),
        in_specs=in_specs,
        out_specs=jax.tree.map(lambda _: VMEM, outs),
        scratch_shapes=list(scratch),
        compiler_params=PARAMS,
        cost_estimate=cost(flops, nbytes),
    )


def sds(shape, dtype=BF16):
    return jax.ShapeDtypeStruct(shape, dtype)


def ring(n, k):
    return [(i, (i + k) % n) for i in range(n)]


def line(n, k):
    return [(i, i + k) for i in range(n) if 0 <= i + k < n]


def body(gf, widths, wq, wkv, wo):
    nlat, nlon = 16, 16
    total = 32
    li = lax.axis_index("lat")
    lj = lax.axis_index("lon")
    first = 2 * li
    even = li % 2 == 0
    swap = [(i, i ^ 1) for i in range(nlat)]
    groups = [list(range(8)), list(range(8, 16))]

    up = lax.ppermute(gf[1:2], "lat", line(nlat, 1))
    dn = lax.ppermute(gf[0:1], "lat", line(nlat, -1))
    west = lax.ppermute(gf[:, 127:], "lon", ring(nlon, 1))
    east = lax.ppermute(gf[:, :1], "lon", ring(nlon, -1))

    wspec = lambda b: pl.BlockSpec((512, 1024), lambda i: (b, 0))
    q, base = call(
        early_kernel,
        (sds((PAIRS, 2, 128, LANES)), sds((256, 1024), F32)),
        [VMEM, VMEM, wspec(0)],
        400_000_000, 3_000_000,
    )(gf, wq, wkv)

    rows = first + jnp.arange(2, dtype=jnp.int32)
    uw, lw = row_weight(rows - 1, total), row_weight(rows + 1, total)
    coef = jnp.stack([uw / (uw + lw), lw / (uw + lw)], axis=1).reshape(4)
    kv = call(
        keyval_kernel, sds((HEADS, 2, 128, LANES)),
        [SMEM] + [VMEM] * 6 + [wspec(1), wspec(2)],
        600_000_000, 4_000_000,
    )(coef, gf, up, dn, west, east, base, wkv, wkv)

    q_a, q_b = q[:, 0], q[:, 1]
    kv_a, kv_b = kv[:, 0], kv[:, 1]
    got_q = lax.ppermute(jnp.where(even, q_a, q_b), "lat", swap)
    got_kv = lax.ppermute(jnp.where(even, kv_b, kv_a), "lat", swap)
    polar_q = jnp.where(li == 0, q_a, jnp.where(li == nlat - 1, q_b, got_q))
    polar_kv = jnp.where(li == 0, kv_a, jnp.where(li == nlat - 1, kv_b, got_kv))
    all_kv = lax.all_to_all(jnp.concatenate([polar_kv, polar_kv], axis=0), "lon", 0, 0)
    all_q = lax.all_to_all(jnp.repeat(polar_q, 2, axis=0), "lon", 0, 0, axis_index_groups=groups)

    kvw = lax.ppermute(kv, "lon", ring(nlon, 1))
    kve = lax.ppermute(kv, "lon", ring(nlon, -1))
    qn = lax.ppermute(q_b, "lat", line(nlat, 1))
    qs = lax.ppermute(q_a, "lat", line(nlat, -1))

    x = jnp.where(li == nlat - 1, kv_b, kv_a)
    for pairs in (
        [(0, 8), (15, 7)],
        [(0, 4), (8, 12), (15, 11), (7, 3)],
        [(0, 2), (4, 6), (8, 10), (12, 14), (15, 13), (11, 9), (7, 5), (3, 1)],
    ):
        got = lax.ppermute(x, "lat", pairs)
        here = np.zeros(nlat, bool)
        here[[b for _, b in pairs]] = True
        x = jnp.where(jnp.asarray(here)[li], got, x)
    got = lax.ppermute(x, "lat", swap)
    pole_n = jnp.where(even, x, got)
    pole_s = jnp.where(even, got, x)

    near = first - 1 + jnp.arange(4, dtype=jnp.int32)
    reach = widths[jnp.clip(near, 0, total - 1)]
    reach = jnp.where((near <= 0) | (near >= total - 1), -1, reach)
    logs = jnp.log(row_weight(rows, total))
    o, st, ret_n, ret_s = call(
        window_kernel,
        (sds((PAIRS, 2, 128, LANES), F32), sds((2, 128, LANES)),
         sds((PAIRS + 1, 128, LANES)), sds((PAIRS + 1, 128, LANES))),
        [SMEM, SMEM] + [VMEM] * 8,
        8_000_000_000, 4_000_000,
        [pltpu.VMEM((384, 384), F32), pltpu.VMEM((384, 384), F32)],
    )(reach, logs, q, qn, qs, kv, kvw, kve, pole_n, pole_s)
    ret_b = lax.ppermute(ret_n, "lat", line(nlat, -1))
    ret_a = lax.ppermute(ret_s, "lat", line(nlat, 1))

    is_pole = (li == 0) | (li == nlat - 1)
    pole_log = jnp.log(row_weight(jnp.where(is_pole, 0, 1), total)).reshape(1)
    part = call(
        polar_kernel, sds((8, 128, LANES)), [SMEM, SMEM, VMEM, VMEM],
        6_000_000_000, 2_000_000, [pltpu.VMEM((2048, 2 * LANES), BF16)],
    )((lj % 2).reshape(1).astype(jnp.int32), pole_log, all_q, all_kv)
    part = lax.all_to_all(part, "lon", 0, 0, axis_index_groups=groups)
    part2 = lax.ppermute(part, "lat", swap)

    role = jnp.stack([li == 0, li == nlat - 1]).astype(jnp.int32)
    return call(
        final_kernel, sds((2, 128, 512)), [SMEM] + [VMEM] * 7,
        1_000_000_000, 3_000_000, [pltpu.VMEM((256, 512), BF16)],
    )(role, o, st, ret_a, ret_b, part, part2, wo)


def solution(mesh):
    in_specs = (P("lat", "lon", None), P(), P(), P(), P())
    return jax.shard_map(body, mesh=mesh, in_specs=in_specs, out_specs=P("lat", "lon", None), check_vma=False)
```

time: 698 us -> 127 us (0.18)
  the two profiles are of different devices: /device:TPU:22 before, /device:TPU:7 now
where the time goes in v1:
time: 127 us; the launch traced here: 126 us
  starting transfers between devices  58 us (46%)
  waiting for transfers between devices  28.5 us (22%)
  Pallas kernels  17.5 us (14%)
  local copies, waits for them, and re-layouts  15.3 us (12%)
  other arithmetic  5.97 us (5%)
    all_to_all x1, waiting for transfers between devices, body(): part = lax.all_to_all(part, 'lon', 0, 0, axis_index_groups=groups)  10.7 us
    all_to_all x1, waiting for transfers between devices, body(): lax.all_to_all(jnp.repeat(polar_q, 2, axis=0), 'lon', 0, 0, axis_index_gr...  8.64 us
    ppermute x1, waiting for transfers between devices, body(): ret_b = lax.ppermute(ret_n, 'lat', line(nlat, -1))  8.01 us
    ppermute x1, starting transfers between devices, body(): ret_a = lax.ppermute(ret_s, 'lat', line(nlat, 1))  7.83 us
    unnamed x34, local copies, waits for them, and re-layouts  7.63 us
    ppermute x1, starting transfers between devices, body(): qn = lax.ppermute(q_b, 'lat', line(nlat, 1))  7.23 us
    pallas_call x1, Pallas kernels, body(): call(window_kernel, (sds((PAIRS, 2, 128, LANES), F32), sds((2, 128, LANES...  6.46 us
    all_to_all x1, starting transfers between devices, body(): part = lax.all_to_all(part, 'lon', 0, 0, axis_index_groups=groups)  5.83 us
  transfers between devices with their start and end apart: 20, of which 5 were waited for; matrix products, arithmetic and copies ran while one was open for 9% of the time, Pallas kernels for 10%

profile of v1, /device:TPU:7, one launch (start us, length us, event | category | flops | bytes accessed | tf_op | source)
XLA Modules:
  0.0 125.6 jit_solution(17165354675651159445)
XLA Ops:
  0.0 1.7 %fusion.3 = (bf16[1,128,512]{2,1,0:T(8,128)(2,1)}, bf16[1,128,512]{2,1,0:T(8,128)(2,1)}) fusion(bf16[2,128,512]{2,1,0:T(8,128)(2,1)} %f_ref.3), kind=kLoop, calls=%fused_computation.30 | loop fusion | bytes 524288 | tf_op jit(solution)/shard_map/slice | solution.py:252
  1.7 5.3 %collective-permute-start.2 = (bf16[1,128,512]{2,1,0:T(8,128)(2,1)}, bf16[1,128,512]{2,1,0:T(8,128)(2,1)S(1)}, u32[]{:S(2)}, u32[]{:S(2)}) collective-permute-start(bf16[1,128,512]{2,1,0:T(8,128)(2,1)} %get-tuple-element.24), channel_id=1, source_target_pairs={{0,16},{16,32},{32,48},{48,64},{64,80},{80,96},{96,112},{112,128},... | collective-permute-start | bytes 393224 | tf_op jit(solution)/shard_map/ppermute | solution.py:251
  7.0 1.9 %collective-permute-start.3 = (bf16[1,128,512]{2,1,0:T(8,128)(2,1)}, bf16[1,128,512]{2,1,0:T(8,128)(2,1)}, u32[]{:S(2)}, u32[]{:S(2)}) collective-permute-start(bf16[1,128,512]{2,1,0:T(8,128)(2,1)} %get-tuple-element.23), channel_id=1, source_target_pairs={{16,0},{32,16},{48,32},{64,48},{80,64},{96,80},{112,96},{128,112},... | collective-permute-start | bytes 393224 | tf_op jit(solution)/shard_map/ppermute | solution.py:252
  9.0 1.3 %fusion.2 = (bf16[2,1,512]{2,1,0:T(2,128)(2,1)}, bf16[2,1,512]{2,1,0:T(2,128)(2,1)}) fusion(bf16[2,128,512]{2,1,0:T(8,128)(2,1)} %f_ref.3), kind=kLoop, calls=%fused_computation.29 | loop fusion | bytes 8192 | tf_op jit(solution)/shard_map/slice | solution.py:254
  10.3 1.6 %collective-permute-start.4 = (bf16[2,1,512]{2,1,0:T(2,128)(2,1)}, bf16[2,1,512]{2,1,0:T(2,128)(2,1)S(1)}, u32[]{:S(2)}, u32[]{:S(2)}) collective-permute-start(bf16[2,1,512]{2,1,0:T(2,128)(2,1)} %get-tuple-element.22), channel_id=1, source_target_pairs={{0,1},{1,2},{2,3},{3,4},{4,5},{5,6},{6,7},{7,8},{8,9},{9,10},{10,1... | collective-permute-start | bytes 6152 | tf_op jit(solution)/shard_map/ppermute | solution.py:253
  11.9 4.1 %collective-permute-start.5 = (bf16[2,1,512]{2,1,0:T(2,128)(2,1)}, bf16[2,1,512]{2,1,0:T(2,128)(2,1)S(1)}, u32[]{:S(2)}, u32[]{:S(2)}) collective-permute-start(bf16[2,1,512]{2,1,0:T(2,128)(2,1)} %get-tuple-element.21), channel_id=1, source_target_pairs={{0,15},{1,0},{2,1},{3,2},{4,3},{5,4},{6,5},{7,6},{8,7},{9,8},{10,9... | collective-permute-start | bytes 6152 | tf_op jit(solution)/shard_map/ppermute | solution.py:254
  16.1 0.6 pad_maximum_fusion.1
  16.7 1.9 %copy-done.1 = bf16[1536,1024]{1,0:T(8,128)(2,1)S(1)} copy-done((bf16[1536,1024]{1,0:T(8,128)(2,1)S(1)}, bf16[1536,1024]{1,0:T(8,128)(2,1)}, u32[]{:S(2)}) %copy-start.1) | copy-done | bytes 3145752
  18.6 0.9 copy-done.5
  19.5 1.0 copy-done.12
  21.2 0.7 copy-done.7
  21.9 1.0 copy-done.10
  22.9 0.7 reshape.108.coef_ref
  23.7 1.2 copy-done.11
  24.9 2.6 %shard_map.83.kv_ref = bf16[8,2,128,128]{3,2,1,0:T(8,128)(2,1)S(1)} custom-call(f32[4]{0:T(128)S(1)} %reshape.108.coef_ref, bf16[2,128,512]{2,1,0:T(8,128)(2,1)S(1)} %copy-done.6, bf16[1,128,512]{2,1,0:T(8,128)(2,1)S(1)} %collective-permute-done.2.up_ref, bf16[1,128,512]{2,1,0:T(8,128)(2,1)} %collective-permute-done.3.dn_ref, ...), custom_call_target="tpu_custom_call" | custom-call | flops 600000000 | bytes 4000000 | tf_op jit(solution)/shard_map/pallas_call | solution.py:267
  27.5 0.8 copy-done.3
  29.1 0.9 collective-permute-done.15
  30.0 1.1 select_select_fusion
  31.1 1.4 %collective-permute-start.8 = (bf16[8,128,128]{2,1,0:T(8,128)(2,1)S(1)}, bf16[8,128,128]{2,1,0:T(8,128)(2,1)S(1)}, u32[]{:S(2)}, u32[]{:S(2)}) collective-permute-start(bf16[8,128,128]{2,1,0:T(8,128)(2,1)S(1)} %get-tuple-element.18), channel_id=1, source_target_pairs={{0,128},{240,112},{1,129},{241,113},{2,130},{242,114},{3,131},{243... | collective-permute-start | bytes 786440 | tf_op jit(solution)/shard_map/ppermute | solution.py:293
  32.5 1.0 select_select_fusion.1
  33.6 0.7 broadcast_in_dim.9
  34.3 5.2 %all-to-all-start = ((bf16[8,128,128]{2,1,0:T(8,128)(2,1)}), bf16[8,128,128]{2,1,0:T(8,128)(2,1)S(1)}, u32[]{:S(2)}, u32[]{:S(2)}) async-start(bf16[8,128,128]{2,1,0:T(8,128)(2,1)} %bitcast.12), calls=%async_computation | async-start | bytes 524288 | tf_op jit(solution)/shard_map/all_to_all | solution.py:280
  39.5 0.6 dynamic_slice.11
  40.1 0.6 broadcast_select_fusion.1
  40.7 1.6 %collective-permute-start.9 = (bf16[8,128,128]{2,1,0:T(8,128)(2,1)S(1)}, bf16[8,128,128]{2,1,0:T(8,128)(2,1)S(1)}, u32[]{:S(2)}, u32[]{:S(2)}) collective-permute-start(bf16[8,128,128]{2,1,0:T(8,128)(2,1)S(1)} %broadcast_select_fusion.1), channel_id=1, source_target_pairs={{0,64},{128,192},{240,176},{112,48},{1,65},{129,193},{241,177},{11... | collective-permute-start | bytes 786440 | tf_op jit(solution)/shard_map/ppermute | solution.py:293
  42.4 0.9 pad_maximum_fusion
  43.3 8.6 %all-to-all-done.q_ref = bf16[8,128,128]{2,1,0:T(8,128)(2,1)S(1)} async-done(((bf16[8,128,128]{2,1,0:T(8,128)(2,1)}), bf16[8,128,128]{2,1,0:T(8,128)(2,1)S(1)}, u32[]{:S(2)}, u32[]{:S(2)}) %all-to-all-start) | async-done | bytes 262176 | tf_op jit(solution)/shard_map/all_to_all | solution.py:280
  51.9 3.6 %all-to-all-start.1 = ((bf16[16,128,128]{2,1,0:T(8,128)(2,1)}), bf16[16,128,128]{2,1,0:T(8,128)(2,1)S(1)}, u32[]{:S(2)}, u32[]{:S(2)}) async-start(bf16[16,128,128]{2,1,0:T(8,128)(2,1)} %pad_maximum_fusion), calls=%async_computation.1 | async-start | bytes 1048576 | tf_op jit(solution)/shard_map/all_to_all | solution.py:279
  55.5 0.7 slice_bitcast_fusion.2
  56.2 7.2 %collective-permute-start = (bf16[4,128,128]{2,1,0:T(8,128)(2,1)}, bf16[4,128,128]{2,1,0:T(8,128)(2,1)S(1)}, u32[]{:S(2)}, u32[]{:S(2)}) collective-permute-start(bf16[4,128,128]{2,1,0:T(8,128)(2,1)} %get-tuple-element.26), channel_id=1, source_target_pairs={{0,16},{16,32},{32,48},{48,64},{64,80},{80,96},{96,112},{112,128},... | collective-permute-start | bytes 393224 | tf_op jit(solution)/shard_map/ppermute | solution.py:284
  63.4 1.9 %collective-permute-start.1 = (bf16[4,128,128]{2,1,0:T(8,128)(2,1)S(1)}, bf16[4,128,128]{2,1,0:T(8,128)(2,1)S(1)}, u32[]{:S(2)}, u32[]{:S(2)}) collective-permute-start(bf16[4,128,128]{2,1,0:T(8,128)(2,1)S(1)} %get-tuple-element.25), channel_id=1, source_target_pairs={{16,0},{32,16},{48,32},{64,48},{80,64},{96,80},{112,96},{128,112},... | collective-permute-start | bytes 393224 | tf_op jit(solution)/shard_map/ppermute | solution.py:285
  65.3 0.6 dynamic_slice.10
  65.9 0.7 broadcast_select_fusion.2
  66.6 2.0 %collective-permute-start.10 = (bf16[8,128,128]{2,1,0:T(8,128)(2,1)S(1)}, bf16[8,128,128]{2,1,0:T(8,128)(2,1)}, u32[]{:S(2)}, u32[]{:S(2)}) collective-permute-start(bf16[8,128,128]{2,1,0:T(8,128)(2,1)S(1)} %broadcast_select_fusion.2), channel_id=1, source_target_pairs={{0,32},{64,96},{128,160},{192,224},{240,208},{176,144},{112,80},{4... | collective-permute-start | bytes 786440 | tf_op jit(solution)/shard_map/ppermute | solution.py:293
  68.6 0.6 dynamic_slice.9
  69.4 0.6 gather_fusion
  70.1 1.6 %collective-permute-start.6 = (bf16[8,2,128,128]{3,2,1,0:T(8,128)(2,1)S(1)}, bf16[8,2,128,128]{3,2,1,0:T(8,128)(2,1)S(1)}, u32[]{:S(2)}, u32[]{:S(2)}) collective-permute-start(bf16[8,2,128,128]{3,2,1,0:T(8,128)(2,1)S(1)} %copy-done.4), channel_id=1, source_target_pairs={{0,1},{1,2},{2,3},{3,4},{4,5},{5,6},{6,7},{7,8},{8,9},{9,10},{10,1... | collective-permute-start | bytes 1572872 | tf_op jit(solution)/shard_map/ppermute | solution.py:282
  71.7 2.1 %collective-permute-start.7 = (bf16[8,2,128,128]{3,2,1,0:T(8,128)(2,1)S(1)}, bf16[8,2,128,128]{3,2,1,0:T(8,128)(2,1)S(1)}, u32[]{:S(2)}, u32[]{:S(2)}) collective-permute-start(bf16[8,2,128,128]{3,2,1,0:T(8,128)(2,1)S(1)} %copy-done.4), channel_id=1, source_target_pairs={{0,15},{1,0},{2,1},{3,2},{4,3},{5,4},{6,5},{7,6},{8,7},{9,8},{10,9... | collective-permute-start | bytes 1572872 | tf_op jit(solution)/shard_map/ppermute | solution.py:283
  73.7 0.7 broadcast_select_fusion.3
  74.5 5.6 %shard_map.85 = bf16[8,128,128]{2,1,0:T(8,128)(2,1)} custom-call(s32[1]{0:T(128)} %bitcast.10.odd_ref, f32[1]{0:T(128)} %bitcast.11.log_ref, bf16[8,128,128]{2,1,0:T(8,128)(2,1)S(1)} %all-to-all-done.q_ref, bf16[16,128,128]{2,1,0:T(8,128)(2,1)S(1)} %all-to-all-done.1.kv_ref), custom_call_target="tpu_custom_call" | custom-call | flops 6000000000 | bytes 2000000 | tf_op jit(solution)/shard_map/pallas_call | solution.py:318
  80.2 5.8 %all-to-all-start.2 = ((bf16[8,128,128]{2,1,0:T(8,128)(2,1)}), bf16[8,128,128]{2,1,0:T(8,128)(2,1)S(1)}, u32[]{:S(2)}, u32[]{:S(2)}) async-start(bf16[8,128,128]{2,1,0:T(8,128)(2,1)} %shard_map.85), calls=%async_computation.2 | async-start | bytes 524288 | tf_op jit(solution)/shard_map/all_to_all | solution.py:322
  86.1 10.7 %all-to-all-done.2.p1_ref = bf16[8,128,128]{2,1,0:T(8,128)(2,1)S(1)} async-done(((bf16[8,128,128]{2,1,0:T(8,128)(2,1)}), bf16[8,128,128]{2,1,0:T(8,128)(2,1)S(1)}, u32[]{:S(2)}, u32[]{:S(2)}) %all-to-all-start.2) | async-done | bytes 262176 | tf_op jit(solution)/shard_map/all_to_all | solution.py:322
  96.7 2.1 %collective-permute-start.16 = (bf16[8,128,128]{2,1,0:T(8,128)(2,1)S(1)}, bf16[8,128,128]{2,1,0:T(8,128)(2,1)S(1)}, u32[]{:S(2)}, u32[]{:S(2)}) collective-permute-start(bf16[8,128,128]{2,1,0:T(8,128)(2,1)S(1)} %all-to-all-done.2.p1_ref), channel_id=1, source_target_pairs={{0,16},{16,0},{32,48},{48,32},{64,80},{80,64},{96,112},{112,96},{1... | collective-permute-start | bytes 786440 | tf_op jit(solution)/shard_map/ppermute | solution.py:323
  98.9 6.5 %shard_map.84 = (f32[4,2,128,128]{3,2,1,0:T(8,128)S(1)}, bf16[2,128,128]{2,1,0:T(8,128)(2,1)S(1)}, bf16[5,128,128]{2,1,0:T(8,128)(2,1)S(1)}, bf16[5,128,128]{2,1,0:T(8,128)(2,1)S(1)}) custom-call(s32[4]{0:T(128)S(1)} %or_select_fusion.width_ref, f32[2]{0:T(128)S(1)} %fusion.1.log_ref, bf16[4,2,128,128]{3,2,1,0:T(8,128)(2,1)S(1)} %copy-done.9, ...), custom_call_target="tpu_custom_call" | custom-call | flops 8000000000 | bytes 4000000 | tf_op jit(solution)/shard_map/pallas_call | solution.py:305
  105.3 7.8 %collective-permute-start.12 = (bf16[5,128,128]{2,1,0:T(8,128)(2,1)S(1)}, bf16[5,128,128]{2,1,0:T(8,128)(2,1)S(1)}, u32[]{:S(2)}, u32[]{:S(2)}) collective-permute-start(bf16[5,128,128]{2,1,0:T(8,128)(2,1)S(1)} %get-tuple-element.15), channel_id=1, source_target_pairs={{0,16},{16,32},{32,48},{48,64},{64,80},{80,96},{96,112},{112,128},... | collective-permute-start | bytes 491528 | tf_op jit(solution)/shard_map/ppermute | solution.py:314
  113.2 1.9 %collective-permute-start.13 = (bf16[5,128,128]{2,1,0:T(8,128)(2,1)S(1)}, bf16[5,128,128]{2,1,0:T(8,128)(2,1)S(1)}, u32[]{:S(2)}, u32[]{:S(2)}) collective-permute-start(bf16[5,128,128]{2,1,0:T(8,128)(2,1)S(1)} %get-tuple-element.16), channel_id=1, source_target_pairs={{16,0},{32,16},{48,32},{64,48},{80,64},{96,80},{112,96},{128,112},... | collective-permute-start | bytes 491528 | tf_op jit(solution)/shard_map/ppermute | solution.py:313
  115.4 8.0 %collective-permute-done.13.rb_ref = bf16[5,128,128]{2,1,0:T(8,128)(2,1)S(1)} collective-permute-done((bf16[5,128,128]{2,1,0:T(8,128)(2,1)S(1)}, bf16[5,128,128]{2,1,0:T(8,128)(2,1)S(1)}, u32[]{:S(2)}, u32[]{:S(2)}) %collective-permute-start.13) | collective-permute-done | bytes 163872 | tf_op jit(solution)/shard_map/ppermute | solution.py:313
  123.4 2.2 %shard_map.86 = bf16[2,128,512]{2,1,0:T(8,128)(2,1)} custom-call(s32[2]{0:T(128)S(1)} %add_convert_fusion.role_ref, f32[4,2,128,128]{3,2,1,0:T(8,128)S(1)} %get-tuple-element.13.o_ref, bf16[2,128,128]{2,1,0:T(8,128)(2,1)S(1)} %get-tuple-element.14.st_ref, bf16[5,128,128]{2,1,0:T(8,128)(2,1)S(1)} %collective-permute-done.12.ra_ref, ...), custom_call_target="tpu_custom_call" | custom-call | flops 1000000000 | bytes 3000000 | tf_op jit(solution)/shard_map/pallas_call | solution.py:326
  (56 shorter events, 2.0 us)
Async XLA Ops:
  0.0 69.4 %copy-start = (s32[32]{0:T(128)S(1)}, s32[32]{0:T(128)}, u32[]{:S(2)}) copy-start(s32[32]{0:T(128)} %param.9) | copy-start | bytes 388
  0.0 23.6 %copy-start.6 = (bf16[2,128,512]{2,1,0:T(8,128)(2,1)S(1)}, bf16[2,128,512]{2,1,0:T(8,128)(2,1)}, u32[]{:S(2)}) copy-start(bf16[2,128,512]{2,1,0:T(8,128)(2,1)} %f_ref.3) | copy-start | bytes 786436
  1.7 21.9 %collective-permute-start.2 = (bf16[1,128,512]{2,1,0:T(8,128)(2,1)}, bf16[1,128,512]{2,1,0:T(8,128)(2,1)S(1)}, u32[]{:S(2)}, u32[]{:S(2)}) collective-permute-start(bf16[1,128,512]{2,1,0:T(8,128)(2,1)} %get-tuple-element.24), channel_id=1, source_target_pairs={{0,16},{16,32},{32,48},{48,64},{64,80},{80,96},{96,112},{112,128},... | collective-permute-start | bytes 393224 | tf_op jit(solution)/shard_map/ppermute | solution.py:251
  7.0 16.6 %collective-permute-start.3 = (bf16[1,128,512]{2,1,0:T(8,128)(2,1)}, bf16[1,128,512]{2,1,0:T(8,128)(2,1)}, u32[]{:S(2)}, u32[]{:S(2)}) collective-permute-start(bf16[1,128,512]{2,1,0:T(8,128)(2,1)} %get-tuple-element.23), channel_id=1, source_target_pairs={{16,0},{32,16},{48,32},{64,48},{80,64},{96,80},{112,96},{128,112},... | collective-permute-start | bytes 393224 | tf_op jit(solution)/shard_map/ppermute | solution.py:252
  10.3 13.3 %collective-permute-start.4 = (bf16[2,1,512]{2,1,0:T(2,128)(2,1)}, bf16[2,1,512]{2,1,0:T(2,128)(2,1)S(1)}, u32[]{:S(2)}, u32[]{:S(2)}) collective-permute-start(bf16[2,1,512]{2,1,0:T(2,128)(2,1)} %get-tuple-element.22), channel_id=1, source_target_pairs={{0,1},{1,2},{2,3},{3,4},{4,5},{5,6},{6,7},{7,8},{8,9},{9,10},{10,1... | collective-permute-start | bytes 6152 | tf_op jit(solution)/shard_map/ppermute | solution.py:253
  11.9 11.7 %collective-permute-start.5 = (bf16[2,1,512]{2,1,0:T(2,128)(2,1)}, bf16[2,1,512]{2,1,0:T(2,128)(2,1)S(1)}, u32[]{:S(2)}, u32[]{:S(2)}) collective-permute-start(bf16[2,1,512]{2,1,0:T(2,128)(2,1)} %get-tuple-element.21), channel_id=1, source_target_pairs={{0,15},{1,0},{2,1},{3,2},{4,3},{5,4},{6,5},{7,6},{8,7},{9,8},{10,9... | collective-permute-start | bytes 6152 | tf_op jit(solution)/shard_map/ppermute | solution.py:254
  16.7 1.9 %copy-start.1 = (bf16[1536,1024]{1,0:T(8,128)(2,1)S(1)}, bf16[1536,1024]{1,0:T(8,128)(2,1)}, u32[]{:S(2)}) copy-start(bf16[1536,1024]{1,0:T(8,128)(2,1)} %w2_ref.1) | copy-start | bytes 9437188
  18.6 0.9 copy-start.5
  19.5 1.0 copy-start.12
  20.6 3.1 %copy-start.2 = (bf16[1536,1024]{1,0:T(8,128)(2,1)S(1)}, bf16[1536,1024]{1,0:T(8,128)(2,1)}, u32[]{:S(2)}) copy-start(bf16[1536,1024]{1,0:T(8,128)(2,1)} %w2_ref.1) | copy-start | bytes 9437188
  21.2 0.7 copy-start.7
  21.9 1.0 copy-start.10
  23.6 1.2 copy-start.11
  24.9 3.8 %copy-start.8 = (bf16[4,2,128,128]{3,2,1,0:T(8,128)(2,1)S(1)}, bf16[4,2,128,128]{3,2,1,0:T(8,128)(2,1)}, u32[]{:S(2)}) copy-start(bf16[4,2,128,128]{3,2,1,0:T(8,128)(2,1)} %copy-done.7) | copy-start | bytes 786436
  27.5 0.8 copy-start.3
  28.3 11.2 %copy-start.16 = (pred[16]{0:T(512)(128)(4,1)S(1)}, pred[16]{0:T(512)(128)(4,1)}, u32[]{:S(2)}) copy-start(pred[16]{0:T(512)(128)(4,1)} %constant.72.clone) | copy-start | bytes 52
  28.3 27.2 %copy-start.9 = (bf16[4,2,128,128]{3,2,1,0:T(8,128)(2,1)S(1)}, bf16[4,2,128,128]{3,2,1,0:T(8,128)(2,1)}, u32[]{:S(2)}) copy-start(bf16[4,2,128,128]{3,2,1,0:T(8,128)(2,1)} %copy-done.7) | copy-start | bytes 786436
  28.3 1.6 %collective-permute-start.15 = (bf16[8,128,128]{2,1,0:T(8,128)(2,1)S(1)}, bf16[8,128,128]{2,1,0:T(8,128)(2,1)S(1)}, u32[]{:S(2)}, u32[]{:S(2)}) collective-permute-start(bf16[8,128,128]{2,1,0:T(8,128)(2,1)S(1)} %broadcast_select_fusion.4), channel_id=1, source_target_pairs={{0,16},{16,0},{32,48},{48,32},{64,80},{80,64},{96,112},{112,96},{1... | collective-permute-start | bytes 786440 | tf_op jit(solution)/shard_map/ppermute | solution.py:276
  28.6 36.7 %copy-start.15 = (pred[16]{0:T(512)(128)(4,1)S(1)}, pred[16]{0:T(512)(128)(4,1)}, u32[]{:S(2)}) copy-start(pred[16]{0:T(512)(128)(4,1)} %constant.73.clone) | copy-start | bytes 52
  28.7 3.8 %collective-permute-start.14 = (bf16[4,128,128]{2,1,0:T(8,128)(2,1)S(1)}, bf16[4,128,128]{2,1,0:T(8,128)(2,1)S(1)}, u32[]{:S(2)}, u32[]{:S(2)}) collective-permute-start(bf16[4,128,128]{2,1,0:T(8,128)(2,1)S(1)} %broadcast_select_fusion.7), channel_id=1, source_target_pairs={{0,16},{16,0},{32,48},{48,32},{64,80},{80,64},{96,112},{112,96},{1... | collective-permute-start | bytes 393224 | tf_op jit(solution)/shard_map/ppermute | solution.py:275
  29.1 39.6 %copy-start.14 = (pred[16]{0:T(512)(128)(4,1)S(1)}, pred[16]{0:T(512)(128)(4,1)}, u32[]{:S(2)}) copy-start(pred[16]{0:T(512)(128)(4,1)} %constant.74.clone) | copy-start | bytes 52
  31.1 39.0 %copy-start.4 = (bf16[8,2,128,128]{3,2,1,0:T(8,128)(2,1)S(1)}, bf16[8,2,128,128]{3,2,1,0:T(8,128)(2,1)}, u32[]{:S(2)}) copy-start(bf16[8,2,128,128]{3,2,1,0:T(8,128)(2,1)} %copy-done.3) | copy-start | bytes 1572868
  31.1 9.0 %collective-permute-start.8 = (bf16[8,128,128]{2,1,0:T(8,128)(2,1)S(1)}, bf16[8,128,128]{2,1,0:T(8,128)(2,1)S(1)}, u32[]{:S(2)}, u32[]{:S(2)}) collective-permute-start(bf16[8,128,128]{2,1,0:T(8,128)(2,1)S(1)} %get-tuple-element.18), channel_id=1, source_target_pairs={{0,128},{240,112},{1,129},{241,113},{2,130},{242,114},{3,131},{243... | collective-permute-start | bytes 786440 | tf_op jit(solution)/shard_map/ppermute | solution.py:293
  34.3 17.6 %all-to-all-start = ((bf16[8,128,128]{2,1,0:T(8,128)(2,1)}), bf16[8,128,128]{2,1,0:T(8,128)(2,1)S(1)}, u32[]{:S(2)}, u32[]{:S(2)}) async-start(bf16[8,128,128]{2,1,0:T(8,128)(2,1)} %bitcast.12), calls=%async_computation | async-start | bytes 524288 | tf_op jit(solution)/shard_map/all_to_all | solution.py:280
  40.7 25.2 %collective-permute-start.9 = (bf16[8,128,128]{2,1,0:T(8,128)(2,1)S(1)}, bf16[8,128,128]{2,1,0:T(8,128)(2,1)S(1)}, u32[]{:S(2)}, u32[]{:S(2)}) collective-permute-start(bf16[8,128,128]{2,1,0:T(8,128)(2,1)S(1)} %broadcast_select_fusion.1), channel_id=1, source_target_pairs={{0,64},{128,192},{240,176},{112,48},{1,65},{129,193},{241,177},{11... | collective-permute-start | bytes 786440 | tf_op jit(solution)/shard_map/ppermute | solution.py:293
  51.9 22.6 %all-to-all-start.1 = ((bf16[16,128,128]{2,1,0:T(8,128)(2,1)}), bf16[16,128,128]{2,1,0:T(8,128)(2,1)S(1)}, u32[]{:S(2)}, u32[]{:S(2)}) async-start(bf16[16,128,128]{2,1,0:T(8,128)(2,1)} %pad_maximum_fusion), calls=%async_computation.1 | async-start | bytes 1048576 | tf_op jit(solution)/shard_map/all_to_all | solution.py:279
  56.2 42.7 %collective-permute-start = (bf16[4,128,128]{2,1,0:T(8,128)(2,1)}, bf16[4,128,128]{2,1,0:T(8,128)(2,1)S(1)}, u32[]{:S(2)}, u32[]{:S(2)}) collective-permute-start(bf16[4,128,128]{2,1,0:T(8,128)(2,1)} %get-tuple-element.26), channel_id=1, source_target_pairs={{0,16},{16,32},{32,48},{48,64},{64,80},{80,96},{96,112},{112,128},... | collective-permute-start | bytes 393224 | tf_op jit(solution)/shard_map/ppermute | solution.py:284
  63.4 35.4 %collective-permute-start.1 = (bf16[4,128,128]{2,1,0:T(8,128)(2,1)S(1)}, bf16[4,128,128]{2,1,0:T(8,128)(2,1)S(1)}, u32[]{:S(2)}, u32[]{:S(2)}) collective-permute-start(bf16[4,128,128]{2,1,0:T(8,128)(2,1)S(1)} %get-tuple-element.25), channel_id=1, source_target_pairs={{16,0},{32,16},{48,32},{64,48},{80,64},{96,80},{112,96},{128,112},... | collective-permute-start | bytes 393224 | tf_op jit(solution)/shard_map/ppermute | solution.py:285
  66.6 7.1 %collective-permute-start.10 = (bf16[8,128,128]{2,1,0:T(8,128)(2,1)S(1)}, bf16[8,128,128]{2,1,0:T(8,128)(2,1)}, u32[]{:S(2)}, u32[]{:S(2)}) collective-permute-start(bf16[8,128,128]{2,1,0:T(8,128)(2,1)S(1)} %broadcast_select_fusion.2), channel_id=1, source_target_pairs={{0,32},{64,96},{128,160},{192,224},{240,208},{176,144},{112,80},{4... | collective-permute-start | bytes 786440 | tf_op jit(solution)/shard_map/ppermute | solution.py:293
  70.1 28.8 %collective-permute-start.6 = (bf16[8,2,128,128]{3,2,1,0:T(8,128)(2,1)S(1)}, bf16[8,2,128,128]{3,2,1,0:T(8,128)(2,1)S(1)}, u32[]{:S(2)}, u32[]{:S(2)}) collective-permute-start(bf16[8,2,128,128]{3,2,1,0:T(8,128)(2,1)S(1)} %copy-done.4), channel_id=1, source_target_pairs={{0,1},{1,2},{2,3},{3,4},{4,5},{5,6},{6,7},{7,8},{8,9},{9,10},{10,1... | collective-permute-start | bytes 1572872 | tf_op jit(solution)/shard_map/ppermute | solution.py:282
  71.7 27.2 %collective-permute-start.7 = (bf16[8,2,128,128]{3,2,1,0:T(8,128)(2,1)S(1)}, bf16[8,2,128,128]{3,2,1,0:T(8,128)(2,1)S(1)}, u32[]{:S(2)}, u32[]{:S(2)}) collective-permute-start(bf16[8,2,128,128]{3,2,1,0:T(8,128)(2,1)S(1)} %copy-done.4), channel_id=1, source_target_pairs={{0,15},{1,0},{2,1},{3,2},{4,3},{5,4},{6,5},{7,6},{8,7},{9,8},{10,9... | collective-permute-start | bytes 1572872 | tf_op jit(solution)/shard_map/ppermute | solution.py:283
  74.4 11.6 %collective-permute-start.11 = (bf16[8,128,128]{2,1,0:T(8,128)(2,1)S(1)}, bf16[8,128,128]{2,1,0:T(8,128)(2,1)S(1)}, u32[]{:S(2)}, u32[]{:S(2)}) collective-permute-start(bf16[8,128,128]{2,1,0:T(8,128)(2,1)S(1)} %broadcast_select_fusion.3), channel_id=1, source_target_pairs={{0,16},{16,0},{32,48},{48,32},{64,80},{80,64},{96,112},{112,96},{1... | collective-permute-start | bytes 786440 | tf_op jit(solution)/shard_map/ppermute | solution.py:297
  80.2 16.6 %all-to-all-start.2 = ((bf16[8,128,128]{2,1,0:T(8,128)(2,1)}), bf16[8,128,128]{2,1,0:T(8,128)(2,1)S(1)}, u32[]{:S(2)}, u32[]{:S(2)}) async-start(bf16[8,128,128]{2,1,0:T(8,128)(2,1)} %shard_map.85), calls=%async_computation.2 | async-start | bytes 524288 | tf_op jit(solution)/shard_map/all_to_all | solution.py:322
  96.7 26.7 %collective-permute-start.16 = (bf16[8,128,128]{2,1,0:T(8,128)(2,1)S(1)}, bf16[8,128,128]{2,1,0:T(8,128)(2,1)S(1)}, u32[]{:S(2)}, u32[]{:S(2)}) collective-permute-start(bf16[8,128,128]{2,1,0:T(8,128)(2,1)S(1)} %all-to-all-done.2.p1_ref), channel_id=1, source_target_pairs={{0,16},{16,0},{32,48},{48,32},{64,80},{80,64},{96,112},{112,96},{1... | collective-permute-start | bytes 786440 | tf_op jit(solution)/shard_map/ppermute | solution.py:323
  98.8 24.6 %copy-start.13 = (bf16[512,512]{1,0:T(8,128)(2,1)S(1)}, bf16[512,512]{1,0:T(8,128)(2,1)}, u32[]{:S(2)}) copy-start(bf16[512,512]{1,0:T(8,128)(2,1)} %wo_ref.1) | copy-start | bytes 1572868
  105.3 10.1 %collective-permute-start.12 = (bf16[5,128,128]{2,1,0:T(8,128)(2,1)S(1)}, bf16[5,128,128]{2,1,0:T(8,128)(2,1)S(1)}, u32[]{:S(2)}, u32[]{:S(2)}) collective-permute-start(bf16[5,128,128]{2,1,0:T(8,128)(2,1)S(1)} %get-tuple-element.15), channel_id=1, source_target_pairs={{0,16},{16,32},{32,48},{48,64},{64,80},{80,96},{96,112},{112,128},... | collective-permute-start | bytes 491528 | tf_op jit(solution)/shard_map/ppermute | solution.py:314
  113.2 10.3 %collective-permute-start.13 = (bf16[5,128,128]{2,1,0:T(8,128)(2,1)S(1)}, bf16[5,128,128]{2,1,0:T(8,128)(2,1)S(1)}, u32[]{:S(2)}, u32[]{:S(2)}) collective-permute-start(bf16[5,128,128]{2,1,0:T(8,128)(2,1)S(1)} %get-tuple-element.16), channel_id=1, source_target_pairs={{16,0},{32,16},{48,32},{64,48},{80,64},{96,80},{112,96},{128,112},... | collective-permute-start | bytes 491528 | tf_op jit(solution)/shard_map/ppermute | solution.py:313

commit v2 on v1

v2 whole, which is shorter than its diff:
```python
import jax
import jax.numpy as jnp
import numpy as np
from jax import lax
from jax.experimental import pallas as pl
from jax.experimental.pallas import tpu as pltpu
from jax.sharding import PartitionSpec as P

HEADS = 8
HDIM = 64
NLAT = 32
PAIRS = 4
LANES = 128
MASKED = -1e30
F32 = jnp.float32
BF16 = jnp.bfloat16
VMEM = pl.BlockSpec(memory_space=pltpu.VMEM)
ANY = pl.BlockSpec(memory_space=pl.ANY)
SMEM = pl.BlockSpec(memory_space=pltpu.SMEM)
PARAMS = pltpu.CompilerParams(vmem_limit_bytes=20 * 1024 * 1024)


def cost(flops, nbytes):
    return pl.CostEstimate(flops=flops, bytes_accessed=nbytes, transcendentals=0)


def row_tables():
    weight = lambda row: np.sin(np.pi * (row + 0.5) / NLAT) if 0 <= row < NLAT else 0.0
    table = np.zeros((NLAT // 2, 8), np.float32)
    for band in range(NLAT // 2):
        step = 1 - 2 * (band % 2)
        w = [weight(2 * band + band % 2 + step * k) for k in (-1, 0, 1, 2)]
        table[band, :4] = w[0] / (w[0] + w[2]), w[2] / (w[0] + w[2]), w[1] / (w[1] + w[3]), w[3] / (w[1] + w[3])
        table[band, 4:6] = np.log(w[1]), np.log(w[2])
        table[band, 6] = np.log(weight(0 if band in (0, NLAT // 2 - 1) else 1))
    return table.reshape(-1)


def is_polar(band):
    return (band == 0) | (band == NLAT // 2 - 1)


def lane_ids(shape):
    return lax.broadcasted_iota(jnp.int32, shape, len(shape) - 1)


def dot_nn(a, b):
    return lax.dot_general(a, b, (((1,), (0,)), ((), ())), preferred_element_type=F32)


def dot_nt(a, b):
    return lax.dot_general(a, b, (((1,), (1,)), ((), ())), preferred_element_type=F32)


def dot_tn(a, b):
    return lax.dot_general(a, b, (((0,), (0,)), ((), ())), preferred_element_type=F32)


def half_turn(x):
    return pltpu.roll(x, HDIM, 1)


def three_parts(x):
    a = x.astype(BF16)
    rest = x - a.astype(F32)
    b = rest.astype(BF16)
    c = (rest - b.astype(F32)).astype(BF16)
    return a.astype(F32), b.astype(F32), c.astype(F32)


def edge_kernel(band_ref, f_ref, last_ref, lead_ref, sems):
    odd = band_ref[0] % 2
    copies = []
    for slot in range(2):
        row = f_ref.at[odd if slot == 0 else 1 - odd]
        copies.append(pltpu.make_async_copy(row.at[pl.ds(112, 16)], last_ref.at[slot], sems.at[2 * slot]))
        copies.append(pltpu.make_async_copy(row.at[pl.ds(0, 16)], lead_ref.at[slot], sems.at[2 * slot + 1]))
    for c in copies:
        c.start()
    for c in copies:
        c.wait()


def early_kernel(band_ref, f_ref, wq_ref, w_ref, qx_ref, qy_ref, pq_ref, base_ref):
    odd = band_ref[0] % 2
    low = lane_ids((64, LANES)) < HDIM
    f = jnp.concatenate([f_ref[odd], f_ref[1 - odd]], axis=0)
    q = dot_nn(f, wq_ref[...]).astype(BF16).astype(F32) * HDIM ** -0.5
    for p in range(PAIRS):
        block = q[:, p * LANES : (p + 1) * LANES]
        qx_ref[p] = block[:128].astype(BF16)
        qy_ref[p] = block[128:].astype(BF16)
        top, bottom = block[:64], block[64:128]
        pq_ref[2 * p] = jnp.where(low, top, half_turn(bottom)).astype(BF16)
        pq_ref[2 * p + 1] = jnp.where(low, half_turn(top), bottom).astype(BF16)
    base_ref[...] = dot_nn(f, w_ref[:512])


def keyval_kernel(
    band_ref, table_ref, f_ref, outer_ref, inner_ref, west_ref, east_ref, pq_ref, base_ref, w_ref,
    kv_ref, kvx_ref, mine_ref, swap_ref,
):
    band = band_ref[0]
    odd = band % 2
    coef = [table_ref[8 * band + i] for i in range(4)]
    own = [f_ref[odd], f_ref[1 - odd]]
    rows = [outer_ref[1 - odd].astype(F32), own[0].astype(F32), own[1].astype(F32), inner_ref[odd].astype(F32)]
    cell = lax.broadcasted_iota(jnp.int32, (128, 512), 0)
    lat, lon = [], []
    for r in range(2):
        lat.append((coef[2 * r] * rows[r] + coef[2 * r + 1] * rows[r + 2]).astype(BF16))
        mid = rows[r + 1]
        w = jnp.where(cell == 0, west_ref[r, 15:16].astype(F32), pltpu.roll(mid, 1, 0))
        e = jnp.where(cell == 127, east_ref[r, 0:1].astype(F32), pltpu.roll(mid, 127, 0))
        lon.append((0.5 * (w + e)).astype(BF16))
    basis = [jnp.concatenate(x, axis=0) for x in (lat, lon)]
    low = lane_ids((256, LANES)) < HDIM
    for p in range(PAIRS):
        parts = []
        for side in range(2):
            c = slice(512 * side + p * LANES, 512 * side + (p + 1) * LANES)
            parts.append(
                base_ref[:, c] + dot_nn(basis[0], w_ref[512:1024, c]) + dot_nn(basis[1], w_ref[1024:, c])
            )
        k, v = parts
        v = half_turn(v)
        for h, packed in ((2 * p, jnp.where(low, k, v)), (2 * p + 1, jnp.where(low, v, k))):
            packed = packed.astype(BF16)
            kv_ref[0, h] = packed[:128]
            kv_ref[1, h] = packed[128:]
            kvx_ref[h] = packed[:128]
            mine_ref[h, :128] = packed[:128]
            swap_ref[h, :128] = packed[128:]
    mine_ref[:, 128:] = pq_ref[...]
    swap_ref[:, 128:] = pq_ref[...]


def pick_kernel(band_ref, own_ref, got_ref, out_ref):
    picked = jnp.where(is_polar(band_ref[0]), own_ref[...], got_ref[...])
    out_ref[:HEADS] = picked
    out_ref[HEADS:] = picked


def window_kernel(
    band_ref, table_ref, width_ref, qo_ref, qx_ref, qy_ref, qi_ref, kv_ref, kvw_ref, kve_ref, p1_ref, p2_ref,
    o_ref, st_ref, ro_ref, ri_ref, bias_x, bias_y,
):
    ahead = lax.broadcasted_iota(jnp.int32, (128, 384), 1) - 128
    here = lax.broadcasted_iota(jnp.int32, (128, 384), 0)
    gap = jnp.abs(ahead - here)
    band = band_ref[0]
    first = 2 * band + band % 2
    step = 1 - 2 * (band % 2)
    for t in range(4):
        row = first + step * (t - 1)
        inner_row = (row > 0) & (row < NLAT - 1)
        inside = gap <= jnp.where(inner_row, width_ref[jnp.clip(row, 0, NLAT - 1)], -1)
        if t < 3:
            bias_x[t * 128 : (t + 1) * 128] = jnp.where(inside, table_ref[8 * band + 4], MASKED)
        if t > 0:
            bias_y[(t - 1) * 128 : t * 128] = jnp.where(inside, table_ref[8 * band + 5], MASKED)
    lane = lane_ids((128, LANES))
    low = lane < HDIM
    ones = jnp.ones((384, LANES), BF16)
    stats = [jnp.zeros((128, LANES), F32) for _ in range(4)]
    for p in range(PAIRS):
        halves = []
        for odd in range(2):
            h = 2 * p + odd
            keep = (lane >= HDIM) if odd else low
            qs = [qo_ref[p], qx_ref[p], qy_ref[p], qi_ref[p]]
            qs = [jnp.where(keep, x, jnp.zeros_like(x)) for x in qs]
            kva = jnp.concatenate([kvw_ref[0, h], kv_ref[0, h], kve_ref[0, h]], axis=0)
            kvb = jnp.concatenate([kvw_ref[1, h], kv_ref[1, h], kve_ref[1, h]], axis=0)
            kvp = jnp.concatenate([p1_ref[h], p2_ref[h]], axis=0)
            sa = dot_nt(jnp.concatenate(qs[:3], axis=0), kva) + bias_x[...]
            sb = dot_nt(jnp.concatenate(qs[1:], axis=0), kvb) + bias_y[...]
            sp = dot_nt(jnp.concatenate(qs[1:3], axis=0), kvp)
            ma = jnp.max(sa, axis=1, keepdims=True)
            mb = jnp.max(sb, axis=1, keepdims=True)
            mp = jnp.max(sp, axis=1, keepdims=True)
            mid = jnp.maximum(jnp.maximum(ma[128:], mb[:256]), mp)
            mo = ma[:128]
            mi = mb[256:]
            pa = jnp.exp(sa - jnp.concatenate([mo, mid], axis=0)).astype(BF16)
            pb = jnp.exp(sb - jnp.concatenate([mid, mi], axis=0)).astype(BF16)
            pp = jnp.exp(sp - mid).astype(BF16)
            oa = dot_nn(pa, jnp.concatenate([kva, ones], axis=1))
            ob = dot_nn(pb, jnp.concatenate([kvb, ones], axis=1))
            op = dot_nn(pp, jnp.concatenate([kvp, ones[:256]], axis=1))
            om = oa[128:] + ob[:256] + op
            full = [oa[:128], om[:128], om[128:], ob[256:]]
            tops = [mo, mid[:128], mid[128:], mi]
            halves.append([x[:, :LANES] / x[:, LANES:] for x in full])
            for t in range(4):
                parts = three_parts(tops[t] + jnp.log(full[t][:, LANES:]))
                for i in range(3):
                    stats[t] = jnp.where(lane == 3 * h + i, parts[i], stats[t])
        both = [jnp.where(low, halves[1][t], halves[0][t]) for t in range(4)]
        ro_ref[p] = both[0].astype(BF16)
        o_ref[p, 0] = both[1]
        o_ref[p, 1] = both[2]
        ri_ref[p] = both[3].astype(BF16)
    ro_ref[PAIRS] = stats[0].astype(BF16)
    st_ref[0] = stats[1].astype(BF16)
    st_ref[1] = stats[2].astype(BF16)
    ri_ref[PAIRS] = stats[3].astype(BF16)


def polar_kernel(band_ref, sector_ref, table_ref, in_ref, out_ref, wide, q_all, o_all, l_all):
    odd = sector_ref[0] % 2
    log = table_ref[8 * band_ref[0] + 6]
    lane = lane_ids((128, LANES))
    keep = (lane // HDIM) == odd
    low = lane_ids((64, LANES)) < HDIM
    first_sector = 8 * (sector_ref[0] // 8)
    for b in range(16):
        wide[128 * b : 128 * (b + 1), :LANES] = in_ref[b, :128]
    wide[:, LANES:] = jnp.ones((2048, LANES), BF16)
    for b in range(8):
        packed = in_ref[first_sector + b, 128:].astype(F32)
        turned = half_turn(packed)
        first = jnp.where(odd == 1, turned, packed)
        second = jnp.where(odd == 1, packed, turned)
        q = jnp.where(keep, jnp.concatenate([first, second], axis=0), 0.0)
        q_all[128 * b : 128 * (b + 1)] = q.astype(BF16)

    for b in range(4):
        rows = slice(256 * b, 256 * (b + 1))
        s = dot_nt(q_all[rows], wide[:, :LANES])
        m = jnp.max(s, axis=1, keepdims=True)
        e = jnp.exp(s - m).astype(BF16)
        full = dot_nn(e, wide[...])
        total = full[:, LANES:]
        o_all[rows] = full[:, :LANES] / total
        l_all[rows] = m + jnp.log(total) + log

    pick = jnp.where(
        lax.broadcasted_iota(jnp.int32, (16, LANES), 0) == lane_ids((16, LANES)), 1.0, 0.0
    ).astype(BF16)
    for b in range(8):
        out = o_all[128 * b : 128 * (b + 1)]
        turned = half_turn(out)
        left = jnp.where(odd == 1, out[:64], turned[:64])
        right = jnp.where(odd == 1, turned[64:], out[64:])
        out_ref[b, :64] = jnp.where(low, left, right).astype(BF16)
        parts = three_parts(l_all[128 * b : 128 * (b + 1)])
        stats = jnp.zeros((128, LANES), F32)
        for i in range(3):
            stats = jnp.where(lane == i, parts[i], stats)
        out_ref[b, 64:] = dot_nt(pick, stats.astype(BF16)).astype(BF16)


def final_kernel(band_ref, o_ref, st_ref, rx_ref, ry_ref, p1_ref, p2_ref, wo_ref, out_ref, att):
    odd = band_ref[0] % 2
    polar = is_polar(band_ref[0])
    src = lax.broadcasted_iota(jnp.int32, (LANES, 512), 0) // 3
    dst = lax.broadcasted_iota(jnp.int32, (LANES, 512), 1)
    head = 2 * (dst // LANES) + jnp.where(dst % LANES < HDIM, 1, 0)
    pick = jnp.where(src == head, 1.0, 0.0).astype(BF16)
    for r, ret in ((0, rx_ref), (1, ry_ref)):
        lse = dot_nn(st_ref[r], pick)
        lse_ret = dot_nn(ret[PAIRS], pick)
        mine = jnp.concatenate([o_ref[p, r] for p in range(PAIRS)], axis=1)
        other = jnp.concatenate([ret[p] for p in range(PAIRS)], axis=1).astype(F32)
        if r == 0:
            lse_ret = jnp.where(polar, MASKED, lse_ret)
            other = jnp.where(polar, 0.0, other)
        top = jnp.maximum(lse, lse_ret)
        wa = jnp.exp(lse - top)
        wb = jnp.exp(lse_ret - top)
        att[r * 128 : (r + 1) * 128] = ((mine * wa + other * wb) / (wa + wb)).astype(BF16)
        if r == 0:

            @pl.when(polar)
            def _():
                low = lane_ids((64, LANES)) < HDIM
                row = lax.broadcasted_iota(jnp.int32, (16, LANES), 0)
                col = lane_ids((16, LANES))
                pick_even = jnp.where((row < 3) & (col >= HDIM), 1.0, 0.0).astype(BF16)
                pick_odd = jnp.where((row < 3) & (col < HDIM), 1.0, 0.0).astype(BF16)
                for p in range(PAIRS):
                    ml = lse[:, p * LANES : (p + 1) * LANES]
                    vals, logs = [], []
                    for ref in (p1_ref, p2_ref):
                        even32, odd32 = ref[2 * p, :64].astype(F32), ref[2 * p + 1, :64].astype(F32)
                        first = jnp.where(low, odd32, half_turn(even32))
                        second = jnp.where(low, half_turn(odd32), even32)
                        vals.append(jnp.concatenate([first, second], axis=0))
                        logs.append(dot_tn(ref[2 * p, 64:], pick_even) + dot_tn(ref[2 * p + 1, 64:], pick_odd))
                    best = jnp.maximum(ml, jnp.maximum(logs[0], logs[1]))
                    w0 = jnp.exp(ml - best)
                    w1 = jnp.exp(logs[0] - best)
                    w2 = jnp.exp(logs[1] - best)
                    merged = (o_ref[p, 0] * w0 + vals[0] * w1 + vals[1] * w2) / (w0 + w1 + w2)
                    att[:128, p * LANES : (p + 1) * LANES] = merged.astype(BF16)

    order = []
    for p in range(PAIRS):
        order += [wo_ref[p * LANES + HDIM : (p + 1) * LANES], wo_ref[p * LANES : p * LANES + HDIM]]
    w = jnp.concatenate(order, axis=0)
    out = dot_nn(att[...], w).astype(BF16)
    out_ref[odd] = out[:128]
    out_ref[1 - odd] = out[128:]


def call(kernel, outs, in_specs, flops, nbytes, scratch=()):
    return pl.pallas_call(
        kernel,
        out_shape=outs,
        grid=(1,),
        in_specs=in_specs,
        out_specs=jax.tree.map(lambda _: VMEM, outs),
        scratch_shapes=list(scratch),
        compiler_params=PARAMS,
        cost_estimate=cost(flops, nbytes),
    )


def sds(shape, dtype=BF16):
    return jax.ShapeDtypeStruct(shape, dtype)


def ring(n, k):
    return [(i, (i + k) % n) for i in range(n)]


def body(gf, widths, wq, wkv, wo):
    nlat, nlon = NLAT // 2, 16
    li = lax.axis_index("lat").astype(jnp.int32)
    lj = lax.axis_index("lon").astype(jnp.int32)
    band, sector = li.reshape(1), lj.reshape(1)
    table = jnp.asarray(row_tables())
    inner = [(i, i ^ 1) for i in range(nlat)]
    outer = [(i, i + 1 if i % 2 else i - 1) for i in range(1, nlat - 1)]
    groups = [list(range(8)), list(range(8, 16))]

    last, lead = call(
        edge_kernel, (sds((2, 16, 512)), sds((2, 16, 512))), [SMEM, ANY], 1000, 100_000,
        [pltpu.SemaphoreType.DMA((4,))],
    )(band, gf)
    over = lax.ppermute(gf, "lat", outer)
    beside = lax.ppermute(gf, "lat", inner)
    west = lax.ppermute(last, "lon", ring(nlon, 1))
    east = lax.ppermute(lead, "lon", ring(nlon, -1))
    qx, qy, pq, base = call(
        early_kernel,
        (sds((PAIRS, 128, LANES)), sds((PAIRS, 128, LANES)), sds((HEADS, 64, LANES)), sds((256, 1024), F32)),
        [SMEM, VMEM, VMEM, VMEM],
        600_000_000, 6_000_000,
    )(band, gf, wq, wkv)

    kv, kvx, mine, swap = call(
        keyval_kernel,
        (sds((2, HEADS, 128, LANES)), sds((HEADS, 128, LANES)),
         sds((HEADS, 192, LANES)), sds((HEADS, 192, LANES))),
        [SMEM, SMEM] + [VMEM] * 8,
        1_000_000_000, 4_000_000,
    )(band, table, gf, over, beside, west, east, pq, base, wkv)

    got = lax.ppermute(swap, "lat", inner)
    picked = call(pick_kernel, sds((2 * HEADS, 192, LANES)), [SMEM, VMEM, VMEM], 1000, 1_000_000)(
        band, mine, got
    )
    all_polar = lax.all_to_all(picked, "lon", 0, 0)

    kv_later, all_polar = lax.optimization_barrier((kv, all_polar))
    kvw = lax.ppermute(kv_later, "lon", ring(nlon, 1))
    kve = lax.ppermute(kv_later, "lon", ring(nlon, -1))
    kvx, qx_later, qy_later, picked = lax.optimization_barrier((kvx, qx, qy, picked))
    qo = lax.ppermute(qx_later, "lat", outer)
    qi = lax.ppermute(qy_later, "lat", inner)

    even = li % 2 == 0
    x = kvx
    for pairs, here in (
        ([(0, 8), (15, 7)], jnp.where(even, li == 8, li == 7)),
        ([(0, 4), (8, 12), (15, 11), (7, 3)], li % 8 == jnp.where(even, 4, 3)),
        (
            [(0, 2), (4, 6), (8, 10), (12, 14), (15, 13), (11, 9), (7, 5), (3, 1)],
            li % 4 == jnp.where(even, 2, 1),
        ),
    ):
        x = jnp.where(here, lax.ppermute(x, "lat", pairs), x)
    x2 = lax.ppermute(x, "lat", inner)

    part = call(
        polar_kernel, sds((8, 80, LANES)), [SMEM, SMEM, SMEM, VMEM],
        6_000_000_000, 2_000_000,
        [pltpu.VMEM((2048, 2 * LANES), BF16), pltpu.VMEM((1024, LANES), BF16),
         pltpu.VMEM((1024, LANES), F32), pltpu.VMEM((1024, LANES), F32)],
    )(band, sector, table, all_polar)
    part = lax.all_to_all(part, "lon", 0, 0, axis_index_groups=groups)

    o, st, ret_o, ret_i = call(
        window_kernel,
        (sds((PAIRS, 2, 128, LANES), F32), sds((2, 128, LANES)),
         sds((PAIRS + 1, 128, LANES)), sds((PAIRS + 1, 128, LANES))),
        [SMEM, SMEM, SMEM] + [VMEM] * 9,
        8_000_000_000, 4_000_000,
        [pltpu.VMEM((384, 384), F32), pltpu.VMEM((384, 384), F32)],
    )(band, table, widths, qo, qx, qy, qi, kv, kvw, kve, x, x2)
    ret_x = lax.ppermute(ret_o, "lat", outer)
    ret_y = lax.ppermute(ret_i, "lat", inner)

    part, o = lax.optimization_barrier((part, o))
    part2 = lax.ppermute(part, "lat", inner)

    return call(
        final_kernel, sds((2, 128, 512)), [SMEM] + [VMEM] * 7,
        1_000_000_000, 3_000_000, [pltpu.VMEM((256, 512), BF16)],
    )(band, o, st, ret_x, ret_y, part, part2, wo)


def solution(mesh):
    in_specs = (P("lat", "lon", None), P(), P(), P(), P())
    return jax.shard_map(body, mesh=mesh, in_specs=in_specs, out_specs=P("lat", "lon", None), check_vma=False)
```

time: 127 us -> 92.8 us (0.73)
  the two profiles are of different devices: /device:TPU:7 before, /device:TPU:15 now
where the time goes in v2:
time: 92.8 us; the launch traced here: 92.2 us
  starting transfers between devices  44.8 us (48%)
  waiting for transfers between devices  20.5 us (22%)
  Pallas kernels  16.5 us (18%)
  local copies, waits for them, and re-layouts  10.1 us (11%)
    unnamed x26, local copies, waits for them, and re-layouts  10.1 us
    ppermute x1, waiting for transfers between devices, body(): ret_x = lax.ppermute(ret_o, 'lat', outer)  8.21 us
    ppermute x3, waiting for transfers between devices, body(): x = jnp.where(here, lax.ppermute(x, 'lat', pairs), x)  6.47 us
    pallas_call x1, Pallas kernels, body(): call(window_kernel, (sds((PAIRS, 2, 128, LANES), F32), sds((2, 128, LANES...  6.43 us
    ppermute x1, starting transfers between devices, body(): qo = lax.ppermute(qx_later, 'lat', outer)  6.19 us
    all_to_all x1, starting transfers between devices, body(): all_polar = lax.all_to_all(picked, 'lon', 0, 0)  5.62 us
    all_to_all x1, starting transfers between devices, body(): part = lax.all_to_all(part, 'lon', 0, 0, axis_index_groups=groups)  5.19 us
    ppermute x1, starting transfers between devices, body(): east = lax.ppermute(lead, 'lon', ring(nlon, -1))  4.81 us
  transfers between devices with their start and end apart: 18, of which 6 were waited for; matrix products, arithmetic and copies ran while one was open for 0% of the time, Pallas kernels for 13%

profile of v2, /device:TPU:15, one launch (start us, length us, event | category | flops | bytes accessed | tf_op | source)
XLA Modules:
  0.0 92.2 jit_solution(144913536827002720)
XLA Ops:
  0.0 0.7 collective-permute-start.1
  0.7 3.9 %collective-permute-start = (bf16[2,128,512]{2,1,0:T(8,128)(2,1)}, bf16[2,128,512]{2,1,0:T(8,128)(2,1)S(1)}, u32[]{:S(2)}, u32[]{:S(2)}) collective-permute-start(bf16[2,128,512]{2,1,0:T(8,128)(2,1)} %f_ref.5), channel_id=1, source_target_pairs={{16,32},{32,16},{48,64},{64,48},{80,96},{96,80},{112,128},{128,112... | collective-permute-start | bytes 786440 | tf_op jit(solution)/shard_map/ppermute | solution.py:342
  4.6 0.9 %copy-done.2 = bf16[2,128,512]{2,1,0:T(8,128)(2,1)S(1)} copy-done((bf16[2,128,512]{2,1,0:T(8,128)(2,1)S(1)}, bf16[2,128,512]{2,1,0:T(8,128)(2,1)}, u32[]{:S(2)}) %copy-start.2) | copy-done | bytes 262168
  5.5 0.1 shard_map.64
  5.6 1.7 %collective-permute-start.2 = (bf16[2,16,512]{2,1,0:T(8,128)(2,1)S(1)}, bf16[2,16,512]{2,1,0:T(8,128)(2,1)S(1)}, u32[]{:S(2)}, u32[]{:S(2)}) collective-permute-start(bf16[2,16,512]{2,1,0:T(8,128)(2,1)S(1)} %get-tuple-element.26), channel_id=1, source_target_pairs={{0,1},{1,2},{2,3},{3,4},{4,5},{5,6},{6,7},{7,8},{8,9},{9,10},{10,1... | collective-permute-start | bytes 98312 | tf_op jit(solution)/shard_map/ppermute | solution.py:344
  7.3 4.8 %collective-permute-start.3 = (bf16[2,16,512]{2,1,0:T(8,128)(2,1)S(1)}, bf16[2,16,512]{2,1,0:T(8,128)(2,1)S(1)}, u32[]{:S(2)}, u32[]{:S(2)}) collective-permute-start(bf16[2,16,512]{2,1,0:T(8,128)(2,1)S(1)} %get-tuple-element.27), channel_id=1, source_target_pairs={{0,15},{1,0},{2,1},{3,2},{4,3},{5,4},{6,5},{7,6},{8,7},{9,8},{10,9... | collective-permute-start | bytes 98312 | tf_op jit(solution)/shard_map/ppermute | solution.py:345
  12.1 1.9 %copy-done = bf16[1536,1024]{1,0:T(8,128)(2,1)S(1)} copy-done((bf16[1536,1024]{1,0:T(8,128)(2,1)S(1)}, bf16[1536,1024]{1,0:T(8,128)(2,1)}, u32[]{:S(2)}) %copy-start) | copy-done | bytes 3145752
  14.0 1.0 %copy-done.3 = bf16[512,512]{1,0:T(8,128)(2,1)S(1)} copy-done((bf16[512,512]{1,0:T(8,128)(2,1)S(1)}, bf16[512,512]{1,0:T(8,128)(2,1)}, u32[]{:S(2)}) %copy-start.3) | copy-done | bytes 524312
  15.1 0.6 shard_map.65
  15.7 0.0 collective-permute-done.2.west_ref
  15.7 0.0 collective-permute-done.3.east_ref
  15.7 0.0 collective-permute-done.1.inner_ref
  15.7 0.0 collective-permute-done.outer_ref
  15.7 1.3 %copy-done.1 = bf16[1536,1024]{1,0:T(8,128)(2,1)S(1)} copy-done((bf16[1536,1024]{1,0:T(8,128)(2,1)S(1)}, bf16[1536,1024]{1,0:T(8,128)(2,1)}, u32[]{:S(2)}) %copy-start.1) | copy-done | bytes 3145752
  17.0 2.2 %shard_map.66 = (bf16[2,8,128,128]{3,2,1,0:T(8,128)(2,1)S(1)}, bf16[8,128,128]{2,1,0:T(8,128)(2,1)S(1)}, bf16[8,192,128]{2,1,0:T(8,128)(2,1)S(1)}, bf16[8,192,128]{2,1,0:T(8,128)(2,1)S(1)}) custom-call(s32[1]{0:T(128)} %bitcast.band_ref, f32[128]{0:T(128)S(1)} %copy-done.4, bf16[2,128,512]{2,1,0:T(8,128)(2,1)S(1)} %copy-done.2, ...), custom_call_target="tpu_custom_call" | custom-call | flops 1000000000 | bytes 4000000 | tf_op jit(solution)/shard_map/pallas_call | solution.py:353
  19.2 0.1 collective-permute-start.4
  19.3 1.7 %collective-permute-done.4.got_ref = bf16[8,192,128]{2,1,0:T(8,128)(2,1)S(1)} collective-permute-done((bf16[8,192,128]{2,1,0:T(8,128)(2,1)S(1)}, bf16[8,192,128]{2,1,0:T(8,128)(2,1)S(1)}, u32[]{:S(2)}, u32[]{:S(2)}) %collective-permute-start.4) | collective-permute-done | bytes 393248 | tf_op jit(solution)/shard_map/ppermute | solution.py:361
  21.0 1.0 %shard_map.67 = bf16[16,192,128]{2,1,0:T(8,128)(2,1)} custom-call(s32[1]{0:T(128)} %bitcast.band_ref, bf16[8,192,128]{2,1,0:T(8,128)(2,1)S(1)} %get-tuple-element.31.own_ref, bf16[8,192,128]{2,1,0:T(8,128)(2,1)S(1)} %collective-permute-done.4.got_ref), custom_call_target="tpu_custom_call" | custom-call | flops 1000 | bytes 1000000 | tf_op jit(solution)/shard_map/pallas_call | solution.py:362
  22.0 1.3 %collective-permute-start.9 = (bf16[8,128,128]{2,1,0:T(8,128)(2,1)S(1)}, bf16[8,128,128]{2,1,0:T(8,128)(2,1)S(1)}, u32[]{:S(2)}, u32[]{:S(2)}) collective-permute-start(bf16[8,128,128]{2,1,0:T(8,128)(2,1)S(1)} %get-tuple-element.40), channel_id=1, source_target_pairs={{0,128},{240,112},{1,129},{241,113},{2,130},{242,114},{3,131},{243... | collective-permute-start | bytes 786440 | tf_op jit(solution)/shard_map/ppermute | solution.py:384
  23.3 5.6 %all-to-all-start = ((bf16[16,192,128]{2,1,0:T(8,128)(2,1)}), bf16[16,192,128]{2,1,0:T(8,128)(2,1)S(1)}, u32[]{:S(2)}, u32[]{:S(2)}) async-start(bf16[16,192,128]{2,1,0:T(8,128)(2,1)} %shard_map.67), calls=%async_computation | async-start | bytes 1572864 | tf_op jit(solution)/shard_map/all_to_all | solution.py:365
  28.9 1.7 %collective-permute-done.9 = bf16[8,128,128]{2,1,0:T(8,128)(2,1)S(1)} collective-permute-done((bf16[8,128,128]{2,1,0:T(8,128)(2,1)S(1)}, bf16[8,128,128]{2,1,0:T(8,128)(2,1)S(1)}, u32[]{:S(2)}, u32[]{:S(2)}) %collective-permute-start.9) | collective-permute-done | bytes 262176 | tf_op jit(solution)/shard_map/ppermute | solution.py:384
  30.6 1.3 %collective-permute-start.10 = (bf16[8,128,128]{2,1,0:T(8,128)(2,1)S(1)}, bf16[8,128,128]{2,1,0:T(8,128)(2,1)S(1)}, u32[]{:S(2)}, u32[]{:S(2)}) collective-permute-start(bf16[8,128,128]{2,1,0:T(8,128)(2,1)S(1)} %broadcast_select_fusion), channel_id=1, source_target_pairs={{0,64},{128,192},{240,176},{112,48},{1,65},{129,193},{241,177},{11... | collective-permute-start | bytes 786440 | tf_op jit(solution)/shard_map/ppermute | solution.py:384
  32.0 4.8 %collective-permute-done.10 = bf16[8,128,128]{2,1,0:T(8,128)(2,1)S(1)} collective-permute-done((bf16[8,128,128]{2,1,0:T(8,128)(2,1)S(1)}, bf16[8,128,128]{2,1,0:T(8,128)(2,1)S(1)}, u32[]{:S(2)}, u32[]{:S(2)}) %collective-permute-start.10) | collective-permute-done | bytes 262176 | tf_op jit(solution)/shard_map/ppermute | solution.py:384
  36.8 1.3 %collective-permute-start.11 = (bf16[8,128,128]{2,1,0:T(8,128)(2,1)S(1)}, bf16[8,128,128]{2,1,0:T(8,128)(2,1)S(1)}, u32[]{:S(2)}, u32[]{:S(2)}) collective-permute-start(bf16[8,128,128]{2,1,0:T(8,128)(2,1)S(1)} %broadcast_select_fusion.1), channel_id=1, source_target_pairs={{0,32},{64,96},{128,160},{192,224},{240,208},{176,144},{112,80},{4... | collective-permute-start | bytes 786440 | tf_op jit(solution)/shard_map/ppermute | solution.py:384
  38.1 6.2 %collective-permute-start.5 = (bf16[4,128,128]{2,1,0:T(8,128)(2,1)S(1)}, bf16[4,128,128]{2,1,0:T(8,128)(2,1)S(1)}, u32[]{:S(2)}, u32[]{:S(2)}) collective-permute-start(bf16[4,128,128]{2,1,0:T(8,128)(2,1)S(1)} %get-tuple-element.37.qx_ref), channel_id=1, source_target_pairs={{16,32},{32,16},{48,64},{64,48},{80,96},{96,80},{112,128},{128,112... | collective-permute-start | bytes 393224 | tf_op jit(solution)/shard_map/ppermute | solution.py:371
  44.3 0.1 collective-permute-start.6
  44.4 0.0 collective-permute-done.11
  44.5 2.9 %collective-permute-start.12 = (bf16[8,128,128]{2,1,0:T(8,128)(2,1)S(1)}, bf16[8,128,128]{2,1,0:T(8,128)(2,1)S(1)}, u32[]{:S(2)}, u32[]{:S(2)}) collective-permute-start(bf16[8,128,128]{2,1,0:T(8,128)(2,1)S(1)} %broadcast_select_fusion.2.p1_ref), channel_id=1, source_target_pairs={{0,16},{16,0},{32,48},{48,32},{64,80},{80,64},{96,112},{112,96},{1... | collective-permute-start | bytes 786440 | tf_op jit(solution)/shard_map/ppermute | solution.py:385
  47.3 0.8 all-to-all-done.in_ref
  48.1 3.1 %collective-permute-start.8 = (bf16[2,8,128,128]{3,2,1,0:T(8,128)(2,1)S(1)}, bf16[2,8,128,128]{3,2,1,0:T(8,128)(2,1)S(1)}, u32[]{:S(2)}, u32[]{:S(2)}) collective-permute-start(bf16[2,8,128,128]{3,2,1,0:T(8,128)(2,1)S(1)} %get-tuple-element.39.kv_ref), channel_id=1, source_target_pairs={{0,15},{1,0},{2,1},{3,2},{4,3},{5,4},{6,5},{7,6},{8,7},{9,8},{10,9... | collective-permute-start | bytes 1572872 | tf_op jit(solution)/shard_map/ppermute | solution.py:369
  51.2 4.6 %shard_map.68 = bf16[8,80,128]{2,1,0:T(8,128)(2,1)} custom-call(s32[1]{0:T(128)} %bitcast.band_ref, s32[1]{0:T(128)} %bitcast.1.sector_ref, f32[128]{0:T(128)S(1)} %copy-done.4, bf16[16,192,128]{2,1,0:T(8,128)(2,1)S(1)} %all-to-all-done.in_ref), custom_call_target="tpu_custom_call" | custom-call | flops 6000000000 | bytes 2000000 | tf_op jit(solution)/shard_map/pallas_call | solution.py:387
  55.9 5.2 %all-to-all-start.1 = ((bf16[8,80,128]{2,1,0:T(8,128)(2,1)}), bf16[8,80,128]{2,1,0:T(8,128)(2,1)S(1)}, u32[]{:S(2)}, u32[]{:S(2)}) async-start(bf16[8,80,128]{2,1,0:T(8,128)(2,1)} %shard_map.68), calls=%async_computation.1 | async-start | bytes 327680 | tf_op jit(solution)/shard_map/all_to_all | solution.py:393
  61.1 0.6 copy-done.6
  61.7 0.7 copy-done.8
  62.4 3.2 %collective-permute-done.7.kvw_ref = bf16[2,8,128,128]{3,2,1,0:T(8,128)(2,1)S(1)} collective-permute-done((bf16[2,8,128,128]{3,2,1,0:T(8,128)(2,1)S(1)}, bf16[2,8,128,128]{3,2,1,0:T(8,128)(2,1)S(1)}, u32[]{:S(2)}, u32[]{:S(2)}) %collective-permute-start.7) | collective-permute-done | bytes 524320 | tf_op jit(solution)/shard_map/ppermute | solution.py:368
  65.6 0.9 copy-done.7
  66.5 0.9 copy-done.9
  67.4 6.4 %shard_map.69 = (f32[4,2,128,128]{3,2,1,0:T(8,128)S(1)}, bf16[2,128,128]{2,1,0:T(8,128)(2,1)S(1)}, bf16[5,128,128]{2,1,0:T(8,128)(2,1)S(1)}, bf16[5,128,128]{2,1,0:T(8,128)(2,1)S(1)}) custom-call(s32[1]{0:T(128)} %bitcast.band_ref, f32[128]{0:T(128)S(1)} %copy-done.4, s32[32]{0:T(128)S(1)} %copy-done.10, bf16[4,128,128]{2,1,0:T(8,128)(2,1)S(1)} %copy-done.7, ...), custom_call_target="tpu_custom_call" | custom-call | flops 8000000000 | bytes 4000000 | tf_op jit(solution)/shard_map/pallas_call | solution.py:395
  73.9 0.8 copy-done.11
  74.7 0.0 all-to-all-done.1.p1_ref
  74.7 4.7 %collective-permute-start.15 = (bf16[8,80,128]{2,1,0:T(8,128)(2,1)S(1)}, bf16[8,80,128]{2,1,0:T(8,128)(2,1)S(1)}, u32[]{:S(2)}, u32[]{:S(2)}) collective-permute-start(bf16[8,80,128]{2,1,0:T(8,128)(2,1)S(1)} %all-to-all-done.1.p1_ref), channel_id=1, source_target_pairs={{0,16},{16,0},{32,48},{48,32},{64,80},{80,64},{96,112},{112,96},{1... | collective-permute-start | bytes 491528 | tf_op jit(solution)/shard_map/ppermute | solution.py:407
  79.3 1.9 %collective-permute-start.13 = (bf16[5,128,128]{2,1,0:T(8,128)(2,1)S(1)}, bf16[5,128,128]{2,1,0:T(8,128)(2,1)S(1)}, u32[]{:S(2)}, u32[]{:S(2)}) collective-permute-start(bf16[5,128,128]{2,1,0:T(8,128)(2,1)S(1)} %get-tuple-element.44), channel_id=1, source_target_pairs={{16,32},{32,16},{48,64},{64,48},{80,96},{96,80},{112,128},{128,112... | collective-permute-start | bytes 491528 | tf_op jit(solution)/shard_map/ppermute | solution.py:403
  81.3 0.1 collective-permute-start.14
  81.4 0.0 collective-permute-done.15.p2_ref
  81.4 8.2 %collective-permute-done.13.rx_ref = bf16[5,128,128]{2,1,0:T(8,128)(2,1)S(1)} collective-permute-done((bf16[5,128,128]{2,1,0:T(8,128)(2,1)S(1)}, bf16[5,128,128]{2,1,0:T(8,128)(2,1)S(1)}, u32[]{:S(2)}, u32[]{:S(2)}) %collective-permute-start.13) | collective-permute-done | bytes 163872 | tf_op jit(solution)/shard_map/ppermute | solution.py:403
  89.6 0.0 collective-permute-done.14.ry_ref
  89.6 1.0 %copy-done.12 = f32[4,2,128,128]{3,2,1,0:T(8,128)S(1)} copy-done((f32[4,2,128,128]{3,2,1,0:T(8,128)S(1)}, f32[4,2,128,128]{3,2,1,0:T(8,128)}, u32[]{:S(2)}) %copy-start.12) | copy-done | bytes 524312
  90.6 1.5 %shard_map.70 = bf16[2,128,512]{2,1,0:T(8,128)(2,1)} custom-call(s32[1]{0:T(128)} %bitcast.band_ref, f32[4,2,128,128]{3,2,1,0:T(8,128)S(1)} %copy-done.12, bf16[2,128,128]{2,1,0:T(8,128)(2,1)S(1)} %get-tuple-element.43.st_ref, bf16[5,128,128]{2,1,0:T(8,128)(2,1)S(1)} %collective-permute-done.13.rx_ref, ...), custom_call_target="tpu_custom_call" | custom-call | flops 1000000000 | bytes 3000000 | tf_op jit(solution)/shard_map/pallas_call | solution.py:409
  (24 shorter events, 0.1 us)
Async XLA Ops:
  0.0 15.7 %copy-start.4 = (f32[128]{0:T(128)S(1)}, f32[128]{0:T(128)}, u32[]{:S(2)}) copy-start(f32[128]{0:T(128)} %constant.46.clone.table_ref) | copy-start | bytes 1540
  0.0 15.7 %collective-permute-start.1 = (bf16[2,128,512]{2,1,0:T(8,128)(2,1)}, bf16[2,128,512]{2,1,0:T(8,128)(2,1)S(1)}, u32[]{:S(2)}, u32[]{:S(2)}) collective-permute-start(bf16[2,128,512]{2,1,0:T(8,128)(2,1)} %f_ref.5), channel_id=1, source_target_pairs={{0,16},{16,0},{32,48},{48,32},{64,80},{80,64},{96,112},{112,96},{1... | collective-permute-start | bytes 786440 | tf_op jit(solution)/shard_map/ppermute | solution.py:343
  0.7 15.0 %collective-permute-start = (bf16[2,128,512]{2,1,0:T(8,128)(2,1)}, bf16[2,128,512]{2,1,0:T(8,128)(2,1)S(1)}, u32[]{:S(2)}, u32[]{:S(2)}) collective-permute-start(bf16[2,128,512]{2,1,0:T(8,128)(2,1)} %f_ref.5), channel_id=1, source_target_pairs={{16,32},{32,16},{48,64},{64,48},{80,96},{96,80},{112,128},{128,112... | collective-permute-start | bytes 786440 | tf_op jit(solution)/shard_map/ppermute | solution.py:342
  4.5 1.0 %copy-start.2 = (bf16[2,128,512]{2,1,0:T(8,128)(2,1)S(1)}, bf16[2,128,512]{2,1,0:T(8,128)(2,1)}, u32[]{:S(2)}) copy-start(bf16[2,128,512]{2,1,0:T(8,128)(2,1)} %f_ref.5) | copy-start | bytes 786436
  5.6 10.0 %collective-permute-start.2 = (bf16[2,16,512]{2,1,0:T(8,128)(2,1)S(1)}, bf16[2,16,512]{2,1,0:T(8,128)(2,1)S(1)}, u32[]{:S(2)}, u32[]{:S(2)}) collective-permute-start(bf16[2,16,512]{2,1,0:T(8,128)(2,1)S(1)} %get-tuple-element.26), channel_id=1, source_target_pairs={{0,1},{1,2},{2,3},{3,4},{4,5},{5,6},{6,7},{7,8},{8,9},{9,10},{10,1... | collective-permute-start | bytes 98312 | tf_op jit(solution)/shard_map/ppermute | solution.py:344
  7.3 8.3 %collective-permute-start.3 = (bf16[2,16,512]{2,1,0:T(8,128)(2,1)S(1)}, bf16[2,16,512]{2,1,0:T(8,128)(2,1)S(1)}, u32[]{:S(2)}, u32[]{:S(2)}) collective-permute-start(bf16[2,16,512]{2,1,0:T(8,128)(2,1)S(1)} %get-tuple-element.27), channel_id=1, source_target_pairs={{0,15},{1,0},{2,1},{3,2},{4,3},{5,4},{6,5},{7,6},{8,7},{9,8},{10,9... | collective-permute-start | bytes 98312 | tf_op jit(solution)/shard_map/ppermute | solution.py:345
  12.1 1.9 %copy-start = (bf16[1536,1024]{1,0:T(8,128)(2,1)S(1)}, bf16[1536,1024]{1,0:T(8,128)(2,1)}, u32[]{:S(2)}) copy-start(bf16[1536,1024]{1,0:T(8,128)(2,1)} %w_ref.3) | copy-start | bytes 9437188
  14.0 1.0 %copy-start.3 = (bf16[512,512]{1,0:T(8,128)(2,1)S(1)}, bf16[512,512]{1,0:T(8,128)(2,1)}, u32[]{:S(2)}) copy-start(bf16[512,512]{1,0:T(8,128)(2,1)} %wq_ref.1) | copy-start | bytes 1572868
  15.1 1.9 %copy-start.1 = (bf16[1536,1024]{1,0:T(8,128)(2,1)S(1)}, bf16[1536,1024]{1,0:T(8,128)(2,1)}, u32[]{:S(2)}) copy-start(bf16[1536,1024]{1,0:T(8,128)(2,1)} %w_ref.3) | copy-start | bytes 9437188
  19.2 1.8 %collective-permute-start.4 = (bf16[8,192,128]{2,1,0:T(8,128)(2,1)S(1)}, bf16[8,192,128]{2,1,0:T(8,128)(2,1)S(1)}, u32[]{:S(2)}, u32[]{:S(2)}) collective-permute-start(bf16[8,192,128]{2,1,0:T(8,128)(2,1)S(1)} %get-tuple-element.32), channel_id=1, source_target_pairs={{0,16},{16,0},{32,48},{48,32},{64,80},{80,64},{96,112},{112,96},{1... | collective-permute-start | bytes 1179656 | tf_op jit(solution)/shard_map/ppermute | solution.py:361
  22.0 8.6 %collective-permute-start.9 = (bf16[8,128,128]{2,1,0:T(8,128)(2,1)S(1)}, bf16[8,128,128]{2,1,0:T(8,128)(2,1)S(1)}, u32[]{:S(2)}, u32[]{:S(2)}) collective-permute-start(bf16[8,128,128]{2,1,0:T(8,128)(2,1)S(1)} %get-tuple-element.40), channel_id=1, source_target_pairs={{0,128},{240,112},{1,129},{241,113},{2,130},{242,114},{3,131},{243... | collective-permute-start | bytes 786440 | tf_op jit(solution)/shard_map/ppermute | solution.py:384
  23.3 24.8 %all-to-all-start = ((bf16[16,192,128]{2,1,0:T(8,128)(2,1)}), bf16[16,192,128]{2,1,0:T(8,128)(2,1)S(1)}, u32[]{:S(2)}, u32[]{:S(2)}) async-start(bf16[16,192,128]{2,1,0:T(8,128)(2,1)} %shard_map.67), calls=%async_computation | async-start | bytes 1572864 | tf_op jit(solution)/shard_map/all_to_all | solution.py:365
  30.6 6.1 %collective-permute-start.10 = (bf16[8,128,128]{2,1,0:T(8,128)(2,1)S(1)}, bf16[8,128,128]{2,1,0:T(8,128)(2,1)S(1)}, u32[]{:S(2)}, u32[]{:S(2)}) collective-permute-start(bf16[8,128,128]{2,1,0:T(8,128)(2,1)S(1)} %broadcast_select_fusion), channel_id=1, source_target_pairs={{0,64},{128,192},{240,176},{112,48},{1,65},{129,193},{241,177},{11... | collective-permute-start | bytes 786440 | tf_op jit(solution)/shard_map/ppermute | solution.py:384
  36.8 7.6 %collective-permute-start.11 = (bf16[8,128,128]{2,1,0:T(8,128)(2,1)S(1)}, bf16[8,128,128]{2,1,0:T(8,128)(2,1)S(1)}, u32[]{:S(2)}, u32[]{:S(2)}) collective-permute-start(bf16[8,128,128]{2,1,0:T(8,128)(2,1)S(1)} %broadcast_select_fusion.1), channel_id=1, source_target_pairs={{0,32},{64,96},{128,160},{192,224},{240,208},{176,144},{112,80},{4... | collective-permute-start | bytes 786440 | tf_op jit(solution)/shard_map/ppermute | solution.py:384
  38.1 22.9 %collective-permute-start.5 = (bf16[4,128,128]{2,1,0:T(8,128)(2,1)S(1)}, bf16[4,128,128]{2,1,0:T(8,128)(2,1)S(1)}, u32[]{:S(2)}, u32[]{:S(2)}) collective-permute-start(bf16[4,128,128]{2,1,0:T(8,128)(2,1)S(1)} %get-tuple-element.37.qx_ref), channel_id=1, source_target_pairs={{16,32},{32,16},{48,64},{64,48},{80,96},{96,80},{112,128},{128,112... | collective-permute-start | bytes 393224 | tf_op jit(solution)/shard_map/ppermute | solution.py:371
  44.3 17.4 %collective-permute-start.6 = (bf16[4,128,128]{2,1,0:T(8,128)(2,1)S(1)}, bf16[4,128,128]{2,1,0:T(8,128)(2,1)S(1)}, u32[]{:S(2)}, u32[]{:S(2)}) collective-permute-start(bf16[4,128,128]{2,1,0:T(8,128)(2,1)S(1)} %get-tuple-element.38.qy_ref), channel_id=1, source_target_pairs={{0,16},{16,0},{32,48},{48,32},{64,80},{80,64},{96,112},{112,96},{1... | collective-permute-start | bytes 393224 | tf_op jit(solution)/shard_map/ppermute | solution.py:372
  44.5 17.9 %collective-permute-start.12 = (bf16[8,128,128]{2,1,0:T(8,128)(2,1)S(1)}, bf16[8,128,128]{2,1,0:T(8,128)(2,1)S(1)}, u32[]{:S(2)}, u32[]{:S(2)}) collective-permute-start(bf16[8,128,128]{2,1,0:T(8,128)(2,1)S(1)} %broadcast_select_fusion.2.p1_ref), channel_id=1, source_target_pairs={{0,16},{16,0},{32,48},{48,32},{64,80},{80,64},{96,112},{112,96},{1... | collective-permute-start | bytes 786440 | tf_op jit(solution)/shard_map/ppermute | solution.py:385
  48.1 14.2 %collective-permute-start.8 = (bf16[2,8,128,128]{3,2,1,0:T(8,128)(2,1)S(1)}, bf16[2,8,128,128]{3,2,1,0:T(8,128)(2,1)S(1)}, u32[]{:S(2)}, u32[]{:S(2)}) collective-permute-start(bf16[2,8,128,128]{3,2,1,0:T(8,128)(2,1)S(1)} %get-tuple-element.39.kv_ref), channel_id=1, source_target_pairs={{0,15},{1,0},{2,1},{3,2},{4,3},{5,4},{6,5},{7,6},{8,7},{9,8},{10,9... | collective-permute-start | bytes 1572872 | tf_op jit(solution)/shard_map/ppermute | solution.py:369
  51.2 14.4 %collective-permute-start.7 = (bf16[2,8,128,128]{3,2,1,0:T(8,128)(2,1)S(1)}, bf16[2,8,128,128]{3,2,1,0:T(8,128)(2,1)S(1)}, u32[]{:S(2)}, u32[]{:S(2)}) collective-permute-start(bf16[2,8,128,128]{3,2,1,0:T(8,128)(2,1)S(1)} %get-tuple-element.39.kv_ref), channel_id=1, source_target_pairs={{0,1},{1,2},{2,3},{3,4},{4,5},{5,6},{6,7},{7,8},{8,9},{9,10},{10,1... | collective-permute-start | bytes 1572872 | tf_op jit(solution)/shard_map/ppermute | solution.py:368
  51.2 14.4 %copy-start.10 = (s32[32]{0:T(128)S(1)}, s32[32]{0:T(128)}, u32[]{:S(2)}) copy-start(s32[32]{0:T(128)} %width_ref.1) | copy-start | bytes 388
  55.9 18.8 %all-to-all-start.1 = ((bf16[8,80,128]{2,1,0:T(8,128)(2,1)}), bf16[8,80,128]{2,1,0:T(8,128)(2,1)S(1)}, u32[]{:S(2)}, u32[]{:S(2)}) async-start(bf16[8,80,128]{2,1,0:T(8,128)(2,1)} %shard_map.68), calls=%async_computation.1 | async-start | bytes 327680 | tf_op jit(solution)/shard_map/all_to_all | solution.py:393
  61.0 28.6 %copy-start.5 = (bf16[512,512]{1,0:T(8,128)(2,1)S(1)}, bf16[512,512]{1,0:T(8,128)(2,1)}, u32[]{:S(2)}) copy-start(bf16[512,512]{1,0:T(8,128)(2,1)} %wo_ref.1) | copy-start | bytes 1572868
  61.1 0.6 copy-start.6
  61.7 0.7 copy-start.8
  65.6 0.9 copy-start.7
  66.5 0.9 copy-start.9
  73.9 0.8 copy-start.11
  74.7 6.7 %collective-permute-start.15 = (bf16[8,80,128]{2,1,0:T(8,128)(2,1)S(1)}, bf16[8,80,128]{2,1,0:T(8,128)(2,1)S(1)}, u32[]{:S(2)}, u32[]{:S(2)}) collective-permute-start(bf16[8,80,128]{2,1,0:T(8,128)(2,1)S(1)} %all-to-all-done.1.p1_ref), channel_id=1, source_target_pairs={{0,16},{16,0},{32,48},{48,32},{64,80},{80,64},{96,112},{112,96},{1... | collective-permute-start | bytes 491528 | tf_op jit(solution)/shard_map/ppermute | solution.py:407
  79.3 10.2 %collective-permute-start.13 = (bf16[5,128,128]{2,1,0:T(8,128)(2,1)S(1)}, bf16[5,128,128]{2,1,0:T(8,128)(2,1)S(1)}, u32[]{:S(2)}, u32[]{:S(2)}) collective-permute-start(bf16[5,128,128]{2,1,0:T(8,128)(2,1)S(1)} %get-tuple-element.44), channel_id=1, source_target_pairs={{16,32},{32,16},{48,64},{64,48},{80,96},{96,80},{112,128},{128,112... | collective-permute-start | bytes 491528 | tf_op jit(solution)/shard_map/ppermute | solution.py:403
  81.3 8.3 %collective-permute-start.14 = (bf16[5,128,128]{2,1,0:T(8,128)(2,1)S(1)}, bf16[5,128,128]{2,1,0:T(8,128)(2,1)S(1)}, u32[]{:S(2)}, u32[]{:S(2)}) collective-permute-start(bf16[5,128,128]{2,1,0:T(8,128)(2,1)S(1)} %get-tuple-element.45), channel_id=1, source_target_pairs={{0,16},{16,0},{32,48},{48,32},{64,80},{80,64},{96,112},{112,96},{1... | collective-permute-start | bytes 491528 | tf_op jit(solution)/shard_map/ppermute | solution.py:404
  89.6 1.0 %copy-start.12 = (f32[4,2,128,128]{3,2,1,0:T(8,128)S(1)}, f32[4,2,128,128]{3,2,1,0:T(8,128)}, u32[]{:S(2)}) copy-start(f32[4,2,128,128]{3,2,1,0:T(8,128)} %copy-done.11) | copy-start | bytes 1572868

commit v3 on v2

--- a/solution.py
+++ b/solution.py
@@ -15,7 +15,7 @@
 F32 = jnp.float32
 BF16 = jnp.bfloat16
 VMEM = pl.BlockSpec(memory_space=pltpu.VMEM)
-ANY = pl.BlockSpec(memory_space=pl.ANY)
+HBM = pl.BlockSpec(memory_space=pltpu.HBM)
 SMEM = pl.BlockSpec(memory_space=pltpu.SMEM)
 PARAMS = pltpu.CompilerParams(vmem_limit_bytes=20 * 1024 * 1024)
 
@@ -40,6 +40,18 @@
     return (band == 0) | (band == NLAT // 2 - 1)
 
 
+def start_all(pairs, sems):
+    copies = [pltpu.make_async_copy(src, dst, sems.at[i]) for i, (src, dst) in enumerate(pairs)]
+    for c in copies:
+        c.start()
+    return copies
+
+
+def wait_all(copies):
+    for c in copies:
+        c.wait()
+
+
 def lane_ids(shape):
     return lax.broadcasted_iota(jnp.int32, shape, len(shape) - 1)
 
@@ -70,15 +82,10 @@
 
 def edge_kernel(band_ref, f_ref, last_ref, lead_ref, sems):
     odd = band_ref[0] % 2
-    copies = []
-    for slot in range(2):
-        row = f_ref.at[odd if slot == 0 else 1 - odd]
-        copies.append(pltpu.make_async_copy(row.at[pl.ds(112, 16)], last_ref.at[slot], sems.at[2 * slot]))
-        copies.append(pltpu.make_async_copy(row.at[pl.ds(0, 16)], lead_ref.at[slot], sems.at[2 * slot + 1]))
-    for c in copies:
-        c.start()
-    for c in copies:
-        c.wait()
+    pairs = []
+    for slot, row in ((0, f_ref.at[odd]), (1, f_ref.at[1 - odd])):
+        pairs += [(row.at[pl.ds(112, 16)], last_ref.at[slot]), (row.at[pl.ds(0, 16)], lead_ref.at[slot])]
+    wait_all(start_all(pairs, sems))
 
 
 def early_kernel(band_ref, f_ref, wq_ref, w_ref, qx_ref, qy_ref, pq_ref, base_ref):
@@ -103,6 +110,8 @@
     band = band_ref[0]
     odd = band % 2
     coef = [table_ref[8 * band + i] for i in range(4)]
+    for ref in (mine_ref, swap_ref):
+        ref[:, 128:] = pq_ref[...]
     own = [f_ref[odd], f_ref[1 - odd]]
     rows = [outer_ref[1 - odd].astype(F32), own[0].astype(F32), own[1].astype(F32), inner_ref[odd].astype(F32)]
     cell = lax.broadcasted_iota(jnp.int32, (128, 512), 0)
@@ -110,9 +119,9 @@
     for r in range(2):
         lat.append((coef[2 * r] * rows[r] + coef[2 * r + 1] * rows[r + 2]).astype(BF16))
         mid = rows[r + 1]
-        w = jnp.where(cell == 0, west_ref[r, 15:16].astype(F32), pltpu.roll(mid, 1, 0))
-        e = jnp.where(cell == 127, east_ref[r, 0:1].astype(F32), pltpu.roll(mid, 127, 0))
-        lon.append((0.5 * (w + e)).astype(BF16))
+        before = jnp.where(cell == 0, west_ref[r, 15:16].astype(F32), pltpu.roll(mid, 1, 0))
+        after = jnp.where(cell == 127, east_ref[r, 0:1].astype(F32), pltpu.roll(mid, 127, 0))
+        lon.append((0.5 * (before + after)).astype(BF16))
     basis = [jnp.concatenate(x, axis=0) for x in (lat, lon)]
     low = lane_ids((256, LANES)) < HDIM
     for p in range(PAIRS):
@@ -131,14 +140,10 @@
             kvx_ref[h] = packed[:128]
             mine_ref[h, :128] = packed[:128]
             swap_ref[h, :128] = packed[128:]
-    mine_ref[:, 128:] = pq_ref[...]
-    swap_ref[:, 128:] = pq_ref[...]
 
 
 def pick_kernel(band_ref, own_ref, got_ref, out_ref):
-    picked = jnp.where(is_polar(band_ref[0]), own_ref[...], got_ref[...])
-    out_ref[:HEADS] = picked
-    out_ref[HEADS:] = picked
+    out_ref[...] = jnp.where(is_polar(band_ref[0]), own_ref[...], got_ref[...])
 
 
 def window_kernel(
@@ -207,18 +212,34 @@
     ri_ref[PAIRS] = stats[3].astype(BF16)
 
 
-def polar_kernel(band_ref, sector_ref, table_ref, in_ref, out_ref, wide, q_all, o_all, l_all):
+def polar_near_kernel(band_ref, sector_ref, table_ref, in_ref, out_ref, wide, q_all, o_all, l_all):
+    @pl.when((band_ref[0] < 2) | (band_ref[0] >= NLAT // 2 - 2))
+    def _():
+        queries = [in_ref[b, 128:] for b in range(8)]
+        polar_part(band_ref, sector_ref, table_ref, in_ref, queries, out_ref, 0, wide, q_all, o_all, l_all)
+
+
+def polar_far_kernel(band_ref, sector_ref, table_ref, in_ref, far_ref, part_ref, out_ref, wide, q_all, o_all, l_all):
+    @pl.when((band_ref[0] < 2) | (band_ref[0] >= NLAT // 2 - 2))
+    def _():
+        near = 8 * (sector_ref[0] // 8)
+        queries = [far_ref[b] for b in range(8)]
+        polar_part(band_ref, sector_ref, table_ref, in_ref, queries, out_ref, 8 - near, wide, q_all, o_all, l_all)
+        for b in range(8):
+            out_ref[near + b] = part_ref[b]
+
+
+def polar_part(band_ref, sector_ref, table_ref, in_ref, queries, out_ref, base, wide, q_all, o_all, l_all):
     odd = sector_ref[0] % 2
     log = table_ref[8 * band_ref[0] + 6]
     lane = lane_ids((128, LANES))
     keep = (lane // HDIM) == odd
     low = lane_ids((64, LANES)) < HDIM
-    first_sector = 8 * (sector_ref[0] // 8)
-    for b in range(16):
+    for b in range(8):
         wide[128 * b : 128 * (b + 1), :LANES] = in_ref[b, :128]
-    wide[:, LANES:] = jnp.ones((2048, LANES), BF16)
+    wide[:, LANES:] = jnp.ones((1024, LANES), BF16)
     for b in range(8):
-        packed = in_ref[first_sector + b, 128:].astype(F32)
+        packed = queries[b].astype(F32)
         turned = half_turn(packed)
         first = jnp.where(odd == 1, turned, packed)
         second = jnp.where(odd == 1, packed, turned)
@@ -243,12 +264,12 @@
         turned = half_turn(out)
         left = jnp.where(odd == 1, out[:64], turned[:64])
         right = jnp.where(odd == 1, turned[64:], out[64:])
-        out_ref[b, :64] = jnp.where(low, left, right).astype(BF16)
+        out_ref[base + b, :64] = jnp.where(low, left, right).astype(BF16)
         parts = three_parts(l_all[128 * b : 128 * (b + 1)])
         stats = jnp.zeros((128, LANES), F32)
         for i in range(3):
             stats = jnp.where(lane == i, parts[i], stats)
-        out_ref[b, 64:] = dot_nt(pick, stats.astype(BF16)).astype(BF16)
+        out_ref[base + b, 64:] = dot_nt(pick, stats.astype(BF16)).astype(BF16)
 
 
 def final_kernel(band_ref, o_ref, st_ref, rx_ref, ry_ref, p1_ref, p2_ref, wo_ref, out_ref, att):
@@ -261,7 +282,7 @@
     for r, ret in ((0, rx_ref), (1, ry_ref)):
         lse = dot_nn(st_ref[r], pick)
         lse_ret = dot_nn(ret[PAIRS], pick)
-        mine = jnp.concatenate([o_ref[p, r] for p in range(PAIRS)], axis=1)
+        mine = jnp.concatenate([o_ref[p, r] for p in range(PAIRS)], axis=1).astype(F32)
         other = jnp.concatenate([ret[p] for p in range(PAIRS)], axis=1).astype(F32)
         if r == 0:
             lse_ret = jnp.where(polar, MASKED, lse_ret)
@@ -282,17 +303,17 @@
                 for p in range(PAIRS):
                     ml = lse[:, p * LANES : (p + 1) * LANES]
                     vals, logs = [], []
-                    for ref in (p1_ref, p2_ref):
-                        even32, odd32 = ref[2 * p, :64].astype(F32), ref[2 * p + 1, :64].astype(F32)
+                    for ref, h in ((p1_ref, 2 * p), (p1_ref, 8 + 2 * p), (p2_ref, 2 * p), (p2_ref, 8 + 2 * p)):
+                        even32, odd32 = ref[h, :64].astype(F32), ref[h + 1, :64].astype(F32)
                         first = jnp.where(low, odd32, half_turn(even32))
                         second = jnp.where(low, half_turn(odd32), even32)
                         vals.append(jnp.concatenate([first, second], axis=0))
-                        logs.append(dot_tn(ref[2 * p, 64:], pick_even) + dot_tn(ref[2 * p + 1, 64:], pick_odd))
-                    best = jnp.maximum(ml, jnp.maximum(logs[0], logs[1]))
-                    w0 = jnp.exp(ml - best)
-                    w1 = jnp.exp(logs[0] - best)
-                    w2 = jnp.exp(logs[1] - best)
-                    merged = (o_ref[p, 0] * w0 + vals[0] * w1 + vals[1] * w2) / (w0 + w1 + w2)
+                        logs.append(dot_tn(ref[h, 64:], pick_even) + dot_tn(ref[h + 1, 64:], pick_odd))
+                    vals.append(o_ref[p, 0].astype(F32))
+                    logs.append(ml)
+                    best = jnp.maximum(ml, jnp.maximum(jnp.maximum(logs[0], logs[1]), jnp.maximum(logs[2], logs[3])))
+                    scales = [jnp.exp(x - best) for x in logs]
+                    merged = sum(v * w for v, w in zip(vals, scales)) / sum(scales)
                     att[:128, p * LANES : (p + 1) * LANES] = merged.astype(BF16)
 
     order = []
@@ -304,13 +325,13 @@
     out_ref[1 - odd] = out[128:]
 
 
-def call(kernel, outs, in_specs, flops, nbytes, scratch=()):
+def call(kernel, outs, in_specs, flops, nbytes, scratch=(), out_specs=None):
     return pl.pallas_call(
         kernel,
         out_shape=outs,
         grid=(1,),
         in_specs=in_specs,
-        out_specs=jax.tree.map(lambda _: VMEM, outs),
+        out_specs=out_specs or jax.tree.map(lambda _: VMEM, outs),
         scratch_shapes=list(scratch),
         compiler_params=PARAMS,
         cost_estimate=cost(flops, nbytes),
@@ -336,7 +357,7 @@
     groups = [list(range(8)), list(range(8, 16))]
 
     last, lead = call(
-        edge_kernel, (sds((2, 16, 512)), sds((2, 16, 512))), [SMEM, ANY], 1000, 100_000,
+        edge_kernel, (sds((2, 16, 512)), sds((2, 16, 512))), [SMEM, HBM], 8_000_000_000, 100_000,
         [pltpu.SemaphoreType.DMA((4,))],
     )(band, gf)
     over = lax.ppermute(gf, "lat", outer)
@@ -359,51 +380,52 @@
     )(band, table, gf, over, beside, west, east, pq, base, wkv)
 
     got = lax.ppermute(swap, "lat", inner)
-    picked = call(pick_kernel, sds((2 * HEADS, 192, LANES)), [SMEM, VMEM, VMEM], 1000, 1_000_000)(
+    picked = call(pick_kernel, sds((HEADS, 192, LANES)), [SMEM] + [VMEM] * 2, 1000, 1_000_000)(
         band, mine, got
     )
-    all_polar = lax.all_to_all(picked, "lon", 0, 0)
-
-    kv_later, all_polar = lax.optimization_barrier((kv, all_polar))
+    all_polar = lax.all_to_all(picked, "lon", 0, 0, axis_index_groups=groups)
+
+    kvx, kv_later, picked = lax.optimization_barrier((kvx, kv, picked))
     kvw = lax.ppermute(kv_later, "lon", ring(nlon, 1))
     kve = lax.ppermute(kv_later, "lon", ring(nlon, -1))
-    kvx, qx_later, qy_later, picked = lax.optimization_barrier((kvx, qx, qy, picked))
-    qo = lax.ppermute(qx_later, "lat", outer)
-    qi = lax.ppermute(qy_later, "lat", inner)
+    qo = lax.ppermute(qx, "lat", outer)
+    qi = lax.ppermute(qy, "lat", inner)
 
     even = li % 2 == 0
     x = kvx
-    for pairs, here in (
-        ([(0, 8), (15, 7)], jnp.where(even, li == 8, li == 7)),
-        ([(0, 4), (8, 12), (15, 11), (7, 3)], li % 8 == jnp.where(even, 4, 3)),
-        (
-            [(0, 2), (4, 6), (8, 10), (12, 14), (15, 13), (11, 9), (7, 5), (3, 1)],
-            li % 4 == jnp.where(even, 2, 1),
-        ),
-    ):
-        x = jnp.where(here, lax.ppermute(x, "lat", pairs), x)
+    for step in (4, 8, 12):
+        got = lax.ppermute(kvx, "lat", [(0, step), (nlat - 1, nlat - 1 - step)])
+        x = jnp.where(jnp.where(even, li, nlat - 1 - li) == step, got, x)
+    got = lax.ppermute(x, "lat", [(i, i + 2) for i in range(0, 16, 4)] + [(i, i - 2) for i in range(3, 16, 4)])
+    x = jnp.where(jnp.where(even, li, nlat - 1 - li) % 4 == 2, got, x)
+    x, kvw, kve = lax.optimization_barrier((x, kvw, kve))
     x2 = lax.ppermute(x, "lat", inner)
-
-    part = call(
-        polar_kernel, sds((8, 80, LANES)), [SMEM, SMEM, SMEM, VMEM],
-        6_000_000_000, 2_000_000,
-        [pltpu.VMEM((2048, 2 * LANES), BF16), pltpu.VMEM((1024, LANES), BF16),
-         pltpu.VMEM((1024, LANES), F32), pltpu.VMEM((1024, LANES), F32)],
-    )(band, sector, table, all_polar)
-    part = lax.all_to_all(part, "lon", 0, 0, axis_index_groups=groups)
 
     o, st, ret_o, ret_i = call(
         window_kernel,
         (sds((PAIRS, 2, 128, LANES), F32), sds((2, 128, LANES)),
          sds((PAIRS + 1, 128, LANES)), sds((PAIRS + 1, 128, LANES))),
         [SMEM, SMEM, SMEM] + [VMEM] * 9,
-        8_000_000_000, 4_000_000,
+        1000, 1000,
         [pltpu.VMEM((384, 384), F32), pltpu.VMEM((384, 384), F32)],
     )(band, table, widths, qo, qx, qy, qi, kv, kvw, kve, x, x2)
     ret_x = lax.ppermute(ret_o, "lat", outer)
     ret_y = lax.ppermute(ret_i, "lat", inner)
 
-    part, o = lax.optimization_barrier((part, o))
+    far = lax.ppermute(all_polar[:, 128:], "lon", [(i, i ^ 8) for i in range(nlon)])
+    all_polar, st = lax.optimization_barrier((all_polar, st))
+    scratch = [pltpu.VMEM((1024, 2 * LANES), BF16), pltpu.VMEM((1024, LANES), BF16),
+               pltpu.VMEM((1024, LANES), F32), pltpu.VMEM((1024, LANES), F32)]
+    part = call(
+        polar_near_kernel, sds((8, 80, LANES)), [SMEM, SMEM, SMEM, VMEM], 5_000_000_000, 1_000_000, scratch
+    )(band, sector, table, all_polar)
+    part = call(
+        polar_far_kernel, sds((16, 80, LANES)), [SMEM, SMEM, SMEM, VMEM, VMEM, VMEM],
+        3_000_000_000, 1_000_000, scratch,
+    )(band, sector, table, all_polar, far, part)
+    part = lax.all_to_all(part, "lon", 0, 0)
+
+    part, ret_x, ret_y = lax.optimization_barrier((part, ret_x, ret_y))
     part2 = lax.ppermute(part, "lat", inner)
 
     return call(

time: 92.8 us -> 85.7 us (0.923)
  the two profiles are of different devices: /device:TPU:15 before, /device:TPU:32 now
where the time goes in v3:
time: 85.7 us; the launch traced here: 84.3 us
  starting transfers between devices  38.9 us (45%)
  waiting for transfers between devices  25.3 us (30%)
  Pallas kernels  18 us (21%)
  local copies, waits for them, and re-layouts  1.67 us (2%)
    all_to_all x1, starting transfers between devices, body(): all_polar = lax.all_to_all(picked, 'lon', 0, 0, axis_index_groups=groups)  10.5 us
    ppermute x3, starting transfers between devices, body(): got = lax.ppermute(kvx, 'lat', [(0, step), (nlat - 1, nlat - 1 - step)])  9.88 us
    all_to_all x1, waiting for transfers between devices, body(): part = lax.all_to_all(part, 'lon', 0, 0)  8.61 us
    all_to_all x1, waiting for transfers between devices, body(): all_polar = lax.all_to_all(picked, 'lon', 0, 0, axis_index_groups=groups)  6.88 us
    pallas_call x1, Pallas kernels, body(): call(window_kernel, (sds((PAIRS, 2, 128, LANES), F32), sds((2, 128, LANES...  6.33 us
    all_to_all x1, starting transfers between devices, body(): part = lax.all_to_all(part, 'lon', 0, 0)  4.8 us
    pallas_call x1, Pallas kernels, body(): call(polar_far_kernel, sds((16, 80, LANES)), [SMEM, SMEM, SMEM, VMEM, VME...  3.16 us
    ppermute x1, starting transfers between devices, body(): kvw = lax.ppermute(kv_later, 'lon', ring(nlon, 1))  3.1 us
  transfers between devices with their start and end apart: 20, of which 9 were waited for; matrix products, arithmetic and copies ran while one was open for 0% of the time, Pallas kernels for 11%

profile of v3, /device:TPU:32, one launch (start us, length us, event | category | flops | bytes accessed | tf_op | source)
XLA Modules:
  0.0 84.3 jit_solution(11761112916915850243)
XLA Ops:
  0.0 0.7 collective-permute-start.2
  0.7 2.9 %collective-permute-start.3 = (bf16[2,128,512]{2,1,0:T(8,128)(2,1)}, bf16[2,128,512]{2,1,0:T(8,128)(2,1)S(1)}, u32[]{:S(2)}, u32[]{:S(2)}) collective-permute-start(bf16[2,128,512]{2,1,0:T(8,128)(2,1)} %f_ref.5), channel_id=1, source_target_pairs={{0,16},{16,0},{32,48},{48,32},{64,80},{80,64},{96,112},{112,96},{1... | collective-permute-start | bytes 786440 | tf_op jit(solution)/shard_map/ppermute | solution.py:364
  3.6 0.9 %copy-done.1 = bf16[2,128,512]{2,1,0:T(8,128)(2,1)S(1)} copy-done((bf16[2,128,512]{2,1,0:T(8,128)(2,1)S(1)}, bf16[2,128,512]{2,1,0:T(8,128)(2,1)}, u32[]{:S(2)}) %copy-start.1) | copy-done | bytes 262168
  4.6 0.1 shard_map.65
  4.7 0.0 copy-start.3
  4.7 2.0 %collective-permute-start.4 = (bf16[2,16,512]{2,1,0:T(8,128)(2,1)S(1)}, bf16[2,16,512]{2,1,0:T(8,128)(2,1)S(1)}, u32[]{:S(2)}, u32[]{:S(2)}) collective-permute-start(bf16[2,16,512]{2,1,0:T(8,128)(2,1)S(1)} %get-tuple-element.31), channel_id=1, source_target_pairs={{0,1},{1,2},{2,3},{3,4},{4,5},{5,6},{6,7},{7,8},{8,9},{9,10},{10,1... | collective-permute-start | bytes 98312 | tf_op jit(solution)/shard_map/ppermute | solution.py:365
  6.7 0.1 collective-permute-start.5
  6.8 0.6 shard_map.64
  7.4 1.3 %collective-permute-done.4.west_ref = bf16[2,16,512]{2,1,0:T(8,128)(2,1)S(1)} collective-permute-done((bf16[2,16,512]{2,1,0:T(8,128)(2,1)S(1)}, bf16[2,16,512]{2,1,0:T(8,128)(2,1)S(1)}, u32[]{:S(2)}, u32[]{:S(2)}) %collective-permute-start.4) | collective-permute-done | bytes 32800 | tf_op jit(solution)/shard_map/ppermute | solution.py:365
  8.7 1.9 %collective-permute-done.5.east_ref = bf16[2,16,512]{2,1,0:T(8,128)(2,1)S(1)} collective-permute-done((bf16[2,16,512]{2,1,0:T(8,128)(2,1)S(1)}, bf16[2,16,512]{2,1,0:T(8,128)(2,1)S(1)}, u32[]{:S(2)}, u32[]{:S(2)}) %collective-permute-start.5) | collective-permute-done | bytes 32800 | tf_op jit(solution)/shard_map/ppermute | solution.py:366
  10.6 0.0 collective-permute-done.2.outer_ref
  10.6 0.0 collective-permute-done.3.inner_ref
  10.6 2.2 %shard_map.66 = (bf16[2,8,128,128]{3,2,1,0:T(8,128)(2,1)S(1)}, bf16[8,128,128]{2,1,0:T(8,128)(2,1)S(1)}, bf16[8,192,128]{2,1,0:T(8,128)(2,1)S(1)}, bf16[8,192,128]{2,1,0:T(8,128)(2,1)S(1)}) custom-call(s32[1]{0:T(128)} %bitcast.band_ref, f32[128]{0:T(128)S(1)} %copy-done.3, bf16[2,128,512]{2,1,0:T(8,128)(2,1)S(1)} %copy-done.1, ...), custom_call_target="tpu_custom_call" | custom-call | flops 1000000000 | bytes 4000000 | tf_op jit(solution)/shard_map/pallas_call | solution.py:374
  12.9 0.0 copy-start.4
  12.9 0.1 collective-permute-start.6
  13.0 1.7 %collective-permute-done.6.got_ref = bf16[8,192,128]{2,1,0:T(8,128)(2,1)S(1)} collective-permute-done((bf16[8,192,128]{2,1,0:T(8,128)(2,1)S(1)}, bf16[8,192,128]{2,1,0:T(8,128)(2,1)S(1)}, u32[]{:S(2)}, u32[]{:S(2)}) %collective-permute-start.6) | collective-permute-done | bytes 393248 | tf_op jit(solution)/shard_map/ppermute | solution.py:382
  14.7 0.8 %shard_map.67 = bf16[8,192,128]{2,1,0:T(8,128)(2,1)} custom-call(s32[1]{0:T(128)} %bitcast.band_ref, bf16[8,192,128]{2,1,0:T(8,128)(2,1)S(1)} %get-tuple-element.37.own_ref, bf16[8,192,128]{2,1,0:T(8,128)(2,1)S(1)} %collective-permute-done.6.got_ref), custom_call_target="tpu_custom_call" | custom-call | flops 1000 | bytes 1000000 | tf_op jit(solution)/shard_map/pallas_call | solution.py:383
  15.5 7.3 %collective-permute-start.7 = (bf16[8,128,128]{2,1,0:T(8,128)(2,1)S(1)}, bf16[8,128,128]{2,1,0:T(8,128)(2,1)S(1)}, u32[]{:S(2)}, u32[]{:S(2)}) collective-permute-start(bf16[8,128,128]{2,1,0:T(8,128)(2,1)S(1)} %get-tuple-element.39), channel_id=1, source_target_pairs={{0,192},{240,48},{1,193},{241,49},{2,194},{242,50},{3,195},{243,51... | collective-permute-start | bytes 786440 | tf_op jit(solution)/shard_map/ppermute | solution.py:397
  22.8 1.3 %collective-permute-start.8 = (bf16[8,128,128]{2,1,0:T(8,128)(2,1)S(1)}, bf16[8,128,128]{2,1,0:T(8,128)(2,1)S(1)}, u32[]{:S(2)}, u32[]{:S(2)}) collective-permute-start(bf16[8,128,128]{2,1,0:T(8,128)(2,1)S(1)} %get-tuple-element.39), channel_id=1, source_target_pairs={{0,128},{240,112},{1,129},{241,113},{2,130},{242,114},{3,131},{243... | collective-permute-start | bytes 786440 | tf_op jit(solution)/shard_map/ppermute | solution.py:397
  24.1 1.3 %collective-permute-start.9 = (bf16[8,128,128]{2,1,0:T(8,128)(2,1)S(1)}, bf16[8,128,128]{2,1,0:T(8,128)(2,1)S(1)}, u32[]{:S(2)}, u32[]{:S(2)}) collective-permute-start(bf16[8,128,128]{2,1,0:T(8,128)(2,1)S(1)} %get-tuple-element.39), channel_id=1, source_target_pairs={{0,64},{240,176},{1,65},{241,177},{2,66},{242,178},{3,67},{243,179... | collective-permute-start | bytes 786440 | tf_op jit(solution)/shard_map/ppermute | solution.py:397
  25.4 3.1 %collective-permute-start.11 = (bf16[2,8,128,128]{3,2,1,0:T(8,128)(2,1)S(1)}, bf16[2,8,128,128]{3,2,1,0:T(8,128)(2,1)S(1)}, u32[]{:S(2)}, u32[]{:S(2)}) collective-permute-start(bf16[2,8,128,128]{3,2,1,0:T(8,128)(2,1)S(1)} %get-tuple-element.40.kv_ref), channel_id=1, source_target_pairs={{0,1},{1,2},{2,3},{3,4},{4,5},{5,6},{6,7},{7,8},{8,9},{9,10},{10,1... | collective-permute-start | bytes 1572872 | tf_op jit(solution)/shard_map/ppermute | solution.py:389
  28.5 0.0 collective-permute-start.12
  28.6 0.9 %collective-permute-done.9 = bf16[8,128,128]{2,1,0:T(8,128)(2,1)S(1)} collective-permute-done((bf16[8,128,128]{2,1,0:T(8,128)(2,1)S(1)}, bf16[8,128,128]{2,1,0:T(8,128)(2,1)S(1)}, u32[]{:S(2)}, u32[]{:S(2)}) %collective-permute-start.9) | collective-permute-done | bytes 262176 | tf_op jit(solution)/shard_map/ppermute | solution.py:397
  29.5 0.1 select_select_fusion
  29.5 1.3 %collective-permute-start.10 = (bf16[8,128,128]{2,1,0:T(8,128)(2,1)S(1)}, bf16[8,128,128]{2,1,0:T(8,128)(2,1)S(1)}, u32[]{:S(2)}, u32[]{:S(2)}) collective-permute-start(bf16[8,128,128]{2,1,0:T(8,128)(2,1)S(1)} %select_select_fusion), channel_id=1, source_target_pairs={{0,32},{64,96},{128,160},{192,224},{48,16},{112,80},{176,144},{240... | collective-permute-start | bytes 786440 | tf_op jit(solution)/shard_map/ppermute | solution.py:399
  30.9 10.5 %all-to-all-start = ((bf16[8,192,128]{2,1,0:T(8,128)(2,1)}), bf16[8,192,128]{2,1,0:T(8,128)(2,1)S(1)}, u32[]{:S(2)}, u32[]{:S(2)}) async-start(bf16[8,192,128]{2,1,0:T(8,128)(2,1)} %shard_map.67), calls=%async_computation | async-start | bytes 786432 | tf_op jit(solution)/shard_map/all_to_all | solution.py:386
  41.4 0.0 collective-permute-done.10
  41.4 1.0 %collective-permute-done.12.kve_ref = bf16[2,8,128,128]{3,2,1,0:T(8,128)(2,1)S(1)} collective-permute-done((bf16[2,8,128,128]{3,2,1,0:T(8,128)(2,1)S(1)}, bf16[2,8,128,128]{3,2,1,0:T(8,128)(2,1)S(1)}, u32[]{:S(2)}, u32[]{:S(2)}) %collective-permute-start.12) | collective-permute-done | bytes 524320 | tf_op jit(solution)/shard_map/ppermute | solution.py:390
  42.4 0.0 collective-permute-start.13
  42.4 0.7 collective-permute-start
  43.1 1.8 %collective-permute-start.1 = (bf16[4,128,128]{2,1,0:T(8,128)(2,1)S(1)}, bf16[4,128,128]{2,1,0:T(8,128)(2,1)S(1)}, u32[]{:S(2)}, u32[]{:S(2)}) collective-permute-start(bf16[4,128,128]{2,1,0:T(8,128)(2,1)S(1)} %get-tuple-element.30.qy_ref), channel_id=1, source_target_pairs={{0,16},{16,0},{32,48},{48,32},{64,80},{80,64},{96,112},{112,96},{1... | collective-permute-start | bytes 393224 | tf_op jit(solution)/shard_map/ppermute | solution.py:392
  44.9 6.9 %all-to-all-done.in_ref = bf16[8,192,128]{2,1,0:T(8,128)(2,1)S(1)} async-done(((bf16[8,192,128]{2,1,0:T(8,128)(2,1)}), bf16[8,192,128]{2,1,0:T(8,128)(2,1)S(1)}, u32[]{:S(2)}, u32[]{:S(2)}) %all-to-all-start) | async-done | bytes 393248 | tf_op jit(solution)/shard_map/all_to_all | solution.py:386
  51.8 0.3 collective-permute-start.14
  52.1 0.0 collective-permute-done.qo_ref
  52.1 6.3 %shard_map.68 = (f32[4,2,128,128]{3,2,1,0:T(8,128)S(1)}, bf16[2,128,128]{2,1,0:T(8,128)(2,1)S(1)}, bf16[5,128,128]{2,1,0:T(8,128)(2,1)S(1)}, bf16[5,128,128]{2,1,0:T(8,128)(2,1)S(1)}) custom-call(s32[1]{0:T(128)} %bitcast.band_ref, f32[128]{0:T(128)S(1)} %copy-done.3, s32[32]{0:T(128)S(1)} %copy-done.4, ...), custom_call_target="tpu_custom_call" | custom-call | flops 1000 | bytes 1000 | tf_op jit(solution)/shard_map/pallas_call | solution.py:404
  58.5 0.7 copy-done.6
  59.1 2.4 %shard_map.69.part_ref = bf16[8,80,128]{2,1,0:T(8,128)(2,1)S(1)} custom-call(s32[1]{0:T(128)} %bitcast.band_ref, s32[1]{0:T(128)} %bitcast.1.sector_ref, f32[128]{0:T(128)S(1)} %copy-done.3, bf16[8,192,128]{2,1,0:T(8,128)(2,1)S(1)} %all-to-all-done.in_ref), custom_call_target="tpu_custom_call" | custom-call | flops 5000000000 | bytes 1000000 | tf_op jit(solution)/shard_map/pallas_call | solution.py:419
  61.6 0.0 copy-start.7
  61.6 0.0 copy-start.5
  61.6 0.0 copy-start.9
  61.6 3.2 %shard_map.70 = bf16[16,80,128]{2,1,0:T(8,128)(2,1)} custom-call(s32[1]{0:T(128)} %bitcast.band_ref, s32[1]{0:T(128)} %bitcast.1.sector_ref, f32[128]{0:T(128)S(1)} %copy-done.3, bf16[8,192,128]{2,1,0:T(8,128)(2,1)S(1)} %all-to-all-done.in_ref, bf16[8,64,128]{2,1,0:T(8,128)(2,1)S(1)} %collective-permute-done.14.far_ref, ...), custom_call_target="tpu_custom_call" | custom-call | flops 3000000000 | bytes 1000000 | tf_op jit(solution)/shard_map/pallas_call | solution.py:422
  64.8 4.8 %all-to-all-start.1 = ((bf16[16,80,128]{2,1,0:T(8,128)(2,1)}), bf16[16,80,128]{2,1,0:T(8,128)(2,1)S(1)}, u32[]{:S(2)}, u32[]{:S(2)}) async-start(bf16[16,80,128]{2,1,0:T(8,128)(2,1)} %shard_map.70), calls=%async_computation.1 | async-start | bytes 655360 | tf_op jit(solution)/shard_map/all_to_all | solution.py:426
  69.6 0.7 collective-permute-start.15
  70.3 0.1 collective-permute-start.16
  70.4 1.4 %collective-permute-done.16.ry_ref = bf16[5,128,128]{2,1,0:T(8,128)(2,1)S(1)} collective-permute-done((bf16[5,128,128]{2,1,0:T(8,128)(2,1)S(1)}, bf16[5,128,128]{2,1,0:T(8,128)(2,1)S(1)}, u32[]{:S(2)}, u32[]{:S(2)}) %collective-permute-start.16) | collective-permute-done | bytes 163872 | tf_op jit(solution)/shard_map/ppermute | solution.py:413
  71.7 8.6 %all-to-all-done.1.p1_ref = bf16[16,80,128]{2,1,0:T(8,128)(2,1)S(1)} async-done(((bf16[16,80,128]{2,1,0:T(8,128)(2,1)}), bf16[16,80,128]{2,1,0:T(8,128)(2,1)S(1)}, u32[]{:S(2)}, u32[]{:S(2)}) %all-to-all-start.1) | async-done | bytes 327712 | tf_op jit(solution)/shard_map/all_to_all | solution.py:426
  80.4 1.6 %collective-permute-done.17.p2_ref = bf16[16,80,128]{2,1,0:T(8,128)(2,1)S(1)} collective-permute-done((bf16[16,80,128]{2,1,0:T(8,128)(2,1)S(1)}, bf16[16,80,128]{2,1,0:T(8,128)(2,1)S(1)}, u32[]{:S(2)}, u32[]{:S(2)}) %collective-permute-start.17) | collective-permute-done | bytes 327712 | tf_op jit(solution)/shard_map/ppermute | solution.py:429
  82.0 2.3 %shard_map.71 = bf16[2,128,512]{2,1,0:T(8,128)(2,1)} custom-call(s32[1]{0:T(128)} %bitcast.band_ref, f32[4,2,128,128]{3,2,1,0:T(8,128)S(1)} %get-tuple-element.44.o_ref, bf16[2,128,128]{2,1,0:T(8,128)(2,1)S(1)} %copy-done.11, bf16[5,128,128]{2,1,0:T(8,128)(2,1)S(1)} %collective-permute-done.15.rx_ref, ...), custom_call_target="tpu_custom_call" | custom-call | flops 1000000000 | bytes 3000000 | tf_op jit(solution)/shard_map/pallas_call | solution.py:431
  (27 shorter events, 0.1 us)
Async XLA Ops:
  0.0 10.6 %collective-permute-start.2 = (bf16[2,128,512]{2,1,0:T(8,128)(2,1)}, bf16[2,128,512]{2,1,0:T(8,128)(2,1)S(1)}, u32[]{:S(2)}, u32[]{:S(2)}) collective-permute-start(bf16[2,128,512]{2,1,0:T(8,128)(2,1)} %f_ref.5), channel_id=1, source_target_pairs={{16,32},{32,16},{48,64},{64,48},{80,96},{96,80},{112,128},{128,112... | collective-permute-start | bytes 786440 | tf_op jit(solution)/shard_map/ppermute | solution.py:363
  0.7 9.9 %collective-permute-start.3 = (bf16[2,128,512]{2,1,0:T(8,128)(2,1)}, bf16[2,128,512]{2,1,0:T(8,128)(2,1)S(1)}, u32[]{:S(2)}, u32[]{:S(2)}) collective-permute-start(bf16[2,128,512]{2,1,0:T(8,128)(2,1)} %f_ref.5), channel_id=1, source_target_pairs={{0,16},{16,0},{32,48},{48,32},{64,80},{80,64},{96,112},{112,96},{1... | collective-permute-start | bytes 786440 | tf_op jit(solution)/shard_map/ppermute | solution.py:364
  3.6 0.9 %copy-start.1 = (bf16[2,128,512]{2,1,0:T(8,128)(2,1)S(1)}, bf16[2,128,512]{2,1,0:T(8,128)(2,1)}, u32[]{:S(2)}) copy-start(bf16[2,128,512]{2,1,0:T(8,128)(2,1)} %f_ref.5) | copy-start | bytes 786436
  4.5 2.2 %copy-start = (bf16[1536,1024]{1,0:T(8,128)(2,1)S(1)}, bf16[1536,1024]{1,0:T(8,128)(2,1)}, u32[]{:S(2)}) copy-start(bf16[1536,1024]{1,0:T(8,128)(2,1)} %w_ref.3) | copy-start | bytes 9437188
  4.6 2.2 %copy-start.2 = (bf16[512,512]{1,0:T(8,128)(2,1)S(1)}, bf16[512,512]{1,0:T(8,128)(2,1)}, u32[]{:S(2)}) copy-start(bf16[512,512]{1,0:T(8,128)(2,1)} %wq_ref.1) | copy-start | bytes 1572868
  4.7 5.9 %copy-start.3 = (f32[128]{0:T(128)S(1)}, f32[128]{0:T(128)}, u32[]{:S(2)}) copy-start(f32[128]{0:T(128)} %constant.39.clone.table_ref) | copy-start | bytes 1540
  4.7 4.0 %collective-permute-start.4 = (bf16[2,16,512]{2,1,0:T(8,128)(2,1)S(1)}, bf16[2,16,512]{2,1,0:T(8,128)(2,1)S(1)}, u32[]{:S(2)}, u32[]{:S(2)}) collective-permute-start(bf16[2,16,512]{2,1,0:T(8,128)(2,1)S(1)} %get-tuple-element.31), channel_id=1, source_target_pairs={{0,1},{1,2},{2,3},{3,4},{4,5},{5,6},{6,7},{7,8},{8,9},{9,10},{10,1... | collective-permute-start | bytes 98312 | tf_op jit(solution)/shard_map/ppermute | solution.py:365
  6.7 3.9 %collective-permute-start.5 = (bf16[2,16,512]{2,1,0:T(8,128)(2,1)S(1)}, bf16[2,16,512]{2,1,0:T(8,128)(2,1)S(1)}, u32[]{:S(2)}, u32[]{:S(2)}) collective-permute-start(bf16[2,16,512]{2,1,0:T(8,128)(2,1)S(1)} %get-tuple-element.32), channel_id=1, source_target_pairs={{0,15},{1,0},{2,1},{3,2},{4,3},{5,4},{6,5},{7,6},{8,7},{9,8},{10,9... | collective-permute-start | bytes 98312 | tf_op jit(solution)/shard_map/ppermute | solution.py:366
  12.9 39.3 %copy-start.4 = (s32[32]{0:T(128)S(1)}, s32[32]{0:T(128)}, u32[]{:S(2)}) copy-start(s32[32]{0:T(128)} %width_ref.1) | copy-start | bytes 388
  12.9 1.8 %collective-permute-start.6 = (bf16[8,192,128]{2,1,0:T(8,128)(2,1)S(1)}, bf16[8,192,128]{2,1,0:T(8,128)(2,1)S(1)}, u32[]{:S(2)}, u32[]{:S(2)}) collective-permute-start(bf16[8,192,128]{2,1,0:T(8,128)(2,1)S(1)} %get-tuple-element.38), channel_id=1, source_target_pairs={{0,16},{16,0},{32,48},{48,32},{64,80},{80,64},{96,112},{112,96},{1... | collective-permute-start | bytes 1179656 | tf_op jit(solution)/shard_map/ppermute | solution.py:382
  15.5 13.0 %collective-permute-start.7 = (bf16[8,128,128]{2,1,0:T(8,128)(2,1)S(1)}, bf16[8,128,128]{2,1,0:T(8,128)(2,1)S(1)}, u32[]{:S(2)}, u32[]{:S(2)}) collective-permute-start(bf16[8,128,128]{2,1,0:T(8,128)(2,1)S(1)} %get-tuple-element.39), channel_id=1, source_target_pairs={{0,192},{240,48},{1,193},{241,49},{2,194},{242,50},{3,195},{243,51... | collective-permute-start | bytes 786440 | tf_op jit(solution)/shard_map/ppermute | solution.py:397
  22.8 5.8 %collective-permute-start.8 = (bf16[8,128,128]{2,1,0:T(8,128)(2,1)S(1)}, bf16[8,128,128]{2,1,0:T(8,128)(2,1)S(1)}, u32[]{:S(2)}, u32[]{:S(2)}) collective-permute-start(bf16[8,128,128]{2,1,0:T(8,128)(2,1)S(1)} %get-tuple-element.39), channel_id=1, source_target_pairs={{0,128},{240,112},{1,129},{241,113},{2,130},{242,114},{3,131},{243... | collective-permute-start | bytes 786440 | tf_op jit(solution)/shard_map/ppermute | solution.py:397
  24.1 5.4 %collective-permute-start.9 = (bf16[8,128,128]{2,1,0:T(8,128)(2,1)S(1)}, bf16[8,128,128]{2,1,0:T(8,128)(2,1)S(1)}, u32[]{:S(2)}, u32[]{:S(2)}) collective-permute-start(bf16[8,128,128]{2,1,0:T(8,128)(2,1)S(1)} %get-tuple-element.39), channel_id=1, source_target_pairs={{0,64},{240,176},{1,65},{241,177},{2,66},{242,178},{3,67},{243,179... | collective-permute-start | bytes 786440 | tf_op jit(solution)/shard_map/ppermute | solution.py:397
  25.4 16.0 %collective-permute-start.11 = (bf16[2,8,128,128]{3,2,1,0:T(8,128)(2,1)S(1)}, bf16[2,8,128,128]{3,2,1,0:T(8,128)(2,1)S(1)}, u32[]{:S(2)}, u32[]{:S(2)}) collective-permute-start(bf16[2,8,128,128]{3,2,1,0:T(8,128)(2,1)S(1)} %get-tuple-element.40.kv_ref), channel_id=1, source_target_pairs={{0,1},{1,2},{2,3},{3,4},{4,5},{5,6},{6,7},{7,8},{8,9},{9,10},{10,1... | collective-permute-start | bytes 1572872 | tf_op jit(solution)/shard_map/ppermute | solution.py:389
  28.5 13.8 %collective-permute-start.12 = (bf16[2,8,128,128]{3,2,1,0:T(8,128)(2,1)S(1)}, bf16[2,8,128,128]{3,2,1,0:T(8,128)(2,1)S(1)}, u32[]{:S(2)}, u32[]{:S(2)}) collective-permute-start(bf16[2,8,128,128]{3,2,1,0:T(8,128)(2,1)S(1)} %get-tuple-element.40.kv_ref), channel_id=1, source_target_pairs={{0,15},{1,0},{2,1},{3,2},{4,3},{5,4},{6,5},{7,6},{8,7},{9,8},{10,9... | collective-permute-start | bytes 1572872 | tf_op jit(solution)/shard_map/ppermute | solution.py:390
  29.5 11.8 %collective-permute-start.10 = (bf16[8,128,128]{2,1,0:T(8,128)(2,1)S(1)}, bf16[8,128,128]{2,1,0:T(8,128)(2,1)S(1)}, u32[]{:S(2)}, u32[]{:S(2)}) collective-permute-start(bf16[8,128,128]{2,1,0:T(8,128)(2,1)S(1)} %select_select_fusion), channel_id=1, source_target_pairs={{0,32},{64,96},{128,160},{192,224},{48,16},{112,80},{176,144},{240... | collective-permute-start | bytes 786440 | tf_op jit(solution)/shard_map/ppermute | solution.py:399
  30.9 20.9 %all-to-all-start = ((bf16[8,192,128]{2,1,0:T(8,128)(2,1)}), bf16[8,192,128]{2,1,0:T(8,128)(2,1)S(1)}, u32[]{:S(2)}, u32[]{:S(2)}) async-start(bf16[8,192,128]{2,1,0:T(8,128)(2,1)} %shard_map.67), calls=%async_computation | async-start | bytes 786432 | tf_op jit(solution)/shard_map/all_to_all | solution.py:386
  42.4 9.7 %collective-permute-start.13 = (bf16[8,128,128]{2,1,0:T(8,128)(2,1)S(1)}, bf16[8,128,128]{2,1,0:T(8,128)(2,1)S(1)}, u32[]{:S(2)}, u32[]{:S(2)}) collective-permute-start(bf16[8,128,128]{2,1,0:T(8,128)(2,1)S(1)} %broadcast_select_fusion.p1_ref), channel_id=1, source_target_pairs={{0,16},{16,0},{32,48},{48,32},{64,80},{80,64},{96,112},{112,96},{1... | collective-permute-start | bytes 786440 | tf_op jit(solution)/shard_map/ppermute | solution.py:402
  42.4 9.7 %collective-permute-start = (bf16[4,128,128]{2,1,0:T(8,128)(2,1)S(1)}, bf16[4,128,128]{2,1,0:T(8,128)(2,1)S(1)}, u32[]{:S(2)}, u32[]{:S(2)}) collective-permute-start(bf16[4,128,128]{2,1,0:T(8,128)(2,1)S(1)} %get-tuple-element.29.qx_ref), channel_id=1, source_target_pairs={{16,32},{32,16},{48,64},{64,48},{80,96},{96,80},{112,128},{128,112... | collective-permute-start | bytes 393224 | tf_op jit(solution)/shard_map/ppermute | solution.py:391
  43.1 9.0 %collective-permute-start.1 = (bf16[4,128,128]{2,1,0:T(8,128)(2,1)S(1)}, bf16[4,128,128]{2,1,0:T(8,128)(2,1)S(1)}, u32[]{:S(2)}, u32[]{:S(2)}) collective-permute-start(bf16[4,128,128]{2,1,0:T(8,128)(2,1)S(1)} %get-tuple-element.30.qy_ref), channel_id=1, source_target_pairs={{0,16},{16,0},{32,48},{48,32},{64,80},{80,64},{96,112},{112,96},{1... | collective-permute-start | bytes 393224 | tf_op jit(solution)/shard_map/ppermute | solution.py:392
  51.8 9.8 %collective-permute-start.14 = (bf16[8,64,128]{2,1,0:T(8,128)(2,1)S(1)}, bf16[8,64,128]{2,1,0:T(8,128)(2,1)S(1)}, u32[]{:S(2)}, u32[]{:S(2)}) collective-permute-start(bf16[8,64,128]{2,1,0:T(8,128)(2,1)S(1)} %slice.4), channel_id=1, source_target_pairs={{0,8},{1,9},{2,10},{3,11},{4,12},{5,13},{6,14},{7,15},{8,0},{9,1},... | collective-permute-start | bytes 393224 | tf_op jit(solution)/shard_map/ppermute | solution.py:415
  58.5 0.7 copy-start.6
  59.1 2.4 %copy-start.8 = (bf16[5,128,128]{2,1,0:T(8,128)(2,1)}, bf16[5,128,128]{2,1,0:T(8,128)(2,1)S(1)}, u32[]{:S(2)}) copy-start(bf16[5,128,128]{2,1,0:T(8,128)(2,1)S(1)} %get-tuple-element.48) | copy-start | bytes 491524
  59.1 2.4 %copy-start.10 = (bf16[2,128,128]{2,1,0:T(8,128)(2,1)}, bf16[2,128,128]{2,1,0:T(8,128)(2,1)S(1)}, u32[]{:S(2)}) copy-start(bf16[2,128,128]{2,1,0:T(8,128)(2,1)S(1)} %get-tuple-element.46.st_ref) | copy-start | bytes 196612
  61.6 8.7 %copy-start.7 = (bf16[5,128,128]{2,1,0:T(8,128)(2,1)S(1)}, bf16[5,128,128]{2,1,0:T(8,128)(2,1)}, u32[]{:S(2)}) copy-start(bf16[5,128,128]{2,1,0:T(8,128)(2,1)} %copy-done.6) | copy-start | bytes 491524
  61.6 20.4 %copy-start.5 = (bf16[512,512]{1,0:T(8,128)(2,1)S(1)}, bf16[512,512]{1,0:T(8,128)(2,1)}, u32[]{:S(2)}) copy-start(bf16[512,512]{1,0:T(8,128)(2,1)} %wo_ref.1) | copy-start | bytes 1572868
  61.6 8.0 %copy-start.9 = (bf16[5,128,128]{2,1,0:T(8,128)(2,1)S(1)}, bf16[5,128,128]{2,1,0:T(8,128)(2,1)}, u32[]{:S(2)}) copy-start(bf16[5,128,128]{2,1,0:T(8,128)(2,1)} %copy-done.8) | copy-start | bytes 491524
  61.6 20.4 %copy-start.11 = (bf16[2,128,128]{2,1,0:T(8,128)(2,1)S(1)}, bf16[2,128,128]{2,1,0:T(8,128)(2,1)}, u32[]{:S(2)}) copy-start(bf16[2,128,128]{2,1,0:T(8,128)(2,1)} %copy-done.10) | copy-start | bytes 196612
  64.8 15.6 %all-to-all-start.1 = ((bf16[16,80,128]{2,1,0:T(8,128)(2,1)}), bf16[16,80,128]{2,1,0:T(8,128)(2,1)S(1)}, u32[]{:S(2)}, u32[]{:S(2)}) async-start(bf16[16,80,128]{2,1,0:T(8,128)(2,1)} %shard_map.70), calls=%async_computation.1 | async-start | bytes 655360 | tf_op jit(solution)/shard_map/all_to_all | solution.py:426
  69.6 0.8 collective-permute-start.15
  70.3 1.5 %collective-permute-start.16 = (bf16[5,128,128]{2,1,0:T(8,128)(2,1)S(1)}, bf16[5,128,128]{2,1,0:T(8,128)(2,1)S(1)}, u32[]{:S(2)}, u32[]{:S(2)}) collective-permute-start(bf16[5,128,128]{2,1,0:T(8,128)(2,1)S(1)} %copy-done.7), channel_id=1, source_target_pairs={{0,16},{16,0},{32,48},{48,32},{64,80},{80,64},{96,112},{112,96},{1... | collective-permute-start | bytes 491528 | tf_op jit(solution)/shard_map/ppermute | solution.py:413
  80.4 1.6 %collective-permute-start.17 = (bf16[16,80,128]{2,1,0:T(8,128)(2,1)S(1)}, bf16[16,80,128]{2,1,0:T(8,128)(2,1)S(1)}, u32[]{:S(2)}, u32[]{:S(2)}) collective-permute-start(bf16[16,80,128]{2,1,0:T(8,128)(2,1)S(1)} %all-to-all-done.1.p1_ref), channel_id=1, source_target_pairs={{0,16},{16,0},{32,48},{48,32},{64,80},{80,64},{96,112},{112,96},{1... | collective-permute-start | bytes 983048 | tf_op jit(solution)/shard_map/ppermute | solution.py:429

commit v4 on v3

--- a/solution.py
+++ b/solution.py
@@ -398,7 +398,7 @@
         x = jnp.where(jnp.where(even, li, nlat - 1 - li) == step, got, x)
     got = lax.ppermute(x, "lat", [(i, i + 2) for i in range(0, 16, 4)] + [(i, i - 2) for i in range(3, 16, 4)])
     x = jnp.where(jnp.where(even, li, nlat - 1 - li) % 4 == 2, got, x)
-    x, kvw, kve = lax.optimization_barrier((x, kvw, kve))
+    x, kvw, kve, qo, qi, all_polar = lax.optimization_barrier((x, kvw, kve, qo, qi, all_polar))
     x2 = lax.ppermute(x, "lat", inner)
 
     o, st, ret_o, ret_i = call(

time: 85.7 us -> 84 us (0.980)
  starting transfers between devices: 38.9 us -> 37.5 us
    ppermute x1, waiting for transfers between devices: 0.01 us -> 3.07 us  [body(): lax.ppermute(x, 'lat', [(i, i + 2) for i in range(0, 16, 4)] + [(i, i - 2...]
    ppermute x1, starting transfers between devices: 0.01 us -> 2.83 us  [body(): kve = lax.ppermute(kv_later, 'lon', ring(nlon, -1))]
    ppermute x1, starting transfers between devices: 3.1 us -> 0.36 us  [body(): kvw = lax.ppermute(kv_later, 'lon', ring(nlon, 1))]
    all_to_all x1, starting transfers between devices: 10.5 us -> 8.55 us  [body(): all_polar = lax.all_to_all(picked, 'lon', 0, 0, axis_index_groups=groups)]
    ppermute x1, starting transfers between devices: 1.84 us -> 0.09 us  [body(): qi = lax.ppermute(qy, 'lat', inner)]
    ppermute x1, starting transfers between devices: 0.27 us -> 1.82 us  [body(): lax.ppermute(all_polar[:, 128:], 'lon', [(i, i ^ 8) for i in range(nlon)])]
    ppermute x1, starting transfers between devices: 0.09 us -> 1.29 us  [body(): ret_y = lax.ppermute(ret_i, 'lat', inner)]
    ppermute x1, waiting for transfers between devices: 0.98 us -> 0.01 us  [body(): kve = lax.ppermute(kv_later, 'lon', ring(nlon, -1))]
  transfers between devices with their start and end apart: 20 -> 20, of which waited for: 9 -> 8; matrix products, arithmetic and copies ran while one was open for 0% -> 0% of each run, Pallas kernels for 11% -> 11%
where the time goes in v4:
time: 84 us; the launch traced here: 83.4 us
  starting transfers between devices  37.5 us (45%)
  waiting for transfers between devices  25.8 us (31%)
  Pallas kernels  18 us (21%)
  local copies, waits for them, and re-layouts  1.67 us (2%)
    ppermute x3, starting transfers between devices, body(): got = lax.ppermute(kvx, 'lat', [(0, step), (nlat - 1, nlat - 1 - step)])  9.88 us
    all_to_all x1, waiting for transfers between devices, body(): part = lax.all_to_all(part, 'lon', 0, 0)  9.07 us
    all_to_all x1, starting transfers between devices, body(): all_polar = lax.all_to_all(picked, 'lon', 0, 0, axis_index_groups=groups)  8.55 us
    pallas_call x1, Pallas kernels, body(): call(window_kernel, (sds((PAIRS, 2, 128, LANES), F32), sds((2, 128, LANES...  6.34 us
    all_to_all x1, waiting for transfers between devices, body(): all_polar = lax.all_to_all(picked, 'lon', 0, 0, axis_index_groups=groups)  6.06 us
    all_to_all x1, starting transfers between devices, body(): part = lax.all_to_all(part, 'lon', 0, 0)  4.27 us
    pallas_call x1, Pallas kernels, body(): call(polar_far_kernel, sds((16, 80, LANES)), [SMEM, SMEM, SMEM, VMEM, VME...  3.16 us
    ppermute x1, waiting for transfers between devices, body(): lax.ppermute(x, 'lat', [(i, i + 2) for i in range(0, 16, 4)] + [(i, i - 2...  3.07 us
  transfers between devices with their start and end apart: 20, of which 8 were waited for; matrix products, arithmetic and copies ran while one was open for 0% of the time, Pallas kernels for 11%

profile of v4, /device:TPU:32, one launch (start us, length us, event | category | flops | bytes accessed | tf_op | source)
XLA Modules:
  0.0 83.4 jit_solution(13597875705727891342)
XLA Ops:
  0.0 0.7 collective-permute-start
  0.7 2.9 %collective-permute-start.1 = (bf16[2,128,512]{2,1,0:T(8,128)(2,1)}, bf16[2,128,512]{2,1,0:T(8,128)(2,1)S(1)}, u32[]{:S(2)}, u32[]{:S(2)}) collective-permute-start(bf16[2,128,512]{2,1,0:T(8,128)(2,1)} %f_ref.5), channel_id=1, source_target_pairs={{0,16},{16,0},{32,48},{48,32},{64,80},{80,64},{96,112},{112,96},{1... | collective-permute-start | bytes 786440 | tf_op jit(solution)/shard_map/ppermute | solution.py:364
  3.6 0.9 %copy-done.1 = bf16[2,128,512]{2,1,0:T(8,128)(2,1)S(1)} copy-done((bf16[2,128,512]{2,1,0:T(8,128)(2,1)S(1)}, bf16[2,128,512]{2,1,0:T(8,128)(2,1)}, u32[]{:S(2)}) %copy-start.1) | copy-done | bytes 262168
  4.6 0.1 shard_map.64
  4.7 0.0 copy-start.3
  4.7 2.0 %collective-permute-start.2 = (bf16[2,16,512]{2,1,0:T(8,128)(2,1)S(1)}, bf16[2,16,512]{2,1,0:T(8,128)(2,1)S(1)}, u32[]{:S(2)}, u32[]{:S(2)}) collective-permute-start(bf16[2,16,512]{2,1,0:T(8,128)(2,1)S(1)} %get-tuple-element.32), channel_id=1, source_target_pairs={{0,1},{1,2},{2,3},{3,4},{4,5},{5,6},{6,7},{7,8},{8,9},{9,10},{10,1... | collective-permute-start | bytes 98312 | tf_op jit(solution)/shard_map/ppermute | solution.py:365
  6.7 0.1 collective-permute-start.3
  6.8 0.6 shard_map.65
  7.4 1.3 %collective-permute-done.2.west_ref = bf16[2,16,512]{2,1,0:T(8,128)(2,1)S(1)} collective-permute-done((bf16[2,16,512]{2,1,0:T(8,128)(2,1)S(1)}, bf16[2,16,512]{2,1,0:T(8,128)(2,1)S(1)}, u32[]{:S(2)}, u32[]{:S(2)}) %collective-permute-start.2) | collective-permute-done | bytes 32800 | tf_op jit(solution)/shard_map/ppermute | solution.py:365
  8.7 1.9 %collective-permute-done.3.east_ref = bf16[2,16,512]{2,1,0:T(8,128)(2,1)S(1)} collective-permute-done((bf16[2,16,512]{2,1,0:T(8,128)(2,1)S(1)}, bf16[2,16,512]{2,1,0:T(8,128)(2,1)S(1)}, u32[]{:S(2)}, u32[]{:S(2)}) %collective-permute-start.3) | collective-permute-done | bytes 32800 | tf_op jit(solution)/shard_map/ppermute | solution.py:366
  10.6 2.2 %shard_map.66 = (bf16[2,8,128,128]{3,2,1,0:T(8,128)(2,1)S(1)}, bf16[8,128,128]{2,1,0:T(8,128)(2,1)S(1)}, bf16[8,192,128]{2,1,0:T(8,128)(2,1)S(1)}, bf16[8,192,128]{2,1,0:T(8,128)(2,1)S(1)}) custom-call(s32[1]{0:T(128)} %bitcast.band_ref, f32[128]{0:T(128)S(1)} %copy-done.3, bf16[2,128,512]{2,1,0:T(8,128)(2,1)S(1)} %copy-done.1, ...), custom_call_target="tpu_custom_call" | custom-call | flops 1000000000 | bytes 4000000 | tf_op jit(solution)/shard_map/pallas_call | solution.py:374
  12.9 0.0 copy-start.4
  12.9 0.1 collective-permute-start.4
  13.0 1.7 %collective-permute-done.4.got_ref = bf16[8,192,128]{2,1,0:T(8,128)(2,1)S(1)} collective-permute-done((bf16[8,192,128]{2,1,0:T(8,128)(2,1)S(1)}, bf16[8,192,128]{2,1,0:T(8,128)(2,1)S(1)}, u32[]{:S(2)}, u32[]{:S(2)}) %collective-permute-start.4) | collective-permute-done | bytes 393248 | tf_op jit(solution)/shard_map/ppermute | solution.py:382
  14.7 0.8 %shard_map.67 = bf16[8,192,128]{2,1,0:T(8,128)(2,1)} custom-call(s32[1]{0:T(128)} %bitcast.band_ref, bf16[8,192,128]{2,1,0:T(8,128)(2,1)S(1)} %get-tuple-element.38.own_ref, bf16[8,192,128]{2,1,0:T(8,128)(2,1)S(1)} %collective-permute-done.4.got_ref), custom_call_target="tpu_custom_call" | custom-call | flops 1000 | bytes 1000000 | tf_op jit(solution)/shard_map/pallas_call | solution.py:383
  15.5 7.3 %collective-permute-start.5 = (bf16[8,128,128]{2,1,0:T(8,128)(2,1)S(1)}, bf16[8,128,128]{2,1,0:T(8,128)(2,1)S(1)}, u32[]{:S(2)}, u32[]{:S(2)}) collective-permute-start(bf16[8,128,128]{2,1,0:T(8,128)(2,1)S(1)} %get-tuple-element.40), channel_id=1, source_target_pairs={{0,192},{240,48},{1,193},{241,49},{2,194},{242,50},{3,195},{243,51... | collective-permute-start | bytes 786440 | tf_op jit(solution)/shard_map/ppermute | solution.py:397
  22.8 1.3 %collective-permute-start.6 = (bf16[8,128,128]{2,1,0:T(8,128)(2,1)S(1)}, bf16[8,128,128]{2,1,0:T(8,128)(2,1)S(1)}, u32[]{:S(2)}, u32[]{:S(2)}) collective-permute-start(bf16[8,128,128]{2,1,0:T(8,128)(2,1)S(1)} %get-tuple-element.40), channel_id=1, source_target_pairs={{0,128},{240,112},{1,129},{241,113},{2,130},{242,114},{3,131},{243... | collective-permute-start | bytes 786440 | tf_op jit(solution)/shard_map/ppermute | solution.py:397
  24.1 1.3 %collective-permute-start.7 = (bf16[8,128,128]{2,1,0:T(8,128)(2,1)S(1)}, bf16[8,128,128]{2,1,0:T(8,128)(2,1)S(1)}, u32[]{:S(2)}, u32[]{:S(2)}) collective-permute-start(bf16[8,128,128]{2,1,0:T(8,128)(2,1)S(1)} %get-tuple-element.40), channel_id=1, source_target_pairs={{0,64},{240,176},{1,65},{241,177},{2,66},{242,178},{3,67},{243,179... | collective-permute-start | bytes 786440 | tf_op jit(solution)/shard_map/ppermute | solution.py:397
  25.4 2.8 %collective-permute-start.10 = (bf16[2,8,128,128]{3,2,1,0:T(8,128)(2,1)S(1)}, bf16[2,8,128,128]{3,2,1,0:T(8,128)(2,1)S(1)}, u32[]{:S(2)}, u32[]{:S(2)}) collective-permute-start(bf16[2,8,128,128]{3,2,1,0:T(8,128)(2,1)S(1)} %get-tuple-element.41.kv_ref), channel_id=1, source_target_pairs={{0,15},{1,0},{2,1},{3,2},{4,3},{5,4},{6,5},{7,6},{8,7},{9,8},{10,9... | collective-permute-start | bytes 1572872 | tf_op jit(solution)/shard_map/ppermute | solution.py:390
  28.3 0.4 collective-permute-start.9
  28.6 8.6 %all-to-all-start = ((bf16[8,192,128]{2,1,0:T(8,128)(2,1)}), bf16[8,192,128]{2,1,0:T(8,128)(2,1)S(1)}, u32[]{:S(2)}, u32[]{:S(2)}) async-start(bf16[8,192,128]{2,1,0:T(8,128)(2,1)} %shard_map.67), calls=%async_computation | async-start | bytes 786432 | tf_op jit(solution)/shard_map/all_to_all | solution.py:386
  37.2 0.0 collective-permute-done.5
  37.2 0.0 collective-permute-done.7
  37.2 0.1 select_select_fusion
  37.3 1.3 %collective-permute-start.8 = (bf16[8,128,128]{2,1,0:T(8,128)(2,1)S(1)}, bf16[8,128,128]{2,1,0:T(8,128)(2,1)S(1)}, u32[]{:S(2)}, u32[]{:S(2)}) collective-permute-start(bf16[8,128,128]{2,1,0:T(8,128)(2,1)S(1)} %select_select_fusion), channel_id=1, source_target_pairs={{0,32},{64,96},{128,160},{192,224},{48,16},{112,80},{176,144},{240... | collective-permute-start | bytes 786440 | tf_op jit(solution)/shard_map/ppermute | solution.py:399
  38.6 0.7 collective-permute-start.11
  39.3 0.1 collective-permute-start.12
  39.4 3.1 %collective-permute-done.8 = bf16[8,128,128]{2,1,0:T(8,128)(2,1)S(1)} collective-permute-done((bf16[8,128,128]{2,1,0:T(8,128)(2,1)S(1)}, bf16[8,128,128]{2,1,0:T(8,128)(2,1)S(1)}, u32[]{:S(2)}, u32[]{:S(2)}) %collective-permute-start.8) | collective-permute-done | bytes 262176 | tf_op jit(solution)/shard_map/ppermute | solution.py:399
  42.5 0.0 collective-permute-done.11.qo_ref
  42.5 0.0 collective-permute-done.10.kve_ref
  42.5 0.0 collective-permute-done.9.kvw_ref
  42.5 6.1 %all-to-all-done.in_ref = bf16[8,192,128]{2,1,0:T(8,128)(2,1)S(1)} async-done(((bf16[8,192,128]{2,1,0:T(8,128)(2,1)}), bf16[8,192,128]{2,1,0:T(8,128)(2,1)S(1)}, u32[]{:S(2)}, u32[]{:S(2)}) %all-to-all-start) | async-done | bytes 393248 | tf_op jit(solution)/shard_map/all_to_all | solution.py:386
  48.6 0.0 collective-permute-start.13
  48.6 1.8 %collective-permute-start.14 = (bf16[8,64,128]{2,1,0:T(8,128)(2,1)S(1)}, bf16[8,64,128]{2,1,0:T(8,128)(2,1)S(1)}, u32[]{:S(2)}, u32[]{:S(2)}) collective-permute-start(bf16[8,64,128]{2,1,0:T(8,128)(2,1)S(1)} %slice.3), channel_id=1, source_target_pairs={{0,8},{1,9},{2,10},{3,11},{4,12},{5,13},{6,14},{7,15},{8,0},{9,1},... | collective-permute-start | bytes 393224 | tf_op jit(solution)/shard_map/ppermute | solution.py:415
  50.4 6.3 %shard_map.68 = (f32[4,2,128,128]{3,2,1,0:T(8,128)S(1)}, bf16[2,128,128]{2,1,0:T(8,128)(2,1)S(1)}, bf16[5,128,128]{2,1,0:T(8,128)(2,1)S(1)}, bf16[5,128,128]{2,1,0:T(8,128)(2,1)S(1)}) custom-call(s32[1]{0:T(128)} %bitcast.band_ref, f32[128]{0:T(128)S(1)} %copy-done.3, s32[32]{0:T(128)S(1)} %copy-done.4, ...), custom_call_target="tpu_custom_call" | custom-call | flops 1000 | bytes 1000 | tf_op jit(solution)/shard_map/pallas_call | solution.py:404
  56.8 0.7 copy-done.6
  57.5 2.4 %shard_map.69.part_ref = bf16[8,80,128]{2,1,0:T(8,128)(2,1)S(1)} custom-call(s32[1]{0:T(128)} %bitcast.band_ref, s32[1]{0:T(128)} %bitcast.1.sector_ref, f32[128]{0:T(128)S(1)} %copy-done.3, bf16[8,192,128]{2,1,0:T(8,128)(2,1)S(1)} %all-to-all-done.in_ref), custom_call_target="tpu_custom_call" | custom-call | flops 5000000000 | bytes 1000000 | tf_op jit(solution)/shard_map/pallas_call | solution.py:419
  59.9 0.0 copy-start.7
  59.9 0.0 copy-start.5
  59.9 0.0 copy-start.9
  59.9 3.2 %shard_map.70 = bf16[16,80,128]{2,1,0:T(8,128)(2,1)} custom-call(s32[1]{0:T(128)} %bitcast.band_ref, s32[1]{0:T(128)} %bitcast.1.sector_ref, f32[128]{0:T(128)S(1)} %copy-done.3, bf16[8,192,128]{2,1,0:T(8,128)(2,1)S(1)} %all-to-all-done.in_ref, bf16[8,64,128]{2,1,0:T(8,128)(2,1)S(1)} %collective-permute-done.14.far_ref, ...), custom_call_target="tpu_custom_call" | custom-call | flops 3000000000 | bytes 1000000 | tf_op jit(solution)/shard_map/pallas_call | solution.py:422
  63.1 4.3 %all-to-all-start.1 = ((bf16[16,80,128]{2,1,0:T(8,128)(2,1)}), bf16[16,80,128]{2,1,0:T(8,128)(2,1)S(1)}, u32[]{:S(2)}, u32[]{:S(2)}) async-start(bf16[16,80,128]{2,1,0:T(8,128)(2,1)} %shard_map.70), calls=%async_computation.1 | async-start | bytes 655360 | tf_op jit(solution)/shard_map/all_to_all | solution.py:426
  67.4 0.7 collective-permute-start.15
  68.0 1.3 %collective-permute-start.16 = (bf16[5,128,128]{2,1,0:T(8,128)(2,1)S(1)}, bf16[5,128,128]{2,1,0:T(8,128)(2,1)S(1)}, u32[]{:S(2)}, u32[]{:S(2)}) collective-permute-start(bf16[5,128,128]{2,1,0:T(8,128)(2,1)S(1)} %copy-done.7), channel_id=1, source_target_pairs={{0,16},{16,0},{32,48},{48,32},{64,80},{80,64},{96,112},{112,96},{1... | collective-permute-start | bytes 491528 | tf_op jit(solution)/shard_map/ppermute | solution.py:413
  69.3 1.0 %collective-permute-done.16.ry_ref = bf16[5,128,128]{2,1,0:T(8,128)(2,1)S(1)} collective-permute-done((bf16[5,128,128]{2,1,0:T(8,128)(2,1)S(1)}, bf16[5,128,128]{2,1,0:T(8,128)(2,1)S(1)}, u32[]{:S(2)}, u32[]{:S(2)}) %collective-permute-start.16) | collective-permute-done | bytes 163872 | tf_op jit(solution)/shard_map/ppermute | solution.py:413
  70.4 9.1 %all-to-all-done.1.p1_ref = bf16[16,80,128]{2,1,0:T(8,128)(2,1)S(1)} async-done(((bf16[16,80,128]{2,1,0:T(8,128)(2,1)}), bf16[16,80,128]{2,1,0:T(8,128)(2,1)S(1)}, u32[]{:S(2)}, u32[]{:S(2)}) %all-to-all-start.1) | async-done | bytes 327712 | tf_op jit(solution)/shard_map/all_to_all | solution.py:426
  79.4 1.6 %collective-permute-done.17.p2_ref = bf16[16,80,128]{2,1,0:T(8,128)(2,1)S(1)} collective-permute-done((bf16[16,80,128]{2,1,0:T(8,128)(2,1)S(1)}, bf16[16,80,128]{2,1,0:T(8,128)(2,1)S(1)}, u32[]{:S(2)}, u32[]{:S(2)}) %collective-permute-start.17) | collective-permute-done | bytes 327712 | tf_op jit(solution)/shard_map/ppermute | solution.py:429
  81.1 2.3 %shard_map.71 = bf16[2,128,512]{2,1,0:T(8,128)(2,1)} custom-call(s32[1]{0:T(128)} %bitcast.band_ref, f32[4,2,128,128]{3,2,1,0:T(8,128)S(1)} %get-tuple-element.49.o_ref, bf16[2,128,128]{2,1,0:T(8,128)(2,1)S(1)} %copy-done.11, bf16[5,128,128]{2,1,0:T(8,128)(2,1)S(1)} %collective-permute-done.15.rx_ref, ...), custom_call_target="tpu_custom_call" | custom-call | flops 1000000000 | bytes 3000000 | tf_op jit(solution)/shard_map/pallas_call | solution.py:431
  (27 shorter events, 0.1 us)
Async XLA Ops:
  0.0 10.6 %collective-permute-start = (bf16[2,128,512]{2,1,0:T(8,128)(2,1)}, bf16[2,128,512]{2,1,0:T(8,128)(2,1)S(1)}, u32[]{:S(2)}, u32[]{:S(2)}) collective-permute-start(bf16[2,128,512]{2,1,0:T(8,128)(2,1)} %f_ref.5), channel_id=1, source_target_pairs={{16,32},{32,16},{48,64},{64,48},{80,96},{96,80},{112,128},{128,112... | collective-permute-start | bytes 786440 | tf_op jit(solution)/shard_map/ppermute | solution.py:363
  0.7 9.9 %collective-permute-start.1 = (bf16[2,128,512]{2,1,0:T(8,128)(2,1)}, bf16[2,128,512]{2,1,0:T(8,128)(2,1)S(1)}, u32[]{:S(2)}, u32[]{:S(2)}) collective-permute-start(bf16[2,128,512]{2,1,0:T(8,128)(2,1)} %f_ref.5), channel_id=1, source_target_pairs={{0,16},{16,0},{32,48},{48,32},{64,80},{80,64},{96,112},{112,96},{1... | collective-permute-start | bytes 786440 | tf_op jit(solution)/shard_map/ppermute | solution.py:364
  3.6 0.9 %copy-start.1 = (bf16[2,128,512]{2,1,0:T(8,128)(2,1)S(1)}, bf16[2,128,512]{2,1,0:T(8,128)(2,1)}, u32[]{:S(2)}) copy-start(bf16[2,128,512]{2,1,0:T(8,128)(2,1)} %f_ref.5) | copy-start | bytes 786436
  4.5 2.2 %copy-start = (bf16[1536,1024]{1,0:T(8,128)(2,1)S(1)}, bf16[1536,1024]{1,0:T(8,128)(2,1)}, u32[]{:S(2)}) copy-start(bf16[1536,1024]{1,0:T(8,128)(2,1)} %w_ref.3) | copy-start | bytes 9437188
  4.6 2.2 %copy-start.2 = (bf16[512,512]{1,0:T(8,128)(2,1)S(1)}, bf16[512,512]{1,0:T(8,128)(2,1)}, u32[]{:S(2)}) copy-start(bf16[512,512]{1,0:T(8,128)(2,1)} %wq_ref.1) | copy-start | bytes 1572868
  4.7 5.9 %copy-start.3 = (f32[128]{0:T(128)S(1)}, f32[128]{0:T(128)}, u32[]{:S(2)}) copy-start(f32[128]{0:T(128)} %constant.39.clone.table_ref) | copy-start | bytes 1540
  4.7 4.0 %collective-permute-start.2 = (bf16[2,16,512]{2,1,0:T(8,128)(2,1)S(1)}, bf16[2,16,512]{2,1,0:T(8,128)(2,1)S(1)}, u32[]{:S(2)}, u32[]{:S(2)}) collective-permute-start(bf16[2,16,512]{2,1,0:T(8,128)(2,1)S(1)} %get-tuple-element.32), channel_id=1, source_target_pairs={{0,1},{1,2},{2,3},{3,4},{4,5},{5,6},{6,7},{7,8},{8,9},{9,10},{10,1... | collective-permute-start | bytes 98312 | tf_op jit(solution)/shard_map/ppermute | solution.py:365
  6.7 3.9 %collective-permute-start.3 = (bf16[2,16,512]{2,1,0:T(8,128)(2,1)S(1)}, bf16[2,16,512]{2,1,0:T(8,128)(2,1)S(1)}, u32[]{:S(2)}, u32[]{:S(2)}) collective-permute-start(bf16[2,16,512]{2,1,0:T(8,128)(2,1)S(1)} %get-tuple-element.33), channel_id=1, source_target_pairs={{0,15},{1,0},{2,1},{3,2},{4,3},{5,4},{6,5},{7,6},{8,7},{9,8},{10,9... | collective-permute-start | bytes 98312 | tf_op jit(solution)/shard_map/ppermute | solution.py:366
  12.9 37.6 %copy-start.4 = (s32[32]{0:T(128)S(1)}, s32[32]{0:T(128)}, u32[]{:S(2)}) copy-start(s32[32]{0:T(128)} %width_ref.1) | copy-start | bytes 388
  12.9 1.8 %collective-permute-start.4 = (bf16[8,192,128]{2,1,0:T(8,128)(2,1)S(1)}, bf16[8,192,128]{2,1,0:T(8,128)(2,1)S(1)}, u32[]{:S(2)}, u32[]{:S(2)}) collective-permute-start(bf16[8,192,128]{2,1,0:T(8,128)(2,1)S(1)} %get-tuple-element.39), channel_id=1, source_target_pairs={{0,16},{16,0},{32,48},{48,32},{64,80},{80,64},{96,112},{112,96},{1... | collective-permute-start | bytes 1179656 | tf_op jit(solution)/shard_map/ppermute | solution.py:382
  15.5 21.7 %collective-permute-start.5 = (bf16[8,128,128]{2,1,0:T(8,128)(2,1)S(1)}, bf16[8,128,128]{2,1,0:T(8,128)(2,1)S(1)}, u32[]{:S(2)}, u32[]{:S(2)}) collective-permute-start(bf16[8,128,128]{2,1,0:T(8,128)(2,1)S(1)} %get-tuple-element.40), channel_id=1, source_target_pairs={{0,192},{240,48},{1,193},{241,49},{2,194},{242,50},{3,195},{243,51... | collective-permute-start | bytes 786440 | tf_op jit(solution)/shard_map/ppermute | solution.py:397
  22.8 14.4 %collective-permute-start.6 = (bf16[8,128,128]{2,1,0:T(8,128)(2,1)S(1)}, bf16[8,128,128]{2,1,0:T(8,128)(2,1)S(1)}, u32[]{:S(2)}, u32[]{:S(2)}) collective-permute-start(bf16[8,128,128]{2,1,0:T(8,128)(2,1)S(1)} %get-tuple-element.40), channel_id=1, source_target_pairs={{0,128},{240,112},{1,129},{241,113},{2,130},{242,114},{3,131},{243... | collective-permute-start | bytes 786440 | tf_op jit(solution)/shard_map/ppermute | solution.py:397
  24.1 13.1 %collective-permute-start.7 = (bf16[8,128,128]{2,1,0:T(8,128)(2,1)S(1)}, bf16[8,128,128]{2,1,0:T(8,128)(2,1)S(1)}, u32[]{:S(2)}, u32[]{:S(2)}) collective-permute-start(bf16[8,128,128]{2,1,0:T(8,128)(2,1)S(1)} %get-tuple-element.40), channel_id=1, source_target_pairs={{0,64},{240,176},{1,65},{241,177},{2,66},{242,178},{3,67},{243,179... | collective-permute-start | bytes 786440 | tf_op jit(solution)/shard_map/ppermute | solution.py:397
  25.4 17.1 %collective-permute-start.10 = (bf16[2,8,128,128]{3,2,1,0:T(8,128)(2,1)S(1)}, bf16[2,8,128,128]{3,2,1,0:T(8,128)(2,1)S(1)}, u32[]{:S(2)}, u32[]{:S(2)}) collective-permute-start(bf16[2,8,128,128]{3,2,1,0:T(8,128)(2,1)S(1)} %get-tuple-element.41.kv_ref), channel_id=1, source_target_pairs={{0,15},{1,0},{2,1},{3,2},{4,3},{5,4},{6,5},{7,6},{8,7},{9,8},{10,9... | collective-permute-start | bytes 1572872 | tf_op jit(solution)/shard_map/ppermute | solution.py:390
  28.3 14.3 %collective-permute-start.9 = (bf16[2,8,128,128]{3,2,1,0:T(8,128)(2,1)S(1)}, bf16[2,8,128,128]{3,2,1,0:T(8,128)(2,1)S(1)}, u32[]{:S(2)}, u32[]{:S(2)}) collective-permute-start(bf16[2,8,128,128]{3,2,1,0:T(8,128)(2,1)S(1)} %get-tuple-element.41.kv_ref), channel_id=1, source_target_pairs={{0,1},{1,2},{2,3},{3,4},{4,5},{5,6},{6,7},{7,8},{8,9},{9,10},{10,1... | collective-permute-start | bytes 1572872 | tf_op jit(solution)/shard_map/ppermute | solution.py:389
  28.6 20.0 %all-to-all-start = ((bf16[8,192,128]{2,1,0:T(8,128)(2,1)}), bf16[8,192,128]{2,1,0:T(8,128)(2,1)S(1)}, u32[]{:S(2)}, u32[]{:S(2)}) async-start(bf16[8,192,128]{2,1,0:T(8,128)(2,1)} %shard_map.67), calls=%async_computation | async-start | bytes 786432 | tf_op jit(solution)/shard_map/all_to_all | solution.py:386
  37.3 5.2 %collective-permute-start.8 = (bf16[8,128,128]{2,1,0:T(8,128)(2,1)S(1)}, bf16[8,128,128]{2,1,0:T(8,128)(2,1)S(1)}, u32[]{:S(2)}, u32[]{:S(2)}) collective-permute-start(bf16[8,128,128]{2,1,0:T(8,128)(2,1)S(1)} %select_select_fusion), channel_id=1, source_target_pairs={{0,32},{64,96},{128,160},{192,224},{48,16},{112,80},{176,144},{240... | collective-permute-start | bytes 786440 | tf_op jit(solution)/shard_map/ppermute | solution.py:399
  38.6 3.9 %collective-permute-start.11 = (bf16[4,128,128]{2,1,0:T(8,128)(2,1)S(1)}, bf16[4,128,128]{2,1,0:T(8,128)(2,1)S(1)}, u32[]{:S(2)}, u32[]{:S(2)}) collective-permute-start(bf16[4,128,128]{2,1,0:T(8,128)(2,1)S(1)} %get-tuple-element.42.qx_ref), channel_id=1, source_target_pairs={{16,32},{32,16},{48,64},{64,48},{80,96},{96,80},{112,128},{128,112... | collective-permute-start | bytes 393224 | tf_op jit(solution)/shard_map/ppermute | solution.py:391
  39.3 3.2 %collective-permute-start.12 = (bf16[4,128,128]{2,1,0:T(8,128)(2,1)S(1)}, bf16[4,128,128]{2,1,0:T(8,128)(2,1)S(1)}, u32[]{:S(2)}, u32[]{:S(2)}) collective-permute-start(bf16[4,128,128]{2,1,0:T(8,128)(2,1)S(1)} %get-tuple-element.43.qy_ref), channel_id=1, source_target_pairs={{0,16},{16,0},{32,48},{48,32},{64,80},{80,64},{96,112},{112,96},{1... | collective-permute-start | bytes 393224 | tf_op jit(solution)/shard_map/ppermute | solution.py:392
  48.6 1.8 %collective-permute-start.13 = (bf16[8,128,128]{2,1,0:T(8,128)(2,1)S(1)}, bf16[8,128,128]{2,1,0:T(8,128)(2,1)S(1)}, u32[]{:S(2)}, u32[]{:S(2)}) collective-permute-start(bf16[8,128,128]{2,1,0:T(8,128)(2,1)S(1)} %broadcast_select_fusion.p1_ref), channel_id=1, source_target_pairs={{0,16},{16,0},{32,48},{48,32},{64,80},{80,64},{96,112},{112,96},{1... | collective-permute-start | bytes 786440 | tf_op jit(solution)/shard_map/ppermute | solution.py:402
  48.6 11.3 %collective-permute-start.14 = (bf16[8,64,128]{2,1,0:T(8,128)(2,1)S(1)}, bf16[8,64,128]{2,1,0:T(8,128)(2,1)S(1)}, u32[]{:S(2)}, u32[]{:S(2)}) collective-permute-start(bf16[8,64,128]{2,1,0:T(8,128)(2,1)S(1)} %slice.3), channel_id=1, source_target_pairs={{0,8},{1,9},{2,10},{3,11},{4,12},{5,13},{6,14},{7,15},{8,0},{9,1},... | collective-permute-start | bytes 393224 | tf_op jit(solution)/shard_map/ppermute | solution.py:415
  56.8 0.7 copy-start.6
  57.5 2.4 %copy-start.8 = (bf16[5,128,128]{2,1,0:T(8,128)(2,1)}, bf16[5,128,128]{2,1,0:T(8,128)(2,1)S(1)}, u32[]{:S(2)}) copy-start(bf16[5,128,128]{2,1,0:T(8,128)(2,1)S(1)} %get-tuple-element.54) | copy-start | bytes 491524
  57.5 2.4 %copy-start.10 = (bf16[2,128,128]{2,1,0:T(8,128)(2,1)}, bf16[2,128,128]{2,1,0:T(8,128)(2,1)S(1)}, u32[]{:S(2)}) copy-start(bf16[2,128,128]{2,1,0:T(8,128)(2,1)S(1)} %get-tuple-element.52.st_ref) | copy-start | bytes 196612
  59.9 8.2 %copy-start.7 = (bf16[5,128,128]{2,1,0:T(8,128)(2,1)S(1)}, bf16[5,128,128]{2,1,0:T(8,128)(2,1)}, u32[]{:S(2)}) copy-start(bf16[5,128,128]{2,1,0:T(8,128)(2,1)} %copy-done.6) | copy-start | bytes 491524
  59.9 21.2 %copy-start.5 = (bf16[512,512]{1,0:T(8,128)(2,1)S(1)}, bf16[512,512]{1,0:T(8,128)(2,1)}, u32[]{:S(2)}) copy-start(bf16[512,512]{1,0:T(8,128)(2,1)} %wo_ref.1) | copy-start | bytes 1572868
  59.9 7.4 %copy-start.9 = (bf16[5,128,128]{2,1,0:T(8,128)(2,1)S(1)}, bf16[5,128,128]{2,1,0:T(8,128)(2,1)}, u32[]{:S(2)}) copy-start(bf16[5,128,128]{2,1,0:T(8,128)(2,1)} %copy-done.8) | copy-start | bytes 491524
  59.9 21.1 %copy-start.11 = (bf16[2,128,128]{2,1,0:T(8,128)(2,1)S(1)}, bf16[2,128,128]{2,1,0:T(8,128)(2,1)}, u32[]{:S(2)}) copy-start(bf16[2,128,128]{2,1,0:T(8,128)(2,1)} %copy-done.10) | copy-start | bytes 196612
  63.1 16.3 %all-to-all-start.1 = ((bf16[16,80,128]{2,1,0:T(8,128)(2,1)}), bf16[16,80,128]{2,1,0:T(8,128)(2,1)S(1)}, u32[]{:S(2)}, u32[]{:S(2)}) async-start(bf16[16,80,128]{2,1,0:T(8,128)(2,1)} %shard_map.70), calls=%async_computation.1 | async-start | bytes 655360 | tf_op jit(solution)/shard_map/all_to_all | solution.py:426
  67.4 2.0 %collective-permute-start.15 = (bf16[5,128,128]{2,1,0:T(8,128)(2,1)S(1)}, bf16[5,128,128]{2,1,0:T(8,128)(2,1)S(1)}, u32[]{:S(2)}, u32[]{:S(2)}) collective-permute-start(bf16[5,128,128]{2,1,0:T(8,128)(2,1)S(1)} %copy-done.9), channel_id=1, source_target_pairs={{16,32},{32,16},{48,64},{64,48},{80,96},{96,80},{112,128},{128,112... | collective-permute-start | bytes 491528 | tf_op jit(solution)/shard_map/ppermute | solution.py:412
  68.0 2.3 %collective-permute-start.16 = (bf16[5,128,128]{2,1,0:T(8,128)(2,1)S(1)}, bf16[5,128,128]{2,1,0:T(8,128)(2,1)S(1)}, u32[]{:S(2)}, u32[]{:S(2)}) collective-permute-start(bf16[5,128,128]{2,1,0:T(8,128)(2,1)S(1)} %copy-done.7), channel_id=1, source_target_pairs={{0,16},{16,0},{32,48},{48,32},{64,80},{80,64},{96,112},{112,96},{1... | collective-permute-start | bytes 491528 | tf_op jit(solution)/shard_map/ppermute | solution.py:413
  79.4 1.6 %collective-permute-start.17 = (bf16[16,80,128]{2,1,0:T(8,128)(2,1)S(1)}, bf16[16,80,128]{2,1,0:T(8,128)(2,1)S(1)}, u32[]{:S(2)}, u32[]{:S(2)}) collective-permute-start(bf16[16,80,128]{2,1,0:T(8,128)(2,1)S(1)} %all-to-all-done.1.p1_ref), channel_id=1, source_target_pairs={{0,16},{16,0},{32,48},{48,32},{64,80},{80,64},{96,112},{112,96},{1... | collective-permute-start | bytes 983048 | tf_op jit(solution)/shard_map/ppermute | solution.py:429

commit v5 on v4

--- a/solution.py
+++ b/solution.py
@@ -15,7 +15,6 @@
 F32 = jnp.float32
 BF16 = jnp.bfloat16
 VMEM = pl.BlockSpec(memory_space=pltpu.VMEM)
-HBM = pl.BlockSpec(memory_space=pltpu.HBM)
 SMEM = pl.BlockSpec(memory_space=pltpu.SMEM)
 PARAMS = pltpu.CompilerParams(vmem_limit_bytes=20 * 1024 * 1024)
 
@@ -40,18 +39,6 @@
     return (band == 0) | (band == NLAT // 2 - 1)
 
 
-def start_all(pairs, sems):
-    copies = [pltpu.make_async_copy(src, dst, sems.at[i]) for i, (src, dst) in enumerate(pairs)]
-    for c in copies:
-        c.start()
-    return copies
-
-
-def wait_all(copies):
-    for c in copies:
-        c.wait()
-
-
 def lane_ids(shape):
     return lax.broadcasted_iota(jnp.int32, shape, len(shape) - 1)
 
@@ -80,18 +67,18 @@
     return a.astype(F32), b.astype(F32), c.astype(F32)
 
 
-def edge_kernel(band_ref, f_ref, last_ref, lead_ref, sems):
+def edge_kernel(band_ref, f_ref, fx_ref, fy_ref, last_ref, lead_ref):
     odd = band_ref[0] % 2
-    pairs = []
-    for slot, row in ((0, f_ref.at[odd]), (1, f_ref.at[1 - odd])):
-        pairs += [(row.at[pl.ds(112, 16)], last_ref.at[slot]), (row.at[pl.ds(0, 16)], lead_ref.at[slot])]
-    wait_all(start_all(pairs, sems))
-
-
-def early_kernel(band_ref, f_ref, wq_ref, w_ref, qx_ref, qy_ref, pq_ref, base_ref):
-    odd = band_ref[0] % 2
+    for slot, out_ref in ((0, fx_ref), (1, fy_ref)):
+        f = f_ref[odd if slot == 0 else 1 - odd]
+        out_ref[...] = f
+        last_ref[slot] = f[112:]
+        lead_ref[slot] = f[:16]
+
+
+def early_kernel(fx_ref, fy_ref, wq_ref, w_ref, qx_ref, qy_ref, pq_ref, base_ref):
     low = lane_ids((64, LANES)) < HDIM
-    f = jnp.concatenate([f_ref[odd], f_ref[1 - odd]], axis=0)
+    f = jnp.concatenate([fx_ref[...], fy_ref[...]], axis=0)
     q = dot_nn(f, wq_ref[...]).astype(BF16).astype(F32) * HDIM ** -0.5
     for p in range(PAIRS):
         block = q[:, p * LANES : (p + 1) * LANES]
@@ -104,16 +91,14 @@
 
 
 def keyval_kernel(
-    band_ref, table_ref, f_ref, outer_ref, inner_ref, west_ref, east_ref, pq_ref, base_ref, w_ref,
+    band_ref, table_ref, fx_ref, fy_ref, outer_ref, inner_ref, west_ref, east_ref, pq_ref, base_ref, w_ref,
     kv_ref, kvx_ref, mine_ref, swap_ref,
 ):
     band = band_ref[0]
-    odd = band % 2
     coef = [table_ref[8 * band + i] for i in range(4)]
     for ref in (mine_ref, swap_ref):
         ref[:, 128:] = pq_ref[...]
-    own = [f_ref[odd], f_ref[1 - odd]]
-    rows = [outer_ref[1 - odd].astype(F32), own[0].astype(F32), own[1].astype(F32), inner_ref[odd].astype(F32)]
+    rows = [ref[...].astype(F32) for ref in (outer_ref, fx_ref, fy_ref, inner_ref)]
     cell = lax.broadcasted_iota(jnp.int32, (128, 512), 0)
     lat, lon = [], []
     for r in range(2):
@@ -272,57 +257,66 @@
         out_ref[base + b, 64:] = dot_nt(pick, stats.astype(BF16)).astype(BF16)
 
 
-def final_kernel(band_ref, o_ref, st_ref, rx_ref, ry_ref, p1_ref, p2_ref, wo_ref, out_ref, att):
-    odd = band_ref[0] % 2
-    polar = is_polar(band_ref[0])
+def head_pick():
     src = lax.broadcasted_iota(jnp.int32, (LANES, 512), 0) // 3
     dst = lax.broadcasted_iota(jnp.int32, (LANES, 512), 1)
     head = 2 * (dst // LANES) + jnp.where(dst % LANES < HDIM, 1, 0)
-    pick = jnp.where(src == head, 1.0, 0.0).astype(BF16)
+    return jnp.where(src == head, 1.0, 0.0).astype(BF16)
+
+
+def turned_weights(wo_ref):
+    order = []
+    for p in range(PAIRS):
+        order += [wo_ref[p * LANES + HDIM : (p + 1) * LANES], wo_ref[p * LANES : p * LANES + HDIM]]
+    return jnp.concatenate(order, axis=0)
+
+
+def merge_kernel(band_ref, o_ref, st_ref, rx_ref, ry_ref, wo_ref, out_ref, att):
+    odd = band_ref[0] % 2
+    pick = head_pick()
     for r, ret in ((0, rx_ref), (1, ry_ref)):
         lse = dot_nn(st_ref[r], pick)
         lse_ret = dot_nn(ret[PAIRS], pick)
-        mine = jnp.concatenate([o_ref[p, r] for p in range(PAIRS)], axis=1).astype(F32)
+        mine = jnp.concatenate([o_ref[p, r] for p in range(PAIRS)], axis=1)
         other = jnp.concatenate([ret[p] for p in range(PAIRS)], axis=1).astype(F32)
-        if r == 0:
-            lse_ret = jnp.where(polar, MASKED, lse_ret)
-            other = jnp.where(polar, 0.0, other)
         top = jnp.maximum(lse, lse_ret)
         wa = jnp.exp(lse - top)
         wb = jnp.exp(lse_ret - top)
         att[r * 128 : (r + 1) * 128] = ((mine * wa + other * wb) / (wa + wb)).astype(BF16)
-        if r == 0:
-
-            @pl.when(polar)
-            def _():
-                low = lane_ids((64, LANES)) < HDIM
-                row = lax.broadcasted_iota(jnp.int32, (16, LANES), 0)
-                col = lane_ids((16, LANES))
-                pick_even = jnp.where((row < 3) & (col >= HDIM), 1.0, 0.0).astype(BF16)
-                pick_odd = jnp.where((row < 3) & (col < HDIM), 1.0, 0.0).astype(BF16)
-                for p in range(PAIRS):
-                    ml = lse[:, p * LANES : (p + 1) * LANES]
-                    vals, logs = [], []
-                    for ref, h in ((p1_ref, 2 * p), (p1_ref, 8 + 2 * p), (p2_ref, 2 * p), (p2_ref, 8 + 2 * p)):
-                        even32, odd32 = ref[h, :64].astype(F32), ref[h + 1, :64].astype(F32)
-                        first = jnp.where(low, odd32, half_turn(even32))
-                        second = jnp.where(low, half_turn(odd32), even32)
-                        vals.append(jnp.concatenate([first, second], axis=0))
-                        logs.append(dot_tn(ref[h, 64:], pick_even) + dot_tn(ref[h + 1, 64:], pick_odd))
-                    vals.append(o_ref[p, 0].astype(F32))
-                    logs.append(ml)
-                    best = jnp.maximum(ml, jnp.maximum(jnp.maximum(logs[0], logs[1]), jnp.maximum(logs[2], logs[3])))
-                    scales = [jnp.exp(x - best) for x in logs]
-                    merged = sum(v * w for v, w in zip(vals, scales)) / sum(scales)
-                    att[:128, p * LANES : (p + 1) * LANES] = merged.astype(BF16)
-
-    order = []
-    for p in range(PAIRS):
-        order += [wo_ref[p * LANES + HDIM : (p + 1) * LANES], wo_ref[p * LANES : p * LANES + HDIM]]
-    w = jnp.concatenate(order, axis=0)
-    out = dot_nn(att[...], w).astype(BF16)
+    out = dot_nn(att[...], turned_weights(wo_ref)).astype(BF16)
     out_ref[odd] = out[:128]
     out_ref[1 - odd] = out[128:]
+
+
+def polar_row_kernel(band_ref, o_ref, st_ref, p1_ref, p2_ref, wo_ref, old_ref, out_ref, att, row_ref, sem):
+    odd = band_ref[0] % 2
+
+    @pl.when(is_polar(band_ref[0]))
+    def _():
+        lse = dot_nn(st_ref[0], head_pick())
+        low = lane_ids((64, LANES)) < HDIM
+        row = lax.broadcasted_iota(jnp.int32, (16, LANES), 0)
+        col = lane_ids((16, LANES))
+        pick_even = jnp.where((row < 3) & (col >= HDIM), 1.0, 0.0).astype(BF16)
+        pick_odd = jnp.where((row < 3) & (col < HDIM), 1.0, 0.0).astype(BF16)
+        for p in range(PAIRS):
+            vals, logs = [o_ref[p, 0]], [lse[:, p * LANES : (p + 1) * LANES]]
+            for ref, h in ((p1_ref, 2 * p), (p1_ref, 8 + 2 * p), (p2_ref, 2 * p), (p2_ref, 8 + 2 * p)):
+                even32, odd32 = ref[h, :64].astype(F32), ref[h + 1, :64].astype(F32)
+                first = jnp.where(low, odd32, half_turn(even32))
+                second = jnp.where(low, half_turn(odd32), even32)
+                vals.append(jnp.concatenate([first, second], axis=0))
+                logs.append(dot_tn(ref[h, 64:], pick_even) + dot_tn(ref[h + 1, 64:], pick_odd))
+            best = logs[0]
+            for x in logs[1:]:
+                best = jnp.maximum(best, x)
+            scales = [jnp.exp(x - best) for x in logs]
+            merged = sum(v * w for v, w in zip(vals, scales)) / sum(scales)
+            att[:, p * LANES : (p + 1) * LANES] = merged.astype(BF16)
+        row_ref[...] = dot_nn(att[...], turned_weights(wo_ref)).astype(BF16)
+        copy = pltpu.make_async_copy(row_ref, out_ref.at[odd], sem)
+        copy.start()
+        copy.wait()
 
 
 def call(kernel, outs, in_specs, flops, nbytes, scratch=(), out_specs=None):
@@ -356,28 +350,29 @@
     outer = [(i, i + 1 if i % 2 else i - 1) for i in range(1, nlat - 1)]
     groups = [list(range(8)), list(range(8, 16))]
 
-    last, lead = call(
-        edge_kernel, (sds((2, 16, 512)), sds((2, 16, 512))), [SMEM, HBM], 8_000_000_000, 100_000,
-        [pltpu.SemaphoreType.DMA((4,))],
+    fx, fy, last, lead = call(
+        edge_kernel,
+        (sds((128, 512)), sds((128, 512)), sds((2, 16, 512)), sds((2, 16, 512))),
+        [SMEM, VMEM], 8_000_000_000, 100_000,
     )(band, gf)
-    over = lax.ppermute(gf, "lat", outer)
-    beside = lax.ppermute(gf, "lat", inner)
+    over = lax.ppermute(fx, "lat", outer)
+    beside = lax.ppermute(fy, "lat", inner)
     west = lax.ppermute(last, "lon", ring(nlon, 1))
     east = lax.ppermute(lead, "lon", ring(nlon, -1))
     qx, qy, pq, base = call(
         early_kernel,
         (sds((PAIRS, 128, LANES)), sds((PAIRS, 128, LANES)), sds((HEADS, 64, LANES)), sds((256, 1024), F32)),
-        [SMEM, VMEM, VMEM, VMEM],
+        [VMEM] * 4,
         600_000_000, 6_000_000,
-    )(band, gf, wq, wkv)
+    )(fx, fy, wq, wkv)
 
     kv, kvx, mine, swap = call(
         keyval_kernel,
         (sds((2, HEADS, 128, LANES)), sds((HEADS, 128, LANES)),
          sds((HEADS, 192, LANES)), sds((HEADS, 192, LANES))),
-        [SMEM, SMEM] + [VMEM] * 8,
+        [SMEM, SMEM] + [VMEM] * 9,
         1_000_000_000, 4_000_000,
-    )(band, table, gf, over, beside, west, east, pq, base, wkv)
+    )(band, table, fx, fy, over, beside, west, east, pq, base, wkv)
 
     got = lax.ppermute(swap, "lat", inner)
     picked = call(pick_kernel, sds((HEADS, 192, LANES)), [SMEM] + [VMEM] * 2, 1000, 1_000_000)(
@@ -428,10 +423,20 @@
     part, ret_x, ret_y = lax.optimization_barrier((part, ret_x, ret_y))
     part2 = lax.ppermute(part, "lat", inner)
 
-    return call(
-        final_kernel, sds((2, 128, 512)), [SMEM] + [VMEM] * 7,
+    out = call(
+        merge_kernel, sds((2, 128, 512)), [SMEM] + [VMEM] * 5,
         1_000_000_000, 3_000_000, [pltpu.VMEM((256, 512), BF16)],
-    )(band, o, st, ret_x, ret_y, part, part2, wo)
+    )(band, o, st, ret_x, ret_y, wo)
+    return pl.pallas_call(
+        polar_row_kernel,
+        out_shape=sds((2, 128, 512)),
+        in_specs=[SMEM] + [VMEM] * 5 + [pl.BlockSpec(memory_space=pl.ANY)],
+        out_specs=pl.BlockSpec(memory_space=pl.ANY),
+        scratch_shapes=[pltpu.VMEM((128, 512), BF16), pltpu.VMEM((128, 512), BF16), pltpu.SemaphoreType.DMA],
+        input_output_aliases={6: 0},
+        compiler_params=PARAMS,
+        cost_estimate=cost(1_000_000, 1_000_000),
+    )(band, o, st, part, part2, wo, out)
 
 
 def solution(mesh):

time: 84 us -> 83.1 us (0.989)
  waiting for transfers between devices: 25.8 us -> 24.1 us
    ppermute x1, waiting for transfers between devices: 1.63 us -> 0.32 us  [body(): part2 = lax.ppermute(part, 'lat', inner)]
    pallas_call x2 -> x3, Pallas kernels: 2.42 us -> 2.93 us  [the longest x1 1.6 us: body(): pl.pallas_call(polar_row_kernel, out_shape=sds((2, 128, 512)), in_specs=[...]
  transfers between devices with their start and end apart: 20 -> 20, of which waited for: 8 -> 8; matrix products, arithmetic and copies ran while one was open for 0% -> 0% of each run, Pallas kernels for 11% -> 13%
where the time goes in v5:
time: 83.1 us; the launch traced here: 82.7 us
  starting transfers between devices  38 us (46%)
  waiting for transfers between devices  24.1 us (29%)
  Pallas kernels  18.5 us (22%)
  local copies, waits for them, and re-layouts  1.62 us (2%)
    ppermute x3, starting transfers between devices, body(): got = lax.ppermute(kvx, 'lat', [(0, step), (nlat - 1, nlat - 1 - step)])  9.89 us
    all_to_all x1, waiting for transfers between devices, body(): part = lax.all_to_all(part, 'lon', 0, 0)  9.04 us
    all_to_all x1, starting transfers between devices, body(): all_polar = lax.all_to_all(picked, 'lon', 0, 0, axis_index_groups=groups)  8.55 us
    pallas_call x1, Pallas kernels, body(): call(window_kernel, (sds((PAIRS, 2, 128, LANES), F32), sds((2, 128, LANES...  6.34 us
    all_to_all x1, waiting for transfers between devices, body(): all_polar = lax.all_to_all(picked, 'lon', 0, 0, axis_index_groups=groups)  5.66 us
    all_to_all x1, starting transfers between devices, body(): part = lax.all_to_all(part, 'lon', 0, 0)  4.39 us
    pallas_call x1, Pallas kernels, body(): call(polar_far_kernel, sds((16, 80, LANES)), [SMEM, SMEM, SMEM, VMEM, VME...  3.16 us
    ppermute x1, waiting for transfers between devices, body(): lax.ppermute(x, 'lat', [(i, i + 2) for i in range(0, 16, 4)] + [(i, i - 2...  3.07 us
  transfers between devices with their start and end apart: 20, of which 8 were waited for; matrix products, arithmetic and copies ran while one was open for 0% of the time, Pallas kernels for 13%

profile of v5, /device:TPU:32, one launch (start us, length us, event | category | flops | bytes accessed | tf_op | source)
XLA Modules:
  0.0 82.7 jit_solution(3401393177852085578)
XLA Ops:
  0.0 0.9 %copy-done.7 = bf16[2,128,512]{2,1,0:T(8,128)(2,1)S(1)} copy-done((bf16[2,128,512]{2,1,0:T(8,128)(2,1)S(1)}, bf16[2,128,512]{2,1,0:T(8,128)(2,1)}, u32[]{:S(2)}) %copy-start.7) | copy-done | bytes 262168
  1.0 0.0 copy-start.5
  1.0 0.8 collective-permute-start
  1.8 3.1 %collective-permute-start.1 = (bf16[128,512]{1,0:T(8,128)(2,1)S(1)}, bf16[128,512]{1,0:T(8,128)(2,1)S(1)}, u32[]{:S(2)}, u32[]{:S(2)}) collective-permute-start(bf16[128,512]{1,0:T(8,128)(2,1)S(1)} %get-tuple-element.35.fy_ref), channel_id=1, source_target_pairs={{0,16},{16,0},{32,48},{48,32},{64,80},{80,64},{96,112},{112,96},{1... | collective-permute-start | bytes 393224 | tf_op jit(solution)/shard_map/ppermute | solution.py:359
  4.9 1.9 %collective-permute-start.2 = (bf16[2,16,512]{2,1,0:T(8,128)(2,1)S(1)}, bf16[2,16,512]{2,1,0:T(8,128)(2,1)S(1)}, u32[]{:S(2)}, u32[]{:S(2)}) collective-permute-start(bf16[2,16,512]{2,1,0:T(8,128)(2,1)S(1)} %get-tuple-element.36), channel_id=1, source_target_pairs={{0,1},{1,2},{2,3},{3,4},{4,5},{5,6},{6,7},{7,8},{8,9},{9,10},{10,1... | collective-permute-start | bytes 98312 | tf_op jit(solution)/shard_map/ppermute | solution.py:360
  6.8 0.1 collective-permute-start.3
  6.9 0.6 shard_map.65
  7.5 1.3 %collective-permute-done.2.west_ref = bf16[2,16,512]{2,1,0:T(8,128)(2,1)S(1)} collective-permute-done((bf16[2,16,512]{2,1,0:T(8,128)(2,1)S(1)}, bf16[2,16,512]{2,1,0:T(8,128)(2,1)S(1)}, u32[]{:S(2)}, u32[]{:S(2)}) %collective-permute-start.2) | collective-permute-done | bytes 32800 | tf_op jit(solution)/shard_map/ppermute | solution.py:360
  8.8 1.9 %collective-permute-done.3.east_ref = bf16[2,16,512]{2,1,0:T(8,128)(2,1)S(1)} collective-permute-done((bf16[2,16,512]{2,1,0:T(8,128)(2,1)S(1)}, bf16[2,16,512]{2,1,0:T(8,128)(2,1)S(1)}, u32[]{:S(2)}, u32[]{:S(2)}) %collective-permute-start.3) | collective-permute-done | bytes 32800 | tf_op jit(solution)/shard_map/ppermute | solution.py:361
  10.7 0.0 collective-permute-done.outer_ref
  10.7 0.0 collective-permute-done.1.inner_ref
  10.7 2.2 %shard_map.66 = (bf16[2,8,128,128]{3,2,1,0:T(8,128)(2,1)S(1)}, bf16[8,128,128]{2,1,0:T(8,128)(2,1)S(1)}, bf16[8,192,128]{2,1,0:T(8,128)(2,1)S(1)}, bf16[8,192,128]{2,1,0:T(8,128)(2,1)S(1)}) custom-call(s32[1]{0:T(128)} %bitcast.band_ref, f32[128]{0:T(128)S(1)} %copy-done.5, bf16[128,512]{1,0:T(8,128)(2,1)S(1)} %get-tuple-element.34.fx_ref, ...), custom_call_target="tpu_custom_call" | custom-call | flops 1000000000 | bytes 4000000 | tf_op jit(solution)/shard_map/pallas_call | solution.py:369
  12.9 0.0 copy-start.6
  13.0 0.1 collective-permute-start.4
  13.1 1.7 %collective-permute-done.4.got_ref = bf16[8,192,128]{2,1,0:T(8,128)(2,1)S(1)} collective-permute-done((bf16[8,192,128]{2,1,0:T(8,128)(2,1)S(1)}, bf16[8,192,128]{2,1,0:T(8,128)(2,1)S(1)}, u32[]{:S(2)}, u32[]{:S(2)}) %collective-permute-start.4) | collective-permute-done | bytes 393248 | tf_op jit(solution)/shard_map/ppermute | solution.py:377
  14.8 0.8 %shard_map.67 = bf16[8,192,128]{2,1,0:T(8,128)(2,1)} custom-call(s32[1]{0:T(128)} %bitcast.band_ref, bf16[8,192,128]{2,1,0:T(8,128)(2,1)S(1)} %get-tuple-element.42.own_ref, bf16[8,192,128]{2,1,0:T(8,128)(2,1)S(1)} %collective-permute-done.4.got_ref), custom_call_target="tpu_custom_call" | custom-call | flops 1000 | bytes 1000000 | tf_op jit(solution)/shard_map/pallas_call | solution.py:378
  15.6 7.3 %collective-permute-start.5 = (bf16[8,128,128]{2,1,0:T(8,128)(2,1)S(1)}, bf16[8,128,128]{2,1,0:T(8,128)(2,1)S(1)}, u32[]{:S(2)}, u32[]{:S(2)}) collective-permute-start(bf16[8,128,128]{2,1,0:T(8,128)(2,1)S(1)} %get-tuple-element.44), channel_id=1, source_target_pairs={{0,192},{240,48},{1,193},{241,49},{2,194},{242,50},{3,195},{243,51... | collective-permute-start | bytes 786440 | tf_op jit(solution)/shard_map/ppermute | solution.py:392
  22.9 1.3 %collective-permute-start.6 = (bf16[8,128,128]{2,1,0:T(8,128)(2,1)S(1)}, bf16[8,128,128]{2,1,0:T(8,128)(2,1)S(1)}, u32[]{:S(2)}, u32[]{:S(2)}) collective-permute-start(bf16[8,128,128]{2,1,0:T(8,128)(2,1)S(1)} %get-tuple-element.44), channel_id=1, source_target_pairs={{0,128},{240,112},{1,129},{241,113},{2,130},{242,114},{3,131},{243... | collective-permute-start | bytes 786440 | tf_op jit(solution)/shard_map/ppermute | solution.py:392
  24.2 1.3 %collective-permute-start.7 = (bf16[8,128,128]{2,1,0:T(8,128)(2,1)S(1)}, bf16[8,128,128]{2,1,0:T(8,128)(2,1)S(1)}, u32[]{:S(2)}, u32[]{:S(2)}) collective-permute-start(bf16[8,128,128]{2,1,0:T(8,128)(2,1)S(1)} %get-tuple-element.44), channel_id=1, source_target_pairs={{0,64},{240,176},{1,65},{241,177},{2,66},{242,178},{3,67},{243,179... | collective-permute-start | bytes 786440 | tf_op jit(solution)/shard_map/ppermute | solution.py:392
  25.5 2.8 %collective-permute-start.10 = (bf16[2,8,128,128]{3,2,1,0:T(8,128)(2,1)S(1)}, bf16[2,8,128,128]{3,2,1,0:T(8,128)(2,1)S(1)}, u32[]{:S(2)}, u32[]{:S(2)}) collective-permute-start(bf16[2,8,128,128]{3,2,1,0:T(8,128)(2,1)S(1)} %get-tuple-element.45.kv_ref), channel_id=1, source_target_pairs={{0,15},{1,0},{2,1},{3,2},{4,3},{5,4},{6,5},{7,6},{8,7},{9,8},{10,9... | collective-permute-start | bytes 1572872 | tf_op jit(solution)/shard_map/ppermute | solution.py:385
  28.4 0.4 collective-permute-start.9
  28.7 8.6 %all-to-all-start = ((bf16[8,192,128]{2,1,0:T(8,128)(2,1)}), bf16[8,192,128]{2,1,0:T(8,128)(2,1)S(1)}, u32[]{:S(2)}, u32[]{:S(2)}) async-start(bf16[8,192,128]{2,1,0:T(8,128)(2,1)} %shard_map.67), calls=%async_computation | async-start | bytes 786432 | tf_op jit(solution)/shard_map/all_to_all | solution.py:381
  37.3 0.0 collective-permute-done.5
  37.3 0.0 collective-permute-done.6
  37.3 0.1 select_select_fusion
  37.4 1.3 %collective-permute-start.8 = (bf16[8,128,128]{2,1,0:T(8,128)(2,1)S(1)}, bf16[8,128,128]{2,1,0:T(8,128)(2,1)S(1)}, u32[]{:S(2)}, u32[]{:S(2)}) collective-permute-start(bf16[8,128,128]{2,1,0:T(8,128)(2,1)S(1)} %select_select_fusion), channel_id=1, source_target_pairs={{0,32},{64,96},{128,160},{192,224},{48,16},{112,80},{176,144},{240... | collective-permute-start | bytes 786440 | tf_op jit(solution)/shard_map/ppermute | solution.py:394
  38.7 0.7 collective-permute-start.11
  39.4 0.1 collective-permute-start.12
  39.5 3.1 %collective-permute-done.8 = bf16[8,128,128]{2,1,0:T(8,128)(2,1)S(1)} collective-permute-done((bf16[8,128,128]{2,1,0:T(8,128)(2,1)S(1)}, bf16[8,128,128]{2,1,0:T(8,128)(2,1)S(1)}, u32[]{:S(2)}, u32[]{:S(2)}) %collective-permute-start.8) | collective-permute-done | bytes 262176 | tf_op jit(solution)/shard_map/ppermute | solution.py:394
  42.6 0.0 collective-permute-done.11.qo_ref
  42.6 0.0 collective-permute-done.12.qi_ref
  42.6 0.0 collective-permute-done.9.kvw_ref
  42.6 5.7 %all-to-all-done.in_ref = bf16[8,192,128]{2,1,0:T(8,128)(2,1)S(1)} async-done(((bf16[8,192,128]{2,1,0:T(8,128)(2,1)}), bf16[8,192,128]{2,1,0:T(8,128)(2,1)S(1)}, u32[]{:S(2)}, u32[]{:S(2)}) %all-to-all-start) | async-done | bytes 393248 | tf_op jit(solution)/shard_map/all_to_all | solution.py:381
  48.3 2.1 %collective-permute-start.14 = (bf16[8,64,128]{2,1,0:T(8,128)(2,1)S(1)}, bf16[8,64,128]{2,1,0:T(8,128)(2,1)S(1)}, u32[]{:S(2)}, u32[]{:S(2)}) collective-permute-start(bf16[8,64,128]{2,1,0:T(8,128)(2,1)S(1)} %slice.3), channel_id=1, source_target_pairs={{0,8},{1,9},{2,10},{3,11},{4,12},{5,13},{6,14},{7,15},{8,0},{9,1},... | collective-permute-start | bytes 393224 | tf_op jit(solution)/shard_map/ppermute | solution.py:410
  50.4 6.3 %shard_map.68 = (f32[4,2,128,128]{3,2,1,0:T(8,128)S(1)}, bf16[2,128,128]{2,1,0:T(8,128)(2,1)S(1)}, bf16[5,128,128]{2,1,0:T(8,128)(2,1)S(1)}, bf16[5,128,128]{2,1,0:T(8,128)(2,1)S(1)}) custom-call(s32[1]{0:T(128)} %bitcast.band_ref, f32[128]{0:T(128)S(1)} %copy-done.5, s32[32]{0:T(128)S(1)} %copy-done.6, ...), custom_call_target="tpu_custom_call" | custom-call | flops 1000 | bytes 1000 | tf_op jit(solution)/shard_map/pallas_call | solution.py:399
  56.7 0.6 copy-done.3
  57.3 2.4 %shard_map.69.part_ref = bf16[8,80,128]{2,1,0:T(8,128)(2,1)S(1)} custom-call(s32[1]{0:T(128)} %bitcast.band_ref, s32[1]{0:T(128)} %bitcast.1.sector_ref, f32[128]{0:T(128)S(1)} %copy-done.5, bf16[8,192,128]{2,1,0:T(8,128)(2,1)S(1)} %all-to-all-done.in_ref), custom_call_target="tpu_custom_call" | custom-call | flops 5000000000 | bytes 1000000 | tf_op jit(solution)/shard_map/pallas_call | solution.py:414
  59.7 0.0 copy-start.2
  59.8 0.0 copy-start.11
  59.8 3.2 %shard_map.70 = bf16[16,80,128]{2,1,0:T(8,128)(2,1)} custom-call(s32[1]{0:T(128)} %bitcast.band_ref, s32[1]{0:T(128)} %bitcast.1.sector_ref, f32[128]{0:T(128)S(1)} %copy-done.5, bf16[8,192,128]{2,1,0:T(8,128)(2,1)S(1)} %all-to-all-done.in_ref, bf16[8,64,128]{2,1,0:T(8,128)(2,1)S(1)} %collective-permute-done.14.far_ref, ...), custom_call_target="tpu_custom_call" | custom-call | flops 3000000000 | bytes 1000000 | tf_op jit(solution)/shard_map/pallas_call | solution.py:417
  63.0 4.4 %all-to-all-start.1 = ((bf16[16,80,128]{2,1,0:T(8,128)(2,1)}), bf16[16,80,128]{2,1,0:T(8,128)(2,1)S(1)}, u32[]{:S(2)}, u32[]{:S(2)}) async-start(bf16[16,80,128]{2,1,0:T(8,128)(2,1)} %shard_map.70), calls=%async_computation.1 | async-start | bytes 655360 | tf_op jit(solution)/shard_map/all_to_all | solution.py:421
  67.3 0.7 collective-permute-start.15
  68.0 1.2 %collective-permute-start.16 = (bf16[5,128,128]{2,1,0:T(8,128)(2,1)S(1)}, bf16[5,128,128]{2,1,0:T(8,128)(2,1)S(1)}, u32[]{:S(2)}, u32[]{:S(2)}) collective-permute-start(bf16[5,128,128]{2,1,0:T(8,128)(2,1)S(1)} %copy-done.9), channel_id=1, source_target_pairs={{0,16},{16,0},{32,48},{48,32},{64,80},{80,64},{96,112},{112,96},{1... | collective-permute-start | bytes 491528 | tf_op jit(solution)/shard_map/ppermute | solution.py:408
  69.2 1.0 %collective-permute-done.16.ry_ref = bf16[5,128,128]{2,1,0:T(8,128)(2,1)S(1)} collective-permute-done((bf16[5,128,128]{2,1,0:T(8,128)(2,1)S(1)}, bf16[5,128,128]{2,1,0:T(8,128)(2,1)S(1)}, u32[]{:S(2)}, u32[]{:S(2)}) %collective-permute-start.16) | collective-permute-done | bytes 163872 | tf_op jit(solution)/shard_map/ppermute | solution.py:408
  70.2 9.0 %all-to-all-done.1.p1_ref = bf16[16,80,128]{2,1,0:T(8,128)(2,1)S(1)} async-done(((bf16[16,80,128]{2,1,0:T(8,128)(2,1)}), bf16[16,80,128]{2,1,0:T(8,128)(2,1)S(1)}, u32[]{:S(2)}, u32[]{:S(2)}) %all-to-all-start.1) | async-done | bytes 327712 | tf_op jit(solution)/shard_map/all_to_all | solution.py:421
  79.3 1.3 %shard_map.71.old_ref = bf16[2,128,512]{2,1,0:T(8,128)(2,1)} custom-call(s32[1]{0:T(128)} %bitcast.band_ref, f32[4,2,128,128]{3,2,1,0:T(8,128)S(1)} %get-tuple-element.53.o_ref, bf16[2,128,128]{2,1,0:T(8,128)(2,1)S(1)} %copy-done.4, bf16[5,128,128]{2,1,0:T(8,128)(2,1)S(1)} %collective-permute-done.15.rx_ref, ...), custom_call_target="tpu_custom_call" | custom-call | flops 1000000000 | bytes 3000000 | tf_op jit(solution)/shard_map/pallas_call | solution.py:426
  80.6 0.3 collective-permute-done.17.p2_ref
  80.9 1.6 %shard_map.72 = bf16[2,128,512]{2,1,0:T(8,128)(2,1)} custom-call(s32[1]{0:T(128)} %bitcast.band_ref, f32[4,2,128,128]{3,2,1,0:T(8,128)S(1)} %get-tuple-element.53.o_ref, bf16[2,128,128]{2,1,0:T(8,128)(2,1)S(1)} %copy-done.4, bf16[16,80,128]{2,1,0:T(8,128)(2,1)S(1)} %all-to-all-done.1.p1_ref, ...), custom_call_target="tpu_custom_call", output_to_operand_aliasing={{}: (6, {})} | custom-call | flops 1000000 | bytes 1000000 | tf_op jit(solution)/shard_map/pallas_call | solution.py:430
  (28 shorter events, 0.1 us)
Async XLA Ops:
  0.0 0.9 %copy-start.7 = (bf16[2,128,512]{2,1,0:T(8,128)(2,1)S(1)}, bf16[2,128,512]{2,1,0:T(8,128)(2,1)}, u32[]{:S(2)}) copy-start(bf16[2,128,512]{2,1,0:T(8,128)(2,1)} %f_ref.1) | copy-start | bytes 786436
  1.0 5.9 %copy-start = (bf16[1536,1024]{1,0:T(8,128)(2,1)S(1)}, bf16[1536,1024]{1,0:T(8,128)(2,1)}, u32[]{:S(2)}) copy-start(bf16[1536,1024]{1,0:T(8,128)(2,1)} %w_ref.3) | copy-start | bytes 9437188
  1.0 5.9 %copy-start.1 = (bf16[512,512]{1,0:T(8,128)(2,1)S(1)}, bf16[512,512]{1,0:T(8,128)(2,1)}, u32[]{:S(2)}) copy-start(bf16[512,512]{1,0:T(8,128)(2,1)} %wq_ref.1) | copy-start | bytes 1572868
  1.0 9.7 %copy-start.5 = (f32[128]{0:T(128)S(1)}, f32[128]{0:T(128)}, u32[]{:S(2)}) copy-start(f32[128]{0:T(128)} %constant.39.clone.table_ref) | copy-start | bytes 1540
  1.0 9.7 %collective-permute-start = (bf16[128,512]{1,0:T(8,128)(2,1)S(1)}, bf16[128,512]{1,0:T(8,128)(2,1)S(1)}, u32[]{:S(2)}, u32[]{:S(2)}) collective-permute-start(bf16[128,512]{1,0:T(8,128)(2,1)S(1)} %get-tuple-element.34.fx_ref), channel_id=1, source_target_pairs={{16,32},{32,16},{48,64},{64,48},{80,96},{96,80},{112,128},{128,112... | collective-permute-start | bytes 393224 | tf_op jit(solution)/shard_map/ppermute | solution.py:358
  1.8 8.9 %collective-permute-start.1 = (bf16[128,512]{1,0:T(8,128)(2,1)S(1)}, bf16[128,512]{1,0:T(8,128)(2,1)S(1)}, u32[]{:S(2)}, u32[]{:S(2)}) collective-permute-start(bf16[128,512]{1,0:T(8,128)(2,1)S(1)} %get-tuple-element.35.fy_ref), channel_id=1, source_target_pairs={{0,16},{16,0},{32,48},{48,32},{64,80},{80,64},{96,112},{112,96},{1... | collective-permute-start | bytes 393224 | tf_op jit(solution)/shard_map/ppermute | solution.py:359
  4.9 3.9 %collective-permute-start.2 = (bf16[2,16,512]{2,1,0:T(8,128)(2,1)S(1)}, bf16[2,16,512]{2,1,0:T(8,128)(2,1)S(1)}, u32[]{:S(2)}, u32[]{:S(2)}) collective-permute-start(bf16[2,16,512]{2,1,0:T(8,128)(2,1)S(1)} %get-tuple-element.36), channel_id=1, source_target_pairs={{0,1},{1,2},{2,3},{3,4},{4,5},{5,6},{6,7},{7,8},{8,9},{9,10},{10,1... | collective-permute-start | bytes 98312 | tf_op jit(solution)/shard_map/ppermute | solution.py:360
  6.8 3.9 %collective-permute-start.3 = (bf16[2,16,512]{2,1,0:T(8,128)(2,1)S(1)}, bf16[2,16,512]{2,1,0:T(8,128)(2,1)S(1)}, u32[]{:S(2)}, u32[]{:S(2)}) collective-permute-start(bf16[2,16,512]{2,1,0:T(8,128)(2,1)S(1)} %get-tuple-element.37), channel_id=1, source_target_pairs={{0,15},{1,0},{2,1},{3,2},{4,3},{5,4},{6,5},{7,6},{8,7},{9,8},{10,9... | collective-permute-start | bytes 98312 | tf_op jit(solution)/shard_map/ppermute | solution.py:361
  12.9 37.4 %copy-start.6 = (s32[32]{0:T(128)S(1)}, s32[32]{0:T(128)}, u32[]{:S(2)}) copy-start(s32[32]{0:T(128)} %width_ref.1) | copy-start | bytes 388
  13.0 1.8 %collective-permute-start.4 = (bf16[8,192,128]{2,1,0:T(8,128)(2,1)S(1)}, bf16[8,192,128]{2,1,0:T(8,128)(2,1)S(1)}, u32[]{:S(2)}, u32[]{:S(2)}) collective-permute-start(bf16[8,192,128]{2,1,0:T(8,128)(2,1)S(1)} %get-tuple-element.43), channel_id=1, source_target_pairs={{0,16},{16,0},{32,48},{48,32},{64,80},{80,64},{96,112},{112,96},{1... | collective-permute-start | bytes 1179656 | tf_op jit(solution)/shard_map/ppermute | solution.py:377
  15.6 21.7 %collective-permute-start.5 = (bf16[8,128,128]{2,1,0:T(8,128)(2,1)S(1)}, bf16[8,128,128]{2,1,0:T(8,128)(2,1)S(1)}, u32[]{:S(2)}, u32[]{:S(2)}) collective-permute-start(bf16[8,128,128]{2,1,0:T(8,128)(2,1)S(1)} %get-tuple-element.44), channel_id=1, source_target_pairs={{0,192},{240,48},{1,193},{241,49},{2,194},{242,50},{3,195},{243,51... | collective-permute-start | bytes 786440 | tf_op jit(solution)/shard_map/ppermute | solution.py:392
  22.9 14.4 %collective-permute-start.6 = (bf16[8,128,128]{2,1,0:T(8,128)(2,1)S(1)}, bf16[8,128,128]{2,1,0:T(8,128)(2,1)S(1)}, u32[]{:S(2)}, u32[]{:S(2)}) collective-permute-start(bf16[8,128,128]{2,1,0:T(8,128)(2,1)S(1)} %get-tuple-element.44), channel_id=1, source_target_pairs={{0,128},{240,112},{1,129},{241,113},{2,130},{242,114},{3,131},{243... | collective-permute-start | bytes 786440 | tf_op jit(solution)/shard_map/ppermute | solution.py:392
  24.2 13.1 %collective-permute-start.7 = (bf16[8,128,128]{2,1,0:T(8,128)(2,1)S(1)}, bf16[8,128,128]{2,1,0:T(8,128)(2,1)S(1)}, u32[]{:S(2)}, u32[]{:S(2)}) collective-permute-start(bf16[8,128,128]{2,1,0:T(8,128)(2,1)S(1)} %get-tuple-element.44), channel_id=1, source_target_pairs={{0,64},{240,176},{1,65},{241,177},{2,66},{242,178},{3,67},{243,179... | collective-permute-start | bytes 786440 | tf_op jit(solution)/shard_map/ppermute | solution.py:392
  25.5 17.0 %collective-permute-start.10 = (bf16[2,8,128,128]{3,2,1,0:T(8,128)(2,1)S(1)}, bf16[2,8,128,128]{3,2,1,0:T(8,128)(2,1)S(1)}, u32[]{:S(2)}, u32[]{:S(2)}) collective-permute-start(bf16[2,8,128,128]{3,2,1,0:T(8,128)(2,1)S(1)} %get-tuple-element.45.kv_ref), channel_id=1, source_target_pairs={{0,15},{1,0},{2,1},{3,2},{4,3},{5,4},{6,5},{7,6},{8,7},{9,8},{10,9... | collective-permute-start | bytes 1572872 | tf_op jit(solution)/shard_map/ppermute | solution.py:385
  28.4 14.2 %collective-permute-start.9 = (bf16[2,8,128,128]{3,2,1,0:T(8,128)(2,1)S(1)}, bf16[2,8,128,128]{3,2,1,0:T(8,128)(2,1)S(1)}, u32[]{:S(2)}, u32[]{:S(2)}) collective-permute-start(bf16[2,8,128,128]{3,2,1,0:T(8,128)(2,1)S(1)} %get-tuple-element.45.kv_ref), channel_id=1, source_target_pairs={{0,1},{1,2},{2,3},{3,4},{4,5},{5,6},{6,7},{7,8},{8,9},{9,10},{10,1... | collective-permute-start | bytes 1572872 | tf_op jit(solution)/shard_map/ppermute | solution.py:384
  28.7 19.5 %all-to-all-start = ((bf16[8,192,128]{2,1,0:T(8,128)(2,1)}), bf16[8,192,128]{2,1,0:T(8,128)(2,1)S(1)}, u32[]{:S(2)}, u32[]{:S(2)}) async-start(bf16[8,192,128]{2,1,0:T(8,128)(2,1)} %shard_map.67), calls=%async_computation | async-start | bytes 786432 | tf_op jit(solution)/shard_map/all_to_all | solution.py:381
  37.4 5.2 %collective-permute-start.8 = (bf16[8,128,128]{2,1,0:T(8,128)(2,1)S(1)}, bf16[8,128,128]{2,1,0:T(8,128)(2,1)S(1)}, u32[]{:S(2)}, u32[]{:S(2)}) collective-permute-start(bf16[8,128,128]{2,1,0:T(8,128)(2,1)S(1)} %select_select_fusion), channel_id=1, source_target_pairs={{0,32},{64,96},{128,160},{192,224},{48,16},{112,80},{176,144},{240... | collective-permute-start | bytes 786440 | tf_op jit(solution)/shard_map/ppermute | solution.py:394
  38.7 3.9 %collective-permute-start.11 = (bf16[4,128,128]{2,1,0:T(8,128)(2,1)S(1)}, bf16[4,128,128]{2,1,0:T(8,128)(2,1)S(1)}, u32[]{:S(2)}, u32[]{:S(2)}) collective-permute-start(bf16[4,128,128]{2,1,0:T(8,128)(2,1)S(1)} %get-tuple-element.46.qx_ref), channel_id=1, source_target_pairs={{16,32},{32,16},{48,64},{64,48},{80,96},{96,80},{112,128},{128,112... | collective-permute-start | bytes 393224 | tf_op jit(solution)/shard_map/ppermute | solution.py:386
  39.4 3.2 %collective-permute-start.12 = (bf16[4,128,128]{2,1,0:T(8,128)(2,1)S(1)}, bf16[4,128,128]{2,1,0:T(8,128)(2,1)S(1)}, u32[]{:S(2)}, u32[]{:S(2)}) collective-permute-start(bf16[4,128,128]{2,1,0:T(8,128)(2,1)S(1)} %get-tuple-element.47.qy_ref), channel_id=1, source_target_pairs={{0,16},{16,0},{32,48},{48,32},{64,80},{80,64},{96,112},{112,96},{1... | collective-permute-start | bytes 393224 | tf_op jit(solution)/shard_map/ppermute | solution.py:387
  48.3 2.1 %collective-permute-start.13 = (bf16[8,128,128]{2,1,0:T(8,128)(2,1)S(1)}, bf16[8,128,128]{2,1,0:T(8,128)(2,1)S(1)}, u32[]{:S(2)}, u32[]{:S(2)}) collective-permute-start(bf16[8,128,128]{2,1,0:T(8,128)(2,1)S(1)} %broadcast_select_fusion.p1_ref), channel_id=1, source_target_pairs={{0,16},{16,0},{32,48},{48,32},{64,80},{80,64},{96,112},{112,96},{1... | collective-permute-start | bytes 786440 | tf_op jit(solution)/shard_map/ppermute | solution.py:397
  48.3 11.5 %collective-permute-start.14 = (bf16[8,64,128]{2,1,0:T(8,128)(2,1)S(1)}, bf16[8,64,128]{2,1,0:T(8,128)(2,1)S(1)}, u32[]{:S(2)}, u32[]{:S(2)}) collective-permute-start(bf16[8,64,128]{2,1,0:T(8,128)(2,1)S(1)} %slice.3), channel_id=1, source_target_pairs={{0,8},{1,9},{2,10},{3,11},{4,12},{5,13},{6,14},{7,15},{8,0},{9,1},... | collective-permute-start | bytes 393224 | tf_op jit(solution)/shard_map/ppermute | solution.py:410
  56.7 0.6 copy-start.3
  57.3 2.4 %copy-start.8 = (bf16[5,128,128]{2,1,0:T(8,128)(2,1)}, bf16[5,128,128]{2,1,0:T(8,128)(2,1)S(1)}, u32[]{:S(2)}) copy-start(bf16[5,128,128]{2,1,0:T(8,128)(2,1)S(1)} %get-tuple-element.59) | copy-start | bytes 491524
  57.3 2.4 %copy-start.10 = (bf16[5,128,128]{2,1,0:T(8,128)(2,1)}, bf16[5,128,128]{2,1,0:T(8,128)(2,1)S(1)}, u32[]{:S(2)}) copy-start(bf16[5,128,128]{2,1,0:T(8,128)(2,1)S(1)} %get-tuple-element.58) | copy-start | bytes 491524
  59.7 19.5 %copy-start.2 = (bf16[512,512]{1,0:T(8,128)(2,1)S(1)}, bf16[512,512]{1,0:T(8,128)(2,1)}, u32[]{:S(2)}) copy-start(bf16[512,512]{1,0:T(8,128)(2,1)} %wo_ref.3) | copy-start | bytes 1572868
  59.7 19.5 %copy-start.4 = (bf16[2,128,128]{2,1,0:T(8,128)(2,1)S(1)}, bf16[2,128,128]{2,1,0:T(8,128)(2,1)}, u32[]{:S(2)}) copy-start(bf16[2,128,128]{2,1,0:T(8,128)(2,1)} %copy-done.3) | copy-start | bytes 196612
  59.8 7.6 %copy-start.11 = (bf16[5,128,128]{2,1,0:T(8,128)(2,1)S(1)}, bf16[5,128,128]{2,1,0:T(8,128)(2,1)}, u32[]{:S(2)}) copy-start(bf16[5,128,128]{2,1,0:T(8,128)(2,1)} %copy-done.10) | copy-start | bytes 491524
  59.8 8.2 %copy-start.9 = (bf16[5,128,128]{2,1,0:T(8,128)(2,1)S(1)}, bf16[5,128,128]{2,1,0:T(8,128)(2,1)}, u32[]{:S(2)}) copy-start(bf16[5,128,128]{2,1,0:T(8,128)(2,1)} %copy-done.8) | copy-start | bytes 491524
  63.0 16.3 %all-to-all-start.1 = ((bf16[16,80,128]{2,1,0:T(8,128)(2,1)}), bf16[16,80,128]{2,1,0:T(8,128)(2,1)S(1)}, u32[]{:S(2)}, u32[]{:S(2)}) async-start(bf16[16,80,128]{2,1,0:T(8,128)(2,1)} %shard_map.70), calls=%async_computation.1 | async-start | bytes 655360 | tf_op jit(solution)/shard_map/all_to_all | solution.py:421
  67.3 1.9 %collective-permute-start.15 = (bf16[5,128,128]{2,1,0:T(8,128)(2,1)S(1)}, bf16[5,128,128]{2,1,0:T(8,128)(2,1)S(1)}, u32[]{:S(2)}, u32[]{:S(2)}) collective-permute-start(bf16[5,128,128]{2,1,0:T(8,128)(2,1)S(1)} %copy-done.11), channel_id=1, source_target_pairs={{16,32},{32,16},{48,64},{64,48},{80,96},{96,80},{112,128},{128,112... | collective-permute-start | bytes 491528 | tf_op jit(solution)/shard_map/ppermute | solution.py:407
  68.0 2.2 %collective-permute-start.16 = (bf16[5,128,128]{2,1,0:T(8,128)(2,1)S(1)}, bf16[5,128,128]{2,1,0:T(8,128)(2,1)S(1)}, u32[]{:S(2)}, u32[]{:S(2)}) collective-permute-start(bf16[5,128,128]{2,1,0:T(8,128)(2,1)S(1)} %copy-done.9), channel_id=1, source_target_pairs={{0,16},{16,0},{32,48},{48,32},{64,80},{80,64},{96,112},{112,96},{1... | collective-permute-start | bytes 491528 | tf_op jit(solution)/shard_map/ppermute | solution.py:408
  79.3 1.6 %collective-permute-start.17 = (bf16[16,80,128]{2,1,0:T(8,128)(2,1)S(1)}, bf16[16,80,128]{2,1,0:T(8,128)(2,1)S(1)}, u32[]{:S(2)}, u32[]{:S(2)}) collective-permute-start(bf16[16,80,128]{2,1,0:T(8,128)(2,1)S(1)} %all-to-all-done.1.p1_ref), channel_id=1, source_target_pairs={{0,16},{16,0},{32,48},{48,32},{64,80},{80,64},{96,112},{112,96},{1... | collective-permute-start | bytes 983048 | tf_op jit(solution)/shard_map/ppermute | solution.py:424

commit v6 on v5

--- a/solution.py
+++ b/solution.py
@@ -128,7 +128,13 @@
 
 
 def pick_kernel(band_ref, own_ref, got_ref, out_ref):
-    out_ref[...] = jnp.where(is_polar(band_ref[0]), own_ref[...], got_ref[...])
+    @pl.when(is_polar(band_ref[0]))
+    def _():
+        out_ref[...] = own_ref[...]
+
+    @pl.when((band_ref[0] == 1) | (band_ref[0] == NLAT // 2 - 2))
+    def _():
+        out_ref[...] = got_ref[...]
 
 
 def window_kernel(

time: 83.1 us -> 83 us (level)
  no operation moved by 1% of the time
where the time goes in v6:
time: 83 us; the launch traced here: 82.6 us
  starting transfers between devices  37.9 us (46%)
  waiting for transfers between devices  24.1 us (29%)
  Pallas kernels  18.4 us (22%)
  local copies, waits for them, and re-layouts  1.62 us (2%)
    ppermute x3, starting transfers between devices, body(): got = lax.ppermute(kvx, 'lat', [(0, step), (nlat - 1, nlat - 1 - step)])  9.85 us
    all_to_all x1, waiting for transfers between devices, body(): part = lax.all_to_all(part, 'lon', 0, 0)  9.04 us
    all_to_all x1, starting transfers between devices, body(): all_polar = lax.all_to_all(picked, 'lon', 0, 0, axis_index_groups=groups)  8.55 us
    pallas_call x1, Pallas kernels, body(): call(window_kernel, (sds((PAIRS, 2, 128, LANES), F32), sds((2, 128, LANES...  6.34 us
    all_to_all x1, waiting for transfers between devices, body(): all_polar = lax.all_to_all(picked, 'lon', 0, 0, axis_index_groups=groups)  5.68 us
    all_to_all x1, starting transfers between devices, body(): part = lax.all_to_all(part, 'lon', 0, 0)  4.39 us
    pallas_call x1, Pallas kernels, body(): call(polar_far_kernel, sds((16, 80, LANES)), [SMEM, SMEM, SMEM, VMEM, VME...  3.16 us
    ppermute x1, waiting for transfers between devices, body(): lax.ppermute(x, 'lat', [(i, i + 2) for i in range(0, 16, 4)] + [(i, i - 2...  3.07 us
  transfers between devices with their start and end apart: 20, of which 8 were waited for; matrix products, arithmetic and copies ran while one was open for 0% of the time, Pallas kernels for 13%

profile of v6, /device:TPU:32, one launch (start us, length us, event | category | flops | bytes accessed | tf_op | source)
XLA Modules:
  0.0 82.6 jit_solution(13035356804149565828)
XLA Ops:
  0.0 0.9 %copy-done.7 = bf16[2,128,512]{2,1,0:T(8,128)(2,1)S(1)} copy-done((bf16[2,128,512]{2,1,0:T(8,128)(2,1)S(1)}, bf16[2,128,512]{2,1,0:T(8,128)(2,1)}, u32[]{:S(2)}) %copy-start.7) | copy-done | bytes 262168
  1.0 0.0 copy-start.5
  1.0 0.8 collective-permute-start
  1.8 3.1 %collective-permute-start.1 = (bf16[128,512]{1,0:T(8,128)(2,1)S(1)}, bf16[128,512]{1,0:T(8,128)(2,1)S(1)}, u32[]{:S(2)}, u32[]{:S(2)}) collective-permute-start(bf16[128,512]{1,0:T(8,128)(2,1)S(1)} %get-tuple-element.35.fy_ref), channel_id=1, source_target_pairs={{0,16},{16,0},{32,48},{48,32},{64,80},{80,64},{96,112},{112,96},{1... | collective-permute-start | bytes 393224 | tf_op jit(solution)/shard_map/ppermute | solution.py:365
  4.9 1.9 %collective-permute-start.2 = (bf16[2,16,512]{2,1,0:T(8,128)(2,1)S(1)}, bf16[2,16,512]{2,1,0:T(8,128)(2,1)S(1)}, u32[]{:S(2)}, u32[]{:S(2)}) collective-permute-start(bf16[2,16,512]{2,1,0:T(8,128)(2,1)S(1)} %get-tuple-element.36), channel_id=1, source_target_pairs={{0,1},{1,2},{2,3},{3,4},{4,5},{5,6},{6,7},{7,8},{8,9},{9,10},{10,1... | collective-permute-start | bytes 98312 | tf_op jit(solution)/shard_map/ppermute | solution.py:366
  6.8 0.1 collective-permute-start.3
  6.9 0.6 shard_map.65
  7.5 1.3 %collective-permute-done.2.west_ref = bf16[2,16,512]{2,1,0:T(8,128)(2,1)S(1)} collective-permute-done((bf16[2,16,512]{2,1,0:T(8,128)(2,1)S(1)}, bf16[2,16,512]{2,1,0:T(8,128)(2,1)S(1)}, u32[]{:S(2)}, u32[]{:S(2)}) %collective-permute-start.2) | collective-permute-done | bytes 32800 | tf_op jit(solution)/shard_map/ppermute | solution.py:366
  8.8 1.9 %collective-permute-done.3.east_ref = bf16[2,16,512]{2,1,0:T(8,128)(2,1)S(1)} collective-permute-done((bf16[2,16,512]{2,1,0:T(8,128)(2,1)S(1)}, bf16[2,16,512]{2,1,0:T(8,128)(2,1)S(1)}, u32[]{:S(2)}, u32[]{:S(2)}) %collective-permute-start.3) | collective-permute-done | bytes 32800 | tf_op jit(solution)/shard_map/ppermute | solution.py:367
  10.7 0.0 collective-permute-done.outer_ref
  10.7 2.2 %shard_map.66 = (bf16[2,8,128,128]{3,2,1,0:T(8,128)(2,1)S(1)}, bf16[8,128,128]{2,1,0:T(8,128)(2,1)S(1)}, bf16[8,192,128]{2,1,0:T(8,128)(2,1)S(1)}, bf16[8,192,128]{2,1,0:T(8,128)(2,1)S(1)}) custom-call(s32[1]{0:T(128)} %bitcast.band_ref, f32[128]{0:T(128)S(1)} %copy-done.5, bf16[128,512]{1,0:T(8,128)(2,1)S(1)} %get-tuple-element.34.fx_ref, ...), custom_call_target="tpu_custom_call" | custom-call | flops 1000000000 | bytes 4000000 | tf_op jit(solution)/shard_map/pallas_call | solution.py:375
  12.9 0.0 copy-start.6
  13.0 0.1 collective-permute-start.4
  13.1 1.7 %collective-permute-done.4.got_ref = bf16[8,192,128]{2,1,0:T(8,128)(2,1)S(1)} collective-permute-done((bf16[8,192,128]{2,1,0:T(8,128)(2,1)S(1)}, bf16[8,192,128]{2,1,0:T(8,128)(2,1)S(1)}, u32[]{:S(2)}, u32[]{:S(2)}) %collective-permute-start.4) | collective-permute-done | bytes 393248 | tf_op jit(solution)/shard_map/ppermute | solution.py:383
  14.8 0.8 shard_map.67
  15.5 7.2 %collective-permute-start.5 = (bf16[8,128,128]{2,1,0:T(8,128)(2,1)S(1)}, bf16[8,128,128]{2,1,0:T(8,128)(2,1)S(1)}, u32[]{:S(2)}, u32[]{:S(2)}) collective-permute-start(bf16[8,128,128]{2,1,0:T(8,128)(2,1)S(1)} %get-tuple-element.44), channel_id=1, source_target_pairs={{0,192},{240,48},{1,193},{241,49},{2,194},{242,50},{3,195},{243,51... | collective-permute-start | bytes 786440 | tf_op jit(solution)/shard_map/ppermute | solution.py:398
  22.8 1.3 %collective-permute-start.6 = (bf16[8,128,128]{2,1,0:T(8,128)(2,1)S(1)}, bf16[8,128,128]{2,1,0:T(8,128)(2,1)S(1)}, u32[]{:S(2)}, u32[]{:S(2)}) collective-permute-start(bf16[8,128,128]{2,1,0:T(8,128)(2,1)S(1)} %get-tuple-element.44), channel_id=1, source_target_pairs={{0,128},{240,112},{1,129},{241,113},{2,130},{242,114},{3,131},{243... | collective-permute-start | bytes 786440 | tf_op jit(solution)/shard_map/ppermute | solution.py:398
  24.1 1.3 %collective-permute-start.7 = (bf16[8,128,128]{2,1,0:T(8,128)(2,1)S(1)}, bf16[8,128,128]{2,1,0:T(8,128)(2,1)S(1)}, u32[]{:S(2)}, u32[]{:S(2)}) collective-permute-start(bf16[8,128,128]{2,1,0:T(8,128)(2,1)S(1)} %get-tuple-element.44), channel_id=1, source_target_pairs={{0,64},{240,176},{1,65},{241,177},{2,66},{242,178},{3,67},{243,179... | collective-permute-start | bytes 786440 | tf_op jit(solution)/shard_map/ppermute | solution.py:398
  25.4 2.8 %collective-permute-start.10 = (bf16[2,8,128,128]{3,2,1,0:T(8,128)(2,1)S(1)}, bf16[2,8,128,128]{3,2,1,0:T(8,128)(2,1)S(1)}, u32[]{:S(2)}, u32[]{:S(2)}) collective-permute-start(bf16[2,8,128,128]{3,2,1,0:T(8,128)(2,1)S(1)} %get-tuple-element.45.kv_ref), channel_id=1, source_target_pairs={{0,15},{1,0},{2,1},{3,2},{4,3},{5,4},{6,5},{7,6},{8,7},{9,8},{10,9... | collective-permute-start | bytes 1572872 | tf_op jit(solution)/shard_map/ppermute | solution.py:391
  28.3 0.4 collective-permute-start.9
  28.6 8.6 %all-to-all-start = ((bf16[8,192,128]{2,1,0:T(8,128)(2,1)}), bf16[8,192,128]{2,1,0:T(8,128)(2,1)S(1)}, u32[]{:S(2)}, u32[]{:S(2)}) async-start(bf16[8,192,128]{2,1,0:T(8,128)(2,1)} %shard_map.67), calls=%async_computation | async-start | bytes 786432 | tf_op jit(solution)/shard_map/all_to_all | solution.py:387
  37.2 0.0 collective-permute-done.5
  37.2 0.0 collective-permute-done.6
  37.2 0.1 select_select_fusion
  37.3 1.3 %collective-permute-start.8 = (bf16[8,128,128]{2,1,0:T(8,128)(2,1)S(1)}, bf16[8,128,128]{2,1,0:T(8,128)(2,1)S(1)}, u32[]{:S(2)}, u32[]{:S(2)}) collective-permute-start(bf16[8,128,128]{2,1,0:T(8,128)(2,1)S(1)} %select_select_fusion), channel_id=1, source_target_pairs={{0,32},{64,96},{128,160},{192,224},{48,16},{112,80},{176,144},{240... | collective-permute-start | bytes 786440 | tf_op jit(solution)/shard_map/ppermute | solution.py:400
  38.6 0.7 collective-permute-start.11
  39.2 0.1 collective-permute-start.12
  39.4 3.1 %collective-permute-done.8 = bf16[8,128,128]{2,1,0:T(8,128)(2,1)S(1)} collective-permute-done((bf16[8,128,128]{2,1,0:T(8,128)(2,1)S(1)}, bf16[8,128,128]{2,1,0:T(8,128)(2,1)S(1)}, u32[]{:S(2)}, u32[]{:S(2)}) %collective-permute-start.8) | collective-permute-done | bytes 262176 | tf_op jit(solution)/shard_map/ppermute | solution.py:400
  42.5 0.0 collective-permute-done.11.qo_ref
  42.5 0.0 collective-permute-done.9.kvw_ref
  42.5 5.7 %all-to-all-done.in_ref = bf16[8,192,128]{2,1,0:T(8,128)(2,1)S(1)} async-done(((bf16[8,192,128]{2,1,0:T(8,128)(2,1)}), bf16[8,192,128]{2,1,0:T(8,128)(2,1)S(1)}, u32[]{:S(2)}, u32[]{:S(2)}) %all-to-all-start) | async-done | bytes 393248 | tf_op jit(solution)/shard_map/all_to_all | solution.py:387
  48.2 0.0 collective-permute-start.13
  48.2 2.1 %collective-permute-start.14 = (bf16[8,64,128]{2,1,0:T(8,128)(2,1)S(1)}, bf16[8,64,128]{2,1,0:T(8,128)(2,1)S(1)}, u32[]{:S(2)}, u32[]{:S(2)}) collective-permute-start(bf16[8,64,128]{2,1,0:T(8,128)(2,1)S(1)} %slice.3), channel_id=1, source_target_pairs={{0,8},{1,9},{2,10},{3,11},{4,12},{5,13},{6,14},{7,15},{8,0},{9,1},... | collective-permute-start | bytes 393224 | tf_op jit(solution)/shard_map/ppermute | solution.py:416
  50.3 6.3 %shard_map.68 = (f32[4,2,128,128]{3,2,1,0:T(8,128)S(1)}, bf16[2,128,128]{2,1,0:T(8,128)(2,1)S(1)}, bf16[5,128,128]{2,1,0:T(8,128)(2,1)S(1)}, bf16[5,128,128]{2,1,0:T(8,128)(2,1)S(1)}) custom-call(s32[1]{0:T(128)} %bitcast.band_ref, f32[128]{0:T(128)S(1)} %copy-done.5, s32[32]{0:T(128)S(1)} %copy-done.6, ...), custom_call_target="tpu_custom_call" | custom-call | flops 1000 | bytes 1000 | tf_op jit(solution)/shard_map/pallas_call | solution.py:405
  56.6 0.6 copy-done.3
  57.2 2.4 %shard_map.69.part_ref = bf16[8,80,128]{2,1,0:T(8,128)(2,1)S(1)} custom-call(s32[1]{0:T(128)} %bitcast.band_ref, s32[1]{0:T(128)} %bitcast.1.sector_ref, f32[128]{0:T(128)S(1)} %copy-done.5, bf16[8,192,128]{2,1,0:T(8,128)(2,1)S(1)} %all-to-all-done.in_ref), custom_call_target="tpu_custom_call" | custom-call | flops 5000000000 | bytes 1000000 | tf_op jit(solution)/shard_map/pallas_call | solution.py:420
  59.7 0.0 copy-start.2
  59.7 0.0 copy-start.11
  59.7 3.2 %shard_map.70 = bf16[16,80,128]{2,1,0:T(8,128)(2,1)} custom-call(s32[1]{0:T(128)} %bitcast.band_ref, s32[1]{0:T(128)} %bitcast.1.sector_ref, f32[128]{0:T(128)S(1)} %copy-done.5, bf16[8,192,128]{2,1,0:T(8,128)(2,1)S(1)} %all-to-all-done.in_ref, bf16[8,64,128]{2,1,0:T(8,128)(2,1)S(1)} %collective-permute-done.14.far_ref, ...), custom_call_target="tpu_custom_call" | custom-call | flops 3000000000 | bytes 1000000 | tf_op jit(solution)/shard_map/pallas_call | solution.py:423
  62.9 4.4 %all-to-all-start.1 = ((bf16[16,80,128]{2,1,0:T(8,128)(2,1)}), bf16[16,80,128]{2,1,0:T(8,128)(2,1)S(1)}, u32[]{:S(2)}, u32[]{:S(2)}) async-start(bf16[16,80,128]{2,1,0:T(8,128)(2,1)} %shard_map.70), calls=%async_computation.1 | async-start | bytes 655360 | tf_op jit(solution)/shard_map/all_to_all | solution.py:427
  67.3 0.7 collective-permute-start.15
  68.0 1.2 %collective-permute-start.16 = (bf16[5,128,128]{2,1,0:T(8,128)(2,1)S(1)}, bf16[5,128,128]{2,1,0:T(8,128)(2,1)S(1)}, u32[]{:S(2)}, u32[]{:S(2)}) collective-permute-start(bf16[5,128,128]{2,1,0:T(8,128)(2,1)S(1)} %copy-done.9), channel_id=1, source_target_pairs={{0,16},{16,0},{32,48},{48,32},{64,80},{80,64},{96,112},{112,96},{1... | collective-permute-start | bytes 491528 | tf_op jit(solution)/shard_map/ppermute | solution.py:414
  69.1 0.0 collective-permute-done.15.rx_ref
  69.1 1.0 %collective-permute-done.16.ry_ref = bf16[5,128,128]{2,1,0:T(8,128)(2,1)S(1)} collective-permute-done((bf16[5,128,128]{2,1,0:T(8,128)(2,1)S(1)}, bf16[5,128,128]{2,1,0:T(8,128)(2,1)S(1)}, u32[]{:S(2)}, u32[]{:S(2)}) %collective-permute-start.16) | collective-permute-done | bytes 163872 | tf_op jit(solution)/shard_map/ppermute | solution.py:414
  70.1 9.0 %all-to-all-done.1.p1_ref = bf16[16,80,128]{2,1,0:T(8,128)(2,1)S(1)} async-done(((bf16[16,80,128]{2,1,0:T(8,128)(2,1)}), bf16[16,80,128]{2,1,0:T(8,128)(2,1)S(1)}, u32[]{:S(2)}, u32[]{:S(2)}) %all-to-all-start.1) | async-done | bytes 327712 | tf_op jit(solution)/shard_map/all_to_all | solution.py:427
  79.2 1.3 %shard_map.71.old_ref = bf16[2,128,512]{2,1,0:T(8,128)(2,1)} custom-call(s32[1]{0:T(128)} %bitcast.band_ref, f32[4,2,128,128]{3,2,1,0:T(8,128)S(1)} %get-tuple-element.53.o_ref, bf16[2,128,128]{2,1,0:T(8,128)(2,1)S(1)} %copy-done.4, bf16[5,128,128]{2,1,0:T(8,128)(2,1)S(1)} %collective-permute-done.15.rx_ref, ...), custom_call_target="tpu_custom_call" | custom-call | flops 1000000000 | bytes 3000000 | tf_op jit(solution)/shard_map/pallas_call | solution.py:432
  80.5 0.3 collective-permute-done.17.p2_ref
  80.8 1.6 %shard_map.72 = bf16[2,128,512]{2,1,0:T(8,128)(2,1)} custom-call(s32[1]{0:T(128)} %bitcast.band_ref, f32[4,2,128,128]{3,2,1,0:T(8,128)S(1)} %get-tuple-element.53.o_ref, bf16[2,128,128]{2,1,0:T(8,128)(2,1)S(1)} %copy-done.4, bf16[16,80,128]{2,1,0:T(8,128)(2,1)S(1)} %all-to-all-done.1.p1_ref, ...), custom_call_target="tpu_custom_call", output_to_operand_aliasing={{}: (6, {})} | custom-call | flops 1000000 | bytes 1000000 | tf_op jit(solution)/shard_map/pallas_call | solution.py:436
  (28 shorter events, 0.1 us)
Async XLA Ops:
  0.0 0.9 %copy-start.7 = (bf16[2,128,512]{2,1,0:T(8,128)(2,1)S(1)}, bf16[2,128,512]{2,1,0:T(8,128)(2,1)}, u32[]{:S(2)}) copy-start(bf16[2,128,512]{2,1,0:T(8,128)(2,1)} %f_ref.1) | copy-start | bytes 786436
  1.0 5.9 %copy-start = (bf16[1536,1024]{1,0:T(8,128)(2,1)S(1)}, bf16[1536,1024]{1,0:T(8,128)(2,1)}, u32[]{:S(2)}) copy-start(bf16[1536,1024]{1,0:T(8,128)(2,1)} %w_ref.3) | copy-start | bytes 9437188
  1.0 5.9 %copy-start.1 = (bf16[512,512]{1,0:T(8,128)(2,1)S(1)}, bf16[512,512]{1,0:T(8,128)(2,1)}, u32[]{:S(2)}) copy-start(bf16[512,512]{1,0:T(8,128)(2,1)} %wq_ref.1) | copy-start | bytes 1572868
  1.0 9.7 %copy-start.5 = (f32[128]{0:T(128)S(1)}, f32[128]{0:T(128)}, u32[]{:S(2)}) copy-start(f32[128]{0:T(128)} %constant.39.clone.table_ref) | copy-start | bytes 1540
  1.0 9.7 %collective-permute-start = (bf16[128,512]{1,0:T(8,128)(2,1)S(1)}, bf16[128,512]{1,0:T(8,128)(2,1)S(1)}, u32[]{:S(2)}, u32[]{:S(2)}) collective-permute-start(bf16[128,512]{1,0:T(8,128)(2,1)S(1)} %get-tuple-element.34.fx_ref), channel_id=1, source_target_pairs={{16,32},{32,16},{48,64},{64,48},{80,96},{96,80},{112,128},{128,112... | collective-permute-start | bytes 393224 | tf_op jit(solution)/shard_map/ppermute | solution.py:364
  1.8 8.9 %collective-permute-start.1 = (bf16[128,512]{1,0:T(8,128)(2,1)S(1)}, bf16[128,512]{1,0:T(8,128)(2,1)S(1)}, u32[]{:S(2)}, u32[]{:S(2)}) collective-permute-start(bf16[128,512]{1,0:T(8,128)(2,1)S(1)} %get-tuple-element.35.fy_ref), channel_id=1, source_target_pairs={{0,16},{16,0},{32,48},{48,32},{64,80},{80,64},{96,112},{112,96},{1... | collective-permute-start | bytes 393224 | tf_op jit(solution)/shard_map/ppermute | solution.py:365
  4.9 3.9 %collective-permute-start.2 = (bf16[2,16,512]{2,1,0:T(8,128)(2,1)S(1)}, bf16[2,16,512]{2,1,0:T(8,128)(2,1)S(1)}, u32[]{:S(2)}, u32[]{:S(2)}) collective-permute-start(bf16[2,16,512]{2,1,0:T(8,128)(2,1)S(1)} %get-tuple-element.36), channel_id=1, source_target_pairs={{0,1},{1,2},{2,3},{3,4},{4,5},{5,6},{6,7},{7,8},{8,9},{9,10},{10,1... | collective-permute-start | bytes 98312 | tf_op jit(solution)/shard_map/ppermute | solution.py:366
  6.8 3.9 %collective-permute-start.3 = (bf16[2,16,512]{2,1,0:T(8,128)(2,1)S(1)}, bf16[2,16,512]{2,1,0:T(8,128)(2,1)S(1)}, u32[]{:S(2)}, u32[]{:S(2)}) collective-permute-start(bf16[2,16,512]{2,1,0:T(8,128)(2,1)S(1)} %get-tuple-element.37), channel_id=1, source_target_pairs={{0,15},{1,0},{2,1},{3,2},{4,3},{5,4},{6,5},{7,6},{8,7},{9,8},{10,9... | collective-permute-start | bytes 98312 | tf_op jit(solution)/shard_map/ppermute | solution.py:367
  12.9 37.3 %copy-start.6 = (s32[32]{0:T(128)S(1)}, s32[32]{0:T(128)}, u32[]{:S(2)}) copy-start(s32[32]{0:T(128)} %width_ref.1) | copy-start | bytes 388
  13.0 1.8 %collective-permute-start.4 = (bf16[8,192,128]{2,1,0:T(8,128)(2,1)S(1)}, bf16[8,192,128]{2,1,0:T(8,128)(2,1)S(1)}, u32[]{:S(2)}, u32[]{:S(2)}) collective-permute-start(bf16[8,192,128]{2,1,0:T(8,128)(2,1)S(1)} %get-tuple-element.43), channel_id=1, source_target_pairs={{0,16},{16,0},{32,48},{48,32},{64,80},{80,64},{96,112},{112,96},{1... | collective-permute-start | bytes 1179656 | tf_op jit(solution)/shard_map/ppermute | solution.py:383
  15.5 21.6 %collective-permute-start.5 = (bf16[8,128,128]{2,1,0:T(8,128)(2,1)S(1)}, bf16[8,128,128]{2,1,0:T(8,128)(2,1)S(1)}, u32[]{:S(2)}, u32[]{:S(2)}) collective-permute-start(bf16[8,128,128]{2,1,0:T(8,128)(2,1)S(1)} %get-tuple-element.44), channel_id=1, source_target_pairs={{0,192},{240,48},{1,193},{241,49},{2,194},{242,50},{3,195},{243,51... | collective-permute-start | bytes 786440 | tf_op jit(solution)/shard_map/ppermute | solution.py:398
  22.8 14.4 %collective-permute-start.6 = (bf16[8,128,128]{2,1,0:T(8,128)(2,1)S(1)}, bf16[8,128,128]{2,1,0:T(8,128)(2,1)S(1)}, u32[]{:S(2)}, u32[]{:S(2)}) collective-permute-start(bf16[8,128,128]{2,1,0:T(8,128)(2,1)S(1)} %get-tuple-element.44), channel_id=1, source_target_pairs={{0,128},{240,112},{1,129},{241,113},{2,130},{242,114},{3,131},{243... | collective-permute-start | bytes 786440 | tf_op jit(solution)/shard_map/ppermute | solution.py:398
  24.1 13.1 %collective-permute-start.7 = (bf16[8,128,128]{2,1,0:T(8,128)(2,1)S(1)}, bf16[8,128,128]{2,1,0:T(8,128)(2,1)S(1)}, u32[]{:S(2)}, u32[]{:S(2)}) collective-permute-start(bf16[8,128,128]{2,1,0:T(8,128)(2,1)S(1)} %get-tuple-element.44), channel_id=1, source_target_pairs={{0,64},{240,176},{1,65},{241,177},{2,66},{242,178},{3,67},{243,179... | collective-permute-start | bytes 786440 | tf_op jit(solution)/shard_map/ppermute | solution.py:398
  25.4 17.0 %collective-permute-start.10 = (bf16[2,8,128,128]{3,2,1,0:T(8,128)(2,1)S(1)}, bf16[2,8,128,128]{3,2,1,0:T(8,128)(2,1)S(1)}, u32[]{:S(2)}, u32[]{:S(2)}) collective-permute-start(bf16[2,8,128,128]{3,2,1,0:T(8,128)(2,1)S(1)} %get-tuple-element.45.kv_ref), channel_id=1, source_target_pairs={{0,15},{1,0},{2,1},{3,2},{4,3},{5,4},{6,5},{7,6},{8,7},{9,8},{10,9... | collective-permute-start | bytes 1572872 | tf_op jit(solution)/shard_map/ppermute | solution.py:391
  28.3 14.2 %collective-permute-start.9 = (bf16[2,8,128,128]{3,2,1,0:T(8,128)(2,1)S(1)}, bf16[2,8,128,128]{3,2,1,0:T(8,128)(2,1)S(1)}, u32[]{:S(2)}, u32[]{:S(2)}) collective-permute-start(bf16[2,8,128,128]{3,2,1,0:T(8,128)(2,1)S(1)} %get-tuple-element.45.kv_ref), channel_id=1, source_target_pairs={{0,1},{1,2},{2,3},{3,4},{4,5},{5,6},{6,7},{7,8},{8,9},{9,10},{10,1... | collective-permute-start | bytes 1572872 | tf_op jit(solution)/shard_map/ppermute | solution.py:390
  28.6 19.6 %all-to-all-start = ((bf16[8,192,128]{2,1,0:T(8,128)(2,1)}), bf16[8,192,128]{2,1,0:T(8,128)(2,1)S(1)}, u32[]{:S(2)}, u32[]{:S(2)}) async-start(bf16[8,192,128]{2,1,0:T(8,128)(2,1)} %shard_map.67), calls=%async_computation | async-start | bytes 786432 | tf_op jit(solution)/shard_map/all_to_all | solution.py:387
  37.3 5.2 %collective-permute-start.8 = (bf16[8,128,128]{2,1,0:T(8,128)(2,1)S(1)}, bf16[8,128,128]{2,1,0:T(8,128)(2,1)S(1)}, u32[]{:S(2)}, u32[]{:S(2)}) collective-permute-start(bf16[8,128,128]{2,1,0:T(8,128)(2,1)S(1)} %select_select_fusion), channel_id=1, source_target_pairs={{0,32},{64,96},{128,160},{192,224},{48,16},{112,80},{176,144},{240... | collective-permute-start | bytes 786440 | tf_op jit(solution)/shard_map/ppermute | solution.py:400
  38.6 3.9 %collective-permute-start.11 = (bf16[4,128,128]{2,1,0:T(8,128)(2,1)S(1)}, bf16[4,128,128]{2,1,0:T(8,128)(2,1)S(1)}, u32[]{:S(2)}, u32[]{:S(2)}) collective-permute-start(bf16[4,128,128]{2,1,0:T(8,128)(2,1)S(1)} %get-tuple-element.46.qx_ref), channel_id=1, source_target_pairs={{16,32},{32,16},{48,64},{64,48},{80,96},{96,80},{112,128},{128,112... | collective-permute-start | bytes 393224 | tf_op jit(solution)/shard_map/ppermute | solution.py:392
  39.2 3.2 %collective-permute-start.12 = (bf16[4,128,128]{2,1,0:T(8,128)(2,1)S(1)}, bf16[4,128,128]{2,1,0:T(8,128)(2,1)S(1)}, u32[]{:S(2)}, u32[]{:S(2)}) collective-permute-start(bf16[4,128,128]{2,1,0:T(8,128)(2,1)S(1)} %get-tuple-element.47.qy_ref), channel_id=1, source_target_pairs={{0,16},{16,0},{32,48},{48,32},{64,80},{80,64},{96,112},{112,96},{1... | collective-permute-start | bytes 393224 | tf_op jit(solution)/shard_map/ppermute | solution.py:393
  48.2 2.1 %collective-permute-start.13 = (bf16[8,128,128]{2,1,0:T(8,128)(2,1)S(1)}, bf16[8,128,128]{2,1,0:T(8,128)(2,1)S(1)}, u32[]{:S(2)}, u32[]{:S(2)}) collective-permute-start(bf16[8,128,128]{2,1,0:T(8,128)(2,1)S(1)} %broadcast_select_fusion.p1_ref), channel_id=1, source_target_pairs={{0,16},{16,0},{32,48},{48,32},{64,80},{80,64},{96,112},{112,96},{1... | collective-permute-start | bytes 786440 | tf_op jit(solution)/shard_map/ppermute | solution.py:403
  48.2 11.5 %collective-permute-start.14 = (bf16[8,64,128]{2,1,0:T(8,128)(2,1)S(1)}, bf16[8,64,128]{2,1,0:T(8,128)(2,1)S(1)}, u32[]{:S(2)}, u32[]{:S(2)}) collective-permute-start(bf16[8,64,128]{2,1,0:T(8,128)(2,1)S(1)} %slice.3), channel_id=1, source_target_pairs={{0,8},{1,9},{2,10},{3,11},{4,12},{5,13},{6,14},{7,15},{8,0},{9,1},... | collective-permute-start | bytes 393224 | tf_op jit(solution)/shard_map/ppermute | solution.py:416
  56.6 0.6 copy-start.3
  57.2 2.4 %copy-start.8 = (bf16[5,128,128]{2,1,0:T(8,128)(2,1)}, bf16[5,128,128]{2,1,0:T(8,128)(2,1)S(1)}, u32[]{:S(2)}) copy-start(bf16[5,128,128]{2,1,0:T(8,128)(2,1)S(1)} %get-tuple-element.59) | copy-start | bytes 491524
  57.2 2.4 %copy-start.10 = (bf16[5,128,128]{2,1,0:T(8,128)(2,1)}, bf16[5,128,128]{2,1,0:T(8,128)(2,1)S(1)}, u32[]{:S(2)}) copy-start(bf16[5,128,128]{2,1,0:T(8,128)(2,1)S(1)} %get-tuple-element.58) | copy-start | bytes 491524
  59.7 19.5 %copy-start.2 = (bf16[512,512]{1,0:T(8,128)(2,1)S(1)}, bf16[512,512]{1,0:T(8,128)(2,1)}, u32[]{:S(2)}) copy-start(bf16[512,512]{1,0:T(8,128)(2,1)} %wo_ref.3) | copy-start | bytes 1572868
  59.7 19.5 %copy-start.4 = (bf16[2,128,128]{2,1,0:T(8,128)(2,1)S(1)}, bf16[2,128,128]{2,1,0:T(8,128)(2,1)}, u32[]{:S(2)}) copy-start(bf16[2,128,128]{2,1,0:T(8,128)(2,1)} %copy-done.3) | copy-start | bytes 196612
  59.7 7.6 %copy-start.11 = (bf16[5,128,128]{2,1,0:T(8,128)(2,1)S(1)}, bf16[5,128,128]{2,1,0:T(8,128)(2,1)}, u32[]{:S(2)}) copy-start(bf16[5,128,128]{2,1,0:T(8,128)(2,1)} %copy-done.10) | copy-start | bytes 491524
  59.7 8.2 %copy-start.9 = (bf16[5,128,128]{2,1,0:T(8,128)(2,1)S(1)}, bf16[5,128,128]{2,1,0:T(8,128)(2,1)}, u32[]{:S(2)}) copy-start(bf16[5,128,128]{2,1,0:T(8,128)(2,1)} %copy-done.8) | copy-start | bytes 491524
  62.9 16.3 %all-to-all-start.1 = ((bf16[16,80,128]{2,1,0:T(8,128)(2,1)}), bf16[16,80,128]{2,1,0:T(8,128)(2,1)S(1)}, u32[]{:S(2)}, u32[]{:S(2)}) async-start(bf16[16,80,128]{2,1,0:T(8,128)(2,1)} %shard_map.70), calls=%async_computation.1 | async-start | bytes 655360 | tf_op jit(solution)/shard_map/all_to_all | solution.py:427
  67.3 1.9 %collective-permute-start.15 = (bf16[5,128,128]{2,1,0:T(8,128)(2,1)S(1)}, bf16[5,128,128]{2,1,0:T(8,128)(2,1)S(1)}, u32[]{:S(2)}, u32[]{:S(2)}) collective-permute-start(bf16[5,128,128]{2,1,0:T(8,128)(2,1)S(1)} %copy-done.11), channel_id=1, source_target_pairs={{16,32},{32,16},{48,64},{64,48},{80,96},{96,80},{112,128},{128,112... | collective-permute-start | bytes 491528 | tf_op jit(solution)/shard_map/ppermute | solution.py:413
  68.0 2.2 %collective-permute-start.16 = (bf16[5,128,128]{2,1,0:T(8,128)(2,1)S(1)}, bf16[5,128,128]{2,1,0:T(8,128)(2,1)S(1)}, u32[]{:S(2)}, u32[]{:S(2)}) collective-permute-start(bf16[5,128,128]{2,1,0:T(8,128)(2,1)S(1)} %copy-done.9), channel_id=1, source_target_pairs={{0,16},{16,0},{32,48},{48,32},{64,80},{80,64},{96,112},{112,96},{1... | collective-permute-start | bytes 491528 | tf_op jit(solution)/shard_map/ppermute | solution.py:414
  79.2 1.6 %collective-permute-start.17 = (bf16[16,80,128]{2,1,0:T(8,128)(2,1)S(1)}, bf16[16,80,128]{2,1,0:T(8,128)(2,1)S(1)}, u32[]{:S(2)}, u32[]{:S(2)}) collective-permute-start(bf16[16,80,128]{2,1,0:T(8,128)(2,1)S(1)} %all-to-all-done.1.p1_ref), channel_id=1, source_target_pairs={{0,16},{16,0},{32,48},{48,32},{64,80},{80,64},{96,112},{112,96},{1... | collective-permute-start | bytes 983048 | tf_op jit(solution)/shard_map/ppermute | solution.py:430
